TPU v7x, 32 devices: a whole 2x2x4 slice. The times are simulated.
32 devices in a mesh: groups: 2 (over y), dp: 4 (over x, core), head: 4 (over z).
Axes of the slice: x: 2, y: 2, z: 4, core: 2. Of those that a mesh axis runs over, the one named last changes fastest.
Arguments:
- train_grads: bfloat16 [2, 32, 256, 8192], P(None, ('groups', 'dp'), None, 'head'), parts along dimension 1, may hold values from -6 to 6
- train_acts: bfloat16 [2, 32, 256, 8192], P(None, ('groups', 'dp'), None, 'head'), parts along dimension 1, may hold values from -6 to 6
- train_ids: int32 [32, 256], P(('groups', 'dp')), parts along dimension 0, may hold values from 0 to 128255
- query_grads: bfloat16 [2, 8, 256, 8192], P(None, ('groups', 'dp'), None, 'head'), parts along dimension 1, may hold values from -6 to 6
- query_acts: bfloat16 [2, 8, 256, 8192], P(None, ('groups', 'dp'), None, 'head'), parts along dimension 1, may hold values from -6 to 6
- query_ids: int32 [8, 256], P(('groups', 'dp')), parts along dimension 0, may hold values from 0 to 128255
- token_weight: float32 [128256], replicated, may hold values from 0.25 to 4
- out_proj: bfloat16 [2, 64, 8192], P(None, None, 'head'), may hold values from -0.0625 to 0.0625
- in_proj: bfloat16 [2, 64, 64, 128], P(None, 'head'), may hold values from -0.5 to 0.5
- out_factor: float32 [2, 64, 64], replicated, as said below
- in_factor: float32 [2, 64, 64, 64], P(None, 'head'), as said below
Outputs:
- scores: float32 [4, 32], P(None, ('groups', 'dp')), parts along dimension 1
There are 2 independent parts, one for each index of `groups`. A program takes and returns all parts, laid end to end along the dimension named above; an argument that names none is the same for every part. Nothing has to cross between parts.
Inputs may be any that keep to these rules, and one draw needn't show every extreme that they name: out_factor and in_factor are symmetric matrices. in_factor matrices are symmetric.
All inputs are finite; a program needn't handle non-finite values.
Results may differ from a plain program's by a relative error of at most 0.0053.
Values sent between devices are 32-bit elements; how exact they have to be, the bound alone decides.
No kernel may reach another device: no remote copies, remote signals or barrier semaphores. Data moves between devices by JAX's collectives and lax.ppermute only.
A program may use at most 128 MiB of HBM per device.

v0:
```python
import math

import jax
import jax.numpy as jnp
from jax import lax
from jax.sharding import PartitionSpec as P

HIGH = lax.Precision.HIGHEST


def partial_side(grads_in, out_proj):
    stacked = []
    for layer_idx in range(grads_in.shape[0]):
        flat = grads_in[layer_idx].reshape(-1, grads_in.shape[3])
        stacked.append(jnp.dot(flat, out_proj[layer_idx].T, preferred_element_type=jnp.float32))
    return jnp.stack(stacked)


def example_blocks(summed, acts_in, ids, token_weight, in_proj):
    count, length = ids.shape
    heads_dev, rank_n, head_dim = (in_proj.shape[1], in_proj.shape[2], in_proj.shape[3])
    scale = token_weight[ids].reshape(-1, 1)
    result = []
    for layer_idx in range(acts_in.shape[0]):
        acts_flat = acts_in[layer_idx].reshape(count * length, heads_dev, head_dim)
        in_side = jnp.einsum(
            "thk,hrk->thr", acts_flat, in_proj[layer_idx], preferred_element_type=jnp.float32
        ).astype(jnp.bfloat16)
        weighted = (summed[layer_idx] * scale).astype(jnp.bfloat16).reshape(count, length, rank_n)
        blocks = jnp.einsum(
            "ntr,nths->nhrs",
            weighted,
            in_side.reshape(count, length, heads_dev, rank_n),
            preferred_element_type=jnp.float32,
        )
        result.append(blocks / math.sqrt(length))
    return jnp.stack(result)


def apply_factors(blocks, out_factor, in_factor):
    left = jnp.einsum("lij,lnhjk->lnhik", out_factor, blocks, precision=HIGH)
    return jnp.einsum("lnhik,lhkm->lnhim", left, in_factor, precision=HIGH)


def local(
    train_grads,
    train_acts,
    train_ids,
    query_grads,
    query_acts,
    query_ids,
    token_weight,
    out_proj,
    in_proj,
    out_factor,
    in_factor,
):
    train_sum, query_sum = lax.psum(
        (partial_side(train_grads, out_proj), partial_side(query_grads, out_proj)), "head"
    )
    train_blocks = example_blocks(train_sum, train_acts, train_ids, token_weight, in_proj)
    query_blocks = example_blocks(query_sum, query_acts, query_ids, token_weight, in_proj)
    train_ready = apply_factors(train_blocks, out_factor, in_factor)
    layers_n, heads_dev, rank_n = (
        train_blocks.shape[0],
        train_blocks.shape[2],
        train_blocks.shape[3],
    )
    norm = 1.0 / math.sqrt(layers_n * heads_dev * lax.axis_size("head") * rank_n * rank_n)
    every_query = lax.all_gather(query_blocks, "dp", axis=1, tiled=True)
    partial_scores = jnp.einsum("lqhij,lnhij->qn", every_query, train_ready, precision=HIGH)
    return lax.psum(partial_scores, "head") * norm


def solution(mesh):
    return jax.shard_map(
        local,
        mesh=mesh,
        in_specs=(
            P(None, ("groups", "dp"), None, "head"),
            P(None, ("groups", "dp"), None, "head"),
            P(("groups", "dp"), None),
            P(None, ("groups", "dp"), None, "head"),
            P(None, ("groups", "dp"), None, "head"),
            P(("groups", "dp"), None),
            P(),
            P(None, None, "head"),
            P(None, "head", None, None),
            P(),
            P(None, "head", None, None),
        ),
        out_specs=P(None, ("groups", "dp")),
        check_vma=False,
    )
```

profile of v0, /device:TPU:0, one launch (start us, length us, event | category | flops | bytes accessed | tf_op | source)
XLA Modules:
  0.0 156.3 jit_solution(9725258516442131414)
XLA Ops:
  6.5 0.0 copy-start
  6.5 0.0 all-reduce.3.cloned.1.call-start
  6.5 1.8 %convolution_bitcast_fusion.2 = f32[1,256,64]{1,2,0:T(8,128)S(1)} fusion(bf16[2,1,256,2048]{3,2,1,0:T(8,128)(2,1)} %param.14, bf16[2,64,2048]{2,1,0:T(8,128)(2,1)} %param.18), kind=kOutput, calls=%fused_computation.38 | convolution fusion | flops 67108864 | bytes 1376256 | tf_op jit(solution)/shard_map/dot_general | solution.py:15
  8.3 1.7 %convolution_bitcast_fusion.3 = f32[1,256,64]{1,2,0:T(8,128)S(1)} fusion(bf16[2,1,256,2048]{3,2,1,0:T(8,128)(2,1)} %param.14, bf16[2,64,2048]{2,1,0:T(8,128)(2,1)} %param.18), kind=kOutput, calls=%fused_computation.39 | convolution fusion | flops 67108864 | bytes 1376256 | tf_op jit(solution)/shard_map/dot_general | solution.py:15
  10.0 0.0 copy-start.5
  10.1 4.0 %fusion.88 = (bf16[1,4,256,2048]{3,2,1,0:T(8,128)(2,1)S(1)}, bf16[1,4,256,2048]{3,2,1,0:T(8,128)(2,1)S(1)}) fusion(bf16[2,4,256,2048]{3,2,1,0:T(8,128)(2,1)} %param.11), kind=kLoop, calls=%fused_computation.90 | loop fusion | bytes 16777216 | tf_op jit(solution)/shard_map/slice | solution.py:14
  14.1 0.0 copy-done.5
  14.1 1.4 convolution_bitcast_fusion
  15.5 1.4 convolution_bitcast_fusion.1
  16.9 0.9 pad_maximum_fusion.1
  17.8 0.7 pad_maximum_fusion.2
  18.5 0.0 all-reduce.3.cloned.1.call-update
  18.5 0.0 copy-start.9
  18.5 0.0 copy-start.1
  18.5 0.0 copy-start.3
  18.5 0.0 all-gather.2.cloned.1.call-start
  18.6 3.2 %fusion.89 = (bf16[1,1,256,2048]{3,2,1,0:T(8,128)(2,1)}, bf16[1,1,256,2048]{3,2,1,0:T(8,128)(2,1)}) fusion(bf16[2,1,256,2048]{3,2,1,0:T(8,128)(2,1)} %param.15), kind=kLoop, calls=%fused_computation.91 | loop fusion | bytes 4194304 | tf_op jit(solution)/shard_map/slice | solution.py:25
  21.8 1.5 copy.33
  23.2 2.3 %copy.34 = bf16[1,1,256,2048]{2,3,1,0:T(8,128)(2,1)} copy(bf16[1,1,256,2048]{3,2,1,0:T(8,128)(2,1)} %get-tuple-element.12) | data formatting | bytes 2097152 | tf_op jit(solution)/shard_map/reshape;squeeze | solution.py:25
  25.5 0.0 copy-done.9
  25.5 0.0 copy-done.1
  25.5 1.7 %gather_fusion = f32[256]{0:T(256)S(1)} fusion(f32[128256]{0:T(1024)S(1)} %copy-done.1, s32[1024]{0:T(1024)S(1)} %pad_clamp_fusion), kind=kCustom, calls=%fused_computation | custom fusion | bytes 3072 | tf_op jit(solution)/shard_map/gather | solution.py:22
  27.3 34.8 %all-reduce.3.cloned.1.call-done = (f32[2,256,64]{1,2,0:T(8,128)}, f32[2,1024,64]{1,2,0:T(8,128)}) async-done(((f32[2,256,64]{1,2,0:T(8,128)}, f32[2,1024,64]{1,2,0:T(8,128)}), (f32[2,256,64]{1,2,0:T(8,128)}, f32[2,1024,64]{1,2,0:T(8,128)})) %all-reduce.3.cloned.1.call-update) | async-done | bytes 655376 | tf_op jit(solution)/shard_map/psum | solution.py:58
  62.1 0.0 copy-done.3
  62.1 2.1 %fusion.35 = f32[1,1,16,64,64]{3,4,2,1,0:T(8,128)} fusion(bf16[256,16,128]{0,2,1:T(8,128)(2,1)S(1)} %bitcast.158, bf16[2,16,64,128]{3,2,1,0:T(8,128)(2,1)S(1)} %copy-done.3, f32[2,256,64]{1,2,0:T(8,128)} %get-tuple-element.5, f32[256]{0:T(256)S(1)} %gather_fusion), kind=kOutput, calls=%fused_computation.31 | convolution fusion | flops 101023744 | bytes 1639424 | tf_op jit(solution)/shard_map/ntr,nths->nhrs/dot_general | solution.py:30
  64.3 1.7 %fusion.39 = f32[1,1,16,64,64]{3,4,2,1,0:T(8,128)S(1)} fusion(bf16[256,16,128]{0,2,1:T(8,128)(2,1)} %bitcast.159, bf16[2,16,64,128]{3,2,1,0:T(8,128)(2,1)S(1)} %copy-done.3, f32[2,256,64]{1,2,0:T(8,128)} %get-tuple-element.5, f32[256]{0:T(256)S(1)} %gather_fusion), kind=kOutput, calls=%fused_computation.35 | convolution fusion | flops 101023744 | bytes 1639424 | tf_op jit(solution)/shard_map/ntr,nths->nhrs/dot_general | solution.py:30
  66.0 2.2 %pad_maximum_fusion = f32[2,1,16,64,64]{3,4,2,1,0:T(8,128)} fusion(f32[1,1,16,64,64]{3,4,2,1,0:T(8,128)S(1)} %fusion.39, f32[1,1,16,64,64]{3,4,2,1,0:T(8,128)} %fusion.35), kind=kLoop, calls=%fused_computation.41 | loop fusion | flops 131072 | bytes 1048576 | tf_op jit(solution)/shard_map/stack | solution.py:37
  68.2 0.0 all-gather.2.cloned.1.call-update
  68.2 5.3 %fusion.87 = (bf16[1,4,256,2048]{3,2,1,0:T(8,128)(2,1)}, bf16[1,4,256,2048]{3,2,1,0:T(8,128)(2,1)S(1)}) fusion(bf16[2,4,256,2048]{3,2,1,0:T(8,128)(2,1)} %param.12), kind=kLoop, calls=%fused_computation.89 | loop fusion | bytes 16777216 | tf_op jit(solution)/shard_map/slice | solution.py:25
  73.4 0.0 copy-start.8
  73.4 3.6 %copy.39 = bf16[128,8,16,128]{3,2,1,0:T(8,128)(2,1)} copy(bf16[128,8,16,128]{3,1,2,0:T(8,128)(2,1)S(1)} %bitcast.155) | data formatting | bytes 8388608
  77.0 0.0 copy-done.8
  77.0 6.3 %gather_fusion.1 = f32[1024]{0:T(1024)S(1)} fusion(f32[128256]{0:T(1024)S(1)} %copy-done.1, s32[1024]{0:T(1024)S(1)} %broadcast_clamp_fusion), kind=kCustom, calls=%fused_computation.1 | custom fusion | bytes 12288 | tf_op jit(solution)/shard_map/gather | solution.py:22
  83.4 0.0 copy-start.2
  83.4 3.8 %copy.37 = bf16[128,8,16,128]{3,2,1,0:T(8,128)(2,1)S(1)} copy(bf16[128,8,16,128]{3,1,2,0:T(8,128)(2,1)} %bitcast.154) | data formatting | bytes 8388608
  87.2 0.0 copy-start.4
  87.2 0.0 copy-done.2
  87.2 4.0 %fusion.25 = bf16[16,64,1024]{2,1,0:T(8,128)(2,1)} fusion(bf16[1024,16,128]{2,1,0:T(8,128)(2,1)S(1)} %bitcast.152, bf16[2,16,64,128]{3,2,1,0:T(8,128)(2,1)S(1)} %copy-done.3), kind=kOutput, calls=%fused_computation.25 | convolution fusion | flops 269484032 | bytes 6553600 | tf_op jit(solution)/shard_map/thk,hrk->thr/dot_general | solution.py:26
  91.2 0.0 copy-start.6
  91.2 0.0 copy-done.4
  91.2 2.6 %fusion.22 = bf16[16,64,1024]{2,1,0:T(8,128)(2,1)S(1)} fusion(bf16[1024,16,128]{2,1,0:T(8,128)(2,1)S(1)} %bitcast.153, bf16[2,16,64,128]{3,2,1,0:T(8,128)(2,1)S(1)} %copy-done.4), kind=kOutput, calls=%fused_computation.24 | convolution fusion | flops 269484032 | bytes 6553600 | tf_op jit(solution)/shard_map/thk,hrk->thr/dot_general | solution.py:26
  93.8 0.0 copy-done.6
  93.8 0.8 fusion.90
  94.6 0.8 squeeze.29
  95.4 1.1 squeeze.28
  96.5 0.0 copy-start.7
  96.5 2.3 %multiply_bitcast_fusion = f32[1,4,16,64,64]{3,4,2,1,0:T(8,128)S(1)} fusion(bf16[16,8,4,8,256]{4,3,2,1,0:T(8,128)(2,1)} %bitcast.157, f32[4,256,64]{1,0,2:T(4,128)} %squeeze.29, f32[4,256]{1,0:T(4,128)S(1)} %reshape.69), kind=kOutput, calls=%fused_computation.22 | convolution fusion | flops 134610944 | bytes 3411968 | tf_op jit(solution)/shard_map/ntr,nths->nhrs/dot_general | solution.py:30
  98.8 0.7 multiply_bitcast_fusion.1
  99.5 0.0 copy-done.7
  99.5 4.3 %fusion.13 = f32[2,4,16,64,64]{3,4,2,1,0:T(8,128)S(1)} fusion(f32[1,4,16,64,64]{3,4,2,1,0:T(8,128)S(1)} %multiply_bitcast_fusion, f32[1,4,16,64,64]{3,4,2,1,0:T(8,128)S(1)} %multiply_bitcast_fusion.1, f32[2,64,64]{2,1,0:T(8,128)S(1)} %copy-done.7), kind=kOutput, calls=%fused_computation.15 | convolution fusion | flops 403177472 | bytes 4227072 | tf_op jit(solution)/shard_map/lij,lnhjk->lnhik/dot_general | solution.py:41
  103.9 0.0 copy-done
  103.9 8.6 %fusion.7 = f32[2,16,4,64,64]{4,3,2,1,0:T(8,128)} fusion(f32[2,4,16,64,64]{3,4,2,1,0:T(8,128)S(1)} %fusion.13, f32[2,16,64,64]{3,2,1,0:T(8,128)S(1)} %copy-done), kind=kOutput, calls=%fused_computation.9 | convolution fusion | flops 402653184 | bytes 4718592 | tf_op jit(solution)/shard_map/lnhik,lhkm->lnhim/dot_general | solution.py:42
  112.4 0.0 all-gather.2.cloned.1.call-done
  112.4 5.3 %copy.23 = f32[2,4,16,64,64]{4,1,0,3,2:T(4,128)} copy(f32[2,4,16,64,64]{3,4,2,1,0:T(8,128)} %all-gather.2.cloned.1.call-done) | data formatting | bytes 4194304 | tf_op jit(solution)/shard_map/all_gather | solution.py:70
  117.7 21.3 %fusion.40 = f32[4,4]{1,0:T(4,128)S(1)} fusion(f32[2,4,16,64,64]{4,1,0,3,2:T(4,128)} %copy.23, f32[2,16,4,64,64]{4,3,2,1,0:T(8,128)} %fusion.7), kind=kOutput, calls=%fused_computation.40 | convolution fusion | flops 25165824 | bytes 4194368 | tf_op jit(solution)/shard_map/lqhij,lnhij->qn/dot_general | solution.py:71
  139.0 9.9 %psum.23 = f32[4,4]{1,0:T(4,128)S(1)} all-reduce(f32[4,4]{1,0:T(4,128)S(1)} %fusion.40), channel_id=1, replica_groups=mesh['groups'=2,'dp'=4,'head'=4] {'head'}, use_global_device_ids=true, to_apply=%region_2.0 | all-reduce | flops 16 | bytes 128 | tf_op jit(solution)/shard_map/psum | solution.py:72
  148.9 0.6 broadcast_multiply_fusion
  (6 shorter events, 0.0 us)
Async XLA Ops:
  6.5 97.3 %copy-start = (f32[2,16,64,64]{3,2,1,0:T(8,128)S(1)}, f32[2,16,64,64]{3,2,1,0:T(8,128)}, u32[]{:S(2)}) copy-start(f32[2,16,64,64]{3,2,1,0:T(8,128)} %param.21) | copy-start | bytes 1572868
  6.5 55.6 %all-reduce.3.cloned.1.call-start = ((), (), s32[]{:S(2)}) async-start(), calls=%async_computation.1 | async-start | bytes 1310720 | tf_op jit(solution)/shard_map/psum | solution.py:58
  10.0 4.1 %copy-start.5 = (bf16[2,64,2048]{2,1,0:T(8,128)(2,1)S(1)}, bf16[2,64,2048]{2,1,0:T(8,128)(2,1)}, u32[]{:S(2)}) copy-start(bf16[2,64,2048]{2,1,0:T(8,128)(2,1)} %param.18) | copy-start | bytes 1572868
  18.5 7.0 %copy-start.9 = (s32[1,256]{1,0:T(1,128)S(1)}, s32[1,256]{1,0:T(1,128)}, u32[]{:S(2)}) copy-start(s32[1,256]{1,0:T(1,128)} %param.16) | copy-start | bytes 3076
  18.5 7.0 %copy-start.1 = (f32[128256]{0:T(1024)S(1)}, f32[128256]{0:T(1024)}, u32[]{:S(2)}) copy-start(f32[128256]{0:T(1024)} %param.17) | copy-start | bytes 1539076
  18.5 43.6 %copy-start.3 = (bf16[2,16,64,128]{3,2,1,0:T(8,128)(2,1)S(1)}, bf16[2,16,64,128]{3,2,1,0:T(8,128)(2,1)}, u32[]{:S(2)}) copy-start(bf16[2,16,64,128]{3,2,1,0:T(8,128)(2,1)} %param.19) | copy-start | bytes 1572868
  18.5 93.9 %all-gather.2.cloned.1.call-start = ((), (), s32[]{:S(2)}) async-start(), calls=%async_computation | async-start | bytes 5242880 | tf_op jit(solution)/shard_map/all_gather | solution.py:70
  73.4 3.6 %copy-start.8 = (s32[4,256]{1,0:T(4,128)S(1)}, s32[4,256]{1,0:T(4,128)}, u32[]{:S(2)}) copy-start(s32[4,256]{1,0:T(4,128)} %param.13) | copy-start | bytes 12292
  83.4 3.8 %copy-start.2 = (bf16[128,8,16,128]{3,2,1,0:T(8,128)(2,1)S(1)}, bf16[128,8,16,128]{3,2,1,0:T(8,128)(2,1)}, u32[]{:S(2)}) copy-start(bf16[128,8,16,128]{3,2,1,0:T(8,128)(2,1)} %copy.39) | copy-start | bytes 12582916
  87.2 4.0 %copy-start.4 = (bf16[2,16,64,128]{3,2,1,0:T(8,128)(2,1)S(1)}, bf16[2,16,64,128]{3,2,1,0:T(8,128)(2,1)}, u32[]{:S(2)}) copy-start(bf16[2,16,64,128]{3,2,1,0:T(8,128)(2,1)} %param.19) | copy-start | bytes 1572868
  91.2 2.6 %copy-start.6 = (f32[2,1024,64]{1,2,0:T(8,128)S(1)}, f32[2,1024,64]{1,2,0:T(8,128)}, u32[]{:S(2)}) copy-start(f32[2,1024,64]{1,2,0:T(8,128)} %get-tuple-element.6) | copy-start | bytes 1572868
  96.5 3.1 %copy-start.7 = (f32[2,64,64]{2,1,0:T(8,128)S(1)}, f32[2,64,64]{2,1,0:T(8,128)}, u32[]{:S(2)}) copy-start(f32[2,64,64]{2,1,0:T(8,128)} %param.20) | copy-start | bytes 98308
Sparse Core Ops, SparseCore 0:
  18.6 43.4 all-reduce.2
  68.3 33.8 all-gather.1
where the time goes:
time: 157 us; the launch traced here: 156 us
  matrix products  53.9 us (34%)
  local copies, waits for them, and re-layouts  39.7 us (25%)
  waiting for transfers between devices  34.9 us (22%)
  between operations  13.6 us (9%)
  blocking collectives  9.9 us (6%)
  other arithmetic  4.32 us (3%)
    psum x1, waiting for transfers between devices, local(): lax.psum((partial_side(train_grads, out_proj), partial_side(query_grads,...  34.8 us
    dot_general x1, matrix products, local(): jnp.einsum('lqhij,lnhij->qn', every_query, train_ready, precision=HIGH)  21.3 us
    psum x1, blocking collectives, local(): return lax.psum(partial_scores, 'head') * norm  9.9 us
    dot_general x1, matrix products, apply_factors(): return jnp.einsum('lnhik,lhkm->lnhim', left, in_factor, precision=HIGH)  8.55 us
    slice x2, local copies, waits for them, and re-layouts, example_blocks(): acts_flat = acts_in[layer_idx].reshape(count * length, heads_dev, head_dim)  8.47 us
    gather x3, local copies, waits for them, and re-layouts, example_blocks(): scale = token_weight[ids].reshape(-1, 1)  8.06 us
    unnamed x23, local copies, waits for them, and re-layouts  7.39 us
    dot_general x4, matrix products, example_blocks(): jnp.einsum('ntr,nths->nhrs', weighted, in_side.reshape(count, length, hea...  6.87 us
  transfers between devices with their start and end apart: 2, of which 1 were waited for; matrix products, arithmetic and copies ran while one was open for 34% of the time, Pallas kernels for 0%

commit v1 on v0

v1 whole, which is shorter than its diff:
```python
import math

import jax
import jax.numpy as jnp
from jax import lax
from jax.experimental import pallas as pl
from jax.experimental.pallas import tpu as pltpu
from jax.sharding import PartitionSpec as P

HIGH = lax.Precision.HIGHEST
F32 = jnp.float32
BF16 = jnp.bfloat16
NT = (((1,), (1,)), ((), ()))
VMEM_LIMIT = 48 * 1024 * 1024

NEAR = [(0, 1), (1, 0), (2, 3), (3, 2)]
FAR = [(0, 2), (2, 0), (1, 3), (3, 1)]


def params():
    return pltpu.CompilerParams(vmem_limit_bytes=VMEM_LIMIT)


def cost(flops, nbytes):
    return pl.CostEstimate(flops=int(flops), bytes_accessed=int(nbytes), transcendentals=0)


def side_kernel(layer_ref, grads_ref, proj_ref, out_ref):
    side = lax.dot_general(grads_ref[0, 0], proj_ref[0], NT, preferred_element_type=F32)
    out_ref[0] = side.T


def side_partial(layer, grads, out_proj):
    _, count, length, feats = grads.shape
    rank = out_proj.shape[1]
    return pl.pallas_call(
        side_kernel,
        out_shape=jax.ShapeDtypeStruct((count, rank, length), F32),
        grid_spec=pltpu.PrefetchScalarGridSpec(
            num_scalar_prefetch=1,
            grid=(count,),
            in_specs=[
                pl.BlockSpec((1, 1, length, feats), lambda i, l: (l[0], i, 0, 0)),
                pl.BlockSpec((1, rank, feats), lambda i, l: (l[0], 0, 0)),
            ],
            out_specs=pl.BlockSpec((1, rank, length), lambda i, l: (i, 0, 0)),
        ),
        compiler_params=params(),
        cost_estimate=cost(
            2 * count * length * feats * 256, 2 * (count * length + rank) * feats
        ),
        name="side_partial",
    )(layer, grads, out_proj)


def in_kernel(acts_ref, proj_ref, out_ref):
    heads, rank, width = proj_ref.shape[1:]
    none = jnp.zeros((rank, width), BF16)
    for pair in range(heads // 2):
        one, two = proj_ref[0, 2 * pair], proj_ref[0, 2 * pair + 1]
        both = jnp.concatenate(
            [jnp.concatenate([one, none], axis=1), jnp.concatenate([none, two], axis=1)], axis=0
        )
        acts = acts_ref[0, 0, :, 2 * width * pair : 2 * width * (pair + 1)]
        side = lax.dot_general(acts, both, NT, preferred_element_type=F32)
        out_ref[0, 0, :, 2 * rank * pair : 2 * rank * (pair + 1)] = side.astype(BF16)


def in_side(acts, in_proj):
    layers, count, length, feats = acts.shape
    _, heads, rank, width = in_proj.shape
    return pl.pallas_call(
        in_kernel,
        out_shape=jax.ShapeDtypeStruct((layers, count, length, heads * rank), BF16),
        grid=(layers, count),
        in_specs=[
            pl.BlockSpec((1, 1, length, feats), lambda l, i: (l, i, 0, 0)),
            pl.BlockSpec((1, heads, rank, width), lambda l, i: (l, 0, 0, 0)),
        ],
        out_specs=pl.BlockSpec((1, 1, length, heads * rank), lambda l, i: (l, i, 0, 0)),
        compiler_params=params(),
        cost_estimate=cost(
            2 * layers * count * length * feats * 128, 3 * layers * count * length * feats
        ),
        name="in_side",
    )(acts, in_proj)


def token_kernel(ids_ref, table_ref, out_ref):
    table = table_ref[...]
    rows, lanes = table.shape
    high = table.astype(BF16)
    rest = table - high.astype(F32)
    mid = rest.astype(BF16)
    low = (rest - mid.astype(F32)).astype(BF16)
    turned = [part.T for part in (high, mid, low)]
    length = ids_ref.shape[1]
    for row in range(ids_ref.shape[0]):
        ids = ids_ref[row : row + 1, :]
        block = ids // lanes
        at = lax.broadcasted_iota(jnp.int32, (rows, length), 0) == block
        hot = jnp.where(at, 1.0, 0.0).astype(BF16)
        picked = sum(jnp.dot(part, hot, preferred_element_type=F32) for part in turned)
        lane = lax.broadcasted_iota(jnp.int32, (lanes, length), 0) == ids - block * lanes
        out_ref[row : row + 1, :] = jnp.sum(
            jnp.where(lane, picked, 0.0), axis=0, keepdims=True
        )


def token_scale(ids, token_weight):
    lanes = 128
    table = jnp.pad(token_weight, (0, -token_weight.shape[0] % lanes)).reshape(-1, lanes)
    return pl.pallas_call(
        token_kernel,
        out_shape=jax.ShapeDtypeStruct(ids.shape, F32),
        compiler_params=params(),
        cost_estimate=cost(6 * ids.size * table.size, 4 * table.size),
        name="token_scale",
    )(ids, table)


def weighted_blocks(side, scale, in_side_seq, length):
    weighted = (side * scale).astype(BF16)
    return jnp.dot(weighted, in_side_seq, preferred_element_type=F32) * (1.0 / math.sqrt(length))


def blocks_kernel(layer_ref, side_ref, scale_ref, in_ref, out_ref):
    out_ref[0] = weighted_blocks(side_ref[0], scale_ref[0], in_ref[0, 0], side_ref.shape[2])


def train_blocks(layer, side, scale, in_sides):
    count, rank, length = side.shape
    wide = in_sides.shape[3]
    return pl.pallas_call(
        blocks_kernel,
        out_shape=jax.ShapeDtypeStruct((count, rank, wide), F32),
        grid_spec=pltpu.PrefetchScalarGridSpec(
            num_scalar_prefetch=1,
            grid=(count,),
            in_specs=[
                pl.BlockSpec((1, rank, length), lambda i, l: (i, 0, 0)),
                pl.BlockSpec((1, 1, length), lambda i, l: (i, 0, 0)),
                pl.BlockSpec((1, 1, length, wide), lambda i, l: (l[0], i, 0, 0)),
            ],
            out_specs=pl.BlockSpec((1, rank, wide), lambda i, l: (i, 0, 0)),
        ),
        compiler_params=params(),
        cost_estimate=cost(
            8 * count * rank * length * wide, count * (2 * length + 4 * rank) * wide
        ),
        name="train_blocks",
    )(layer, side, scale.reshape(count, 1, length), in_sides)


def query_kernel(layer_ref, side_ref, scale_ref, in_ref, out_factor_ref, in_factor_ref, out_ref):
    heads, rank = in_factor_ref.shape[1], in_factor_ref.shape[2]
    blocks = weighted_blocks(side_ref[0], scale_ref[0], in_ref[0, 0], side_ref.shape[2])
    left = jnp.dot(out_factor_ref[0], blocks, precision=HIGH, preferred_element_type=F32)
    none = jnp.zeros((rank, rank), F32)
    for pair in range(heads // 2):
        one, two = in_factor_ref[0, 2 * pair], in_factor_ref[0, 2 * pair + 1]
        both = jnp.concatenate(
            [jnp.concatenate([one, none], axis=1), jnp.concatenate([none, two], axis=1)], axis=0
        )
        span = slice(2 * rank * pair, 2 * rank * (pair + 1))
        out_ref[0, :, span] = jnp.dot(
            left[:, span], both, precision=HIGH, preferred_element_type=F32
        )


def query_ready(layer, side, scale, in_sides, out_factor, in_factor):
    count, rank, length = side.shape
    wide = in_sides.shape[3]
    heads = in_factor.shape[1]
    return pl.pallas_call(
        query_kernel,
        out_shape=jax.ShapeDtypeStruct((count, rank, wide), F32),
        grid_spec=pltpu.PrefetchScalarGridSpec(
            num_scalar_prefetch=1,
            grid=(count,),
            in_specs=[
                pl.BlockSpec((1, rank, length), lambda i, l: (i, 0, 0)),
                pl.BlockSpec((1, 1, length), lambda i, l: (i, 0, 0)),
                pl.BlockSpec((1, 1, length, wide), lambda i, l: (l[0], i, 0, 0)),
                pl.BlockSpec((1, rank, rank), lambda i, l: (l[0], 0, 0)),
                pl.BlockSpec((1, heads, rank, rank), lambda i, l: (l[0], 0, 0, 0)),
            ],
            out_specs=pl.BlockSpec((1, rank, wide), lambda i, l: (i, 0, 0)),
        ),
        compiler_params=params(),
        cost_estimate=cost(
            20 * count * rank * length * wide, count * (2 * length + 4 * rank) * wide
        ),
        name="query_ready",
    )(layer, side, scale.reshape(count, 1, length), in_sides, out_factor, in_factor)


def score_kernel(groups, *refs):
    out_ref = refs[-1]
    at = 0
    lanes = out_ref.shape[1]
    total = None
    for queries_n in groups:
        query_refs = refs[at : at + queries_n]
        blocks_ref = refs[at + queries_n]
        at += queries_n + 1
        rows = []
        for query_ref in query_refs:
            for query_idx in range(query_ref.shape[0]):
                query = query_ref[query_idx]
                row = jnp.zeros((1, lanes), F32)
                for seq in range(blocks_ref.shape[0]):
                    product = jnp.sum(query * blocks_ref[seq], axis=0, keepdims=True)
                    value = jnp.sum(product, axis=1, keepdims=True)
                    lane = lax.broadcasted_iota(jnp.int32, (1, lanes), 1)
                    row = jnp.where(lane == seq, value, row)
                rows.append(row)
        stacked = jnp.concatenate(rows, axis=0)
        total = stacked if total is None else total + stacked
    out_ref[...] = total


def score_terms(pairs):
    rows = sum(query.shape[0] for query in pairs[0][0])
    flat = [array for queries, blocks in pairs for array in (*queries, blocks)]
    groups = tuple(len(queries) for queries, _ in pairs)
    return pl.pallas_call(
        lambda *refs: score_kernel(groups, *refs),
        out_shape=jax.ShapeDtypeStruct((rows, 128), F32),
        compiler_params=params(),
        cost_estimate=cost(
            sum(2 * rows * blocks.size for _, blocks in pairs), sum(4 * a.size for a in flat)
        ),
        name="score_terms",
    )(*flat)


def local(
    train_grads,
    train_acts,
    train_ids,
    query_grads,
    query_acts,
    query_ids,
    token_weight,
    out_proj,
    in_proj,
    out_factor,
    in_factor,
):
    layers, train_n = train_grads.shape[:2]
    heads, rank = in_proj.shape[1:3]
    n_head, n_dp = lax.axis_size("head"), lax.axis_size("dp")
    by_pairs = n_head == 4 and n_dp == 4 and layers == 2 and query_ids.shape[0] == 1
    norm = 1.0 / math.sqrt(layers * heads * n_head * rank * rank)

    def layer_at(idx):
        return jnp.full((1,), idx, jnp.int32)

    def near(array, axis="head"):
        return lax.ppermute(array, axis, NEAR)

    def far(array, axis="head"):
        return lax.ppermute(array, axis, FAR)

    if by_pairs:
        mine = (lax.axis_index("head") % 2).astype(jnp.int32).reshape(1)
        order = [mine, 1 - mine]

        def summed(grads):
            sent = near(side_partial(order[1], grads, out_proj))
            pair = side_partial(order[0], grads, out_proj) + sent
            whole = pair + far(pair)
            return [whole, near(whole)]
    else:
        order = [layer_at(idx) for idx in range(layers)]

        def summed(grads):
            return [lax.psum(side_partial(at, grads, out_proj), "head") for at in order]

    query_sides = summed(query_grads)
    train_sides = summed(train_grads)
    query_in = in_side(query_acts, in_proj)
    scale = token_scale(jnp.concatenate([query_ids, train_ids]), token_weight)
    query_scale, train_scale = scale[: query_ids.shape[0]], scale[query_ids.shape[0] :]
    train_in = in_side(train_acts, in_proj)

    pairs = []
    for at, query_side, train_side in zip(order, query_sides, train_sides):
        ready = query_ready(at, query_side, query_scale, query_in, out_factor, in_factor)
        if by_pairs:
            across = far(ready, "dp")
            every = [ready, near(ready, "dp"), across, near(across, "dp")]
        else:
            every = [lax.all_gather(ready, "dp", axis=0, tiled=True)]
        pairs.append((every, train_blocks(at, train_side, train_scale, train_in)))
    terms = score_terms(pairs)

    if by_pairs:
        terms = terms[jnp.arange(4) ^ lax.axis_index("dp")]
        total = terms
        for shift in range(1, 4):
            total = total + lax.ppermute(
                terms, "head", [(idx, (idx + shift) % 4) for idx in range(4)]
            )
    else:
        total = lax.psum(terms, "head")
    return total[:, :train_n] * norm


def solution(mesh):
    return jax.shard_map(
        local,
        mesh=mesh,
        in_specs=(
            P(None, ("groups", "dp"), None, "head"),
            P(None, ("groups", "dp"), None, "head"),
            P(("groups", "dp"), None),
            P(None, ("groups", "dp"), None, "head"),
            P(None, ("groups", "dp"), None, "head"),
            P(("groups", "dp"), None),
            P(),
            P(None, None, "head"),
            P(None, "head", None, None),
            P(),
            P(None, "head", None, None),
        ),
        out_specs=P(None, ("groups", "dp")),
        check_vma=False,
    )
```

time: 157 us -> 63.8 us (0.41)
  matrix products: 53.9 us -> 0 us
  local copies, waits for them, and re-layouts: 39.7 us -> 1.66 us
  Pallas kernels: 0 us -> 23.7 us
  starting transfers between devices: 0.04 us -> 19.9 us
  waiting for transfers between devices: 34.9 us -> 17.3 us
  between operations: 13.6 us -> 0.29 us
  blocking collectives: 9.9 us -> 0 us
  other arithmetic: 4.32 us -> 0.7 us
    dot_general x13 -> x0, matrix products: 53.9 us -> none  [the longest x1 21.3 us: local(): jnp.einsum('lqhij,lnhij->qn', every_query, train_ready, precision=HIGH)]
    psum x1 -> x0, waiting for transfers between devices: 34.8 us -> none  [local(): lax.psum((partial_side(train_grads, out_proj), partial_side(query_grads,...]
    pallas_call x0 -> x12, Pallas kernels: none -> 23.7 us  [the longest x4 9.01 us: side_partial(): pl.pallas_call(side_kernel, out_shape=jax.ShapeDtypeStruct((count, rank,...]
    ppermute x0 -> x15, starting transfers between devices: none -> 19.9 us  [the longest x4 8.16 us: far(): return lax.ppermute(array, axis, FAR)]
    ppermute x0 -> x15, waiting for transfers between devices: none -> 17.3 us  [the longest x4 10.8 us: far(): return lax.ppermute(array, axis, FAR)]
    slice x4 -> x1, local copies, waits for them, and re-layouts: 13.3 us -> 0.01 us  [local(): scale[query_ids.shape[0]:]]
    psum x1 -> x0, blocking collectives: 9.9 us -> none  [local(): return lax.psum(partial_scores, 'head') * norm]
    gather x3 -> x1, local copies, waits for them, and re-layouts: 8.06 us -> 0.56 us  [local(): terms = terms[jnp.arange(4) ^ lax.axis_index('dp')]]
  transfers between devices with their start and end apart: 2 -> 15, of which waited for: 1 -> 7; matrix products, arithmetic and copies ran while one was open for 34% -> 0% of each run, Pallas kernels for 0% -> 29%
where the time goes in v1:
time: 63.8 us; the launch traced here: 63.5 us
  Pallas kernels  23.7 us (37%)
  starting transfers between devices  19.9 us (31%)
  waiting for transfers between devices  17.3 us (27%)
  local copies, waits for them, and re-layouts  1.66 us (3%)
  other arithmetic  0.7 us (1%)
    ppermute x4, waiting for transfers between devices, far(): return lax.ppermute(array, axis, FAR)  10.8 us
    pallas_call x4, Pallas kernels, side_partial(): pl.pallas_call(side_kernel, out_shape=jax.ShapeDtypeStruct((count, rank,...  9.01 us
    pallas_call x2, Pallas kernels, in_side(): pl.pallas_call(in_kernel, out_shape=jax.ShapeDtypeStruct((layers, count,...  8.29 us
    ppermute x4, starting transfers between devices, far(): return lax.ppermute(array, axis, FAR)  8.16 us
    ppermute x3, starting transfers between devices, local(): lax.ppermute(terms, 'head', [(idx, (idx + shift) % 4) for idx in range(4)])  6.15 us
    ppermute x8, starting transfers between devices, near(): return lax.ppermute(array, axis, NEAR)  5.57 us
    ppermute x8, waiting for transfers between devices, near(): return lax.ppermute(array, axis, NEAR)  5.1 us
    pallas_call x2, Pallas kernels, query_ready(): pl.pallas_call(query_kernel, out_shape=jax.ShapeDtypeStruct((count, rank,...  1.89 us
  transfers between devices with their start and end apart: 15, of which 7 were waited for; matrix products, arithmetic and copies ran while one was open for 0% of the time, Pallas kernels for 29%

profile of v1, /device:TPU:0, one launch (start us, length us, event | category | flops | bytes accessed | tf_op | source)
XLA Modules:
  0.0 63.5 jit_solution(4180199091070277074)
XLA Ops:
  0.0 0.0 copy-start.1
  0.0 1.0 %copy-done.1 = bf16[2,64,2048]{2,1,0:T(8,128)(2,1)S(1)} copy-done((bf16[2,64,2048]{2,1,0:T(8,128)(2,1)S(1)}, bf16[2,64,2048]{2,1,0:T(8,128)(2,1)}, u32[]{:S(2)}) %copy-start.1) | copy-done | bytes 524312
  1.0 0.0 copy-start
  1.0 0.0 copy-start.2
  1.0 4.1 %side_partial.7 = f32[4,64,256]{2,1,0:T(8,128)S(1)} custom-call(s32[1]{0:T(128)S(6)} %sub.3.layer_ref, bf16[2,4,256,2048]{3,2,1,0:T(8,128)(2,1)} %grads_ref.7, bf16[2,64,2048]{2,1,0:T(8,128)(2,1)S(1)} %copy-done.1), custom_call_target="tpu_custom_call" | custom-call | flops 1073741824 | bytes 4456448 | tf_op jit(solution)/shard_map/side_partial/pallas_call | solution.py:36
  5.2 0.0 copy-start.8
  5.2 0.0 copy-start.9
  5.2 0.0 copy-start.7
  5.2 3.1 %collective-permute-start.5 = (f32[4,64,256]{2,1,0:T(8,128)S(1)}, f32[4,64,256]{2,1,0:T(8,128)S(1)}, u32[]{:S(2)}, u32[]{:S(2)}) collective-permute-start(f32[4,64,256]{2,1,0:T(8,128)S(1)} %side_partial.7), channel_id=1, source_target_pairs={{0,1},{1,0},{2,3},{3,2},{4,5},{5,4},{6,7},{7,6},{8,9},{9,8},{10,11... | collective-permute-start | bytes 786440 | tf_op jit(solution)/shard_map/ppermute | solution.py:261
  8.3 0.0 copy-done
  8.3 0.5 side_partial.5
  8.8 0.1 collective-permute-start
  8.9 0.0 copy-done.2
  8.9 0.5 side_partial.4
  9.3 0.0 copy-done.8
  9.3 0.0 copy-done.9
  9.4 0.0 copy-done.7
  9.4 1.5 %token_scale.1 = f32[5,256]{1,0:T(8,128)S(1)} custom-call(s32[5,256]{1,0:T(8,128)S(1)} %pad_add_fusion.ids_ref, f32[1002,128]{1,0:T(8,128)S(1)} %bitcast.6), custom_call_target="tpu_custom_call" | custom-call | flops 985006080 | bytes 513024 | tf_op jit(solution)/shard_map/token_scale/pallas_call | solution.py:113
  10.9 5.1 %collective-permute-done = f32[1,64,256]{2,1,0:T(8,128)S(1)} collective-permute-done((f32[1,64,256]{2,1,0:T(8,128)S(1)}, f32[1,64,256]{2,1,0:T(8,128)S(1)}, u32[]{:S(2)}, u32[]{:S(2)}) %collective-permute-start) | collective-permute-done | bytes 65568 | tf_op jit(solution)/shard_map/ppermute | solution.py:261
  16.0 2.8 %collective-permute-start.1 = (f32[1,64,256]{2,1,0:T(8,128)S(1)}, f32[1,64,256]{2,1,0:T(8,128)S(1)}, u32[]{:S(2)}, u32[]{:S(2)}) collective-permute-start(f32[1,64,256]{2,1,0:T(8,128)S(1)} %add.36), channel_id=1, source_target_pairs={{0,2},{2,0},{1,3},{3,1},{4,6},{6,4},{5,7},{7,5},{8,10},{10,8},{9,1... | collective-permute-start | bytes 196616 | tf_op jit(solution)/shard_map/ppermute | solution.py:264
  18.8 2.4 %collective-permute-done.1 = f32[1,64,256]{2,1,0:T(8,128)S(1)} collective-permute-done((f32[1,64,256]{2,1,0:T(8,128)S(1)}, f32[1,64,256]{2,1,0:T(8,128)S(1)}, u32[]{:S(2)}, u32[]{:S(2)}) %collective-permute-start.1) | collective-permute-done | bytes 65568 | tf_op jit(solution)/shard_map/ppermute | solution.py:264
  21.3 0.0 copy-start.4
  21.3 0.0 copy-start.5
  21.3 0.0 copy-start.3
  21.3 0.0 copy-start.6
  21.3 1.8 %collective-permute-start.7 = (f32[1,64,256]{2,1,0:T(8,128)S(1)}, f32[1,64,256]{2,1,0:T(8,128)S(1)}, u32[]{:S(2)}, u32[]{:S(2)}) collective-permute-start(f32[1,64,256]{2,1,0:T(8,128)S(1)} %add.37.side_ref), channel_id=1, source_target_pairs={{0,1},{1,0},{2,3},{3,2},{4,5},{5,4},{6,7},{7,6},{8,9},{9,8},{10,11... | collective-permute-start | bytes 196616 | tf_op jit(solution)/shard_map/ppermute | solution.py:261
  23.1 4.0 %side_partial.6 = f32[4,64,256]{2,1,0:T(8,128)S(1)} custom-call(s32[1]{0:T(128)} %bitcast.layer_ref, bf16[2,4,256,2048]{3,2,1,0:T(8,128)(2,1)} %grads_ref.7, bf16[2,64,2048]{2,1,0:T(8,128)(2,1)S(1)} %copy-done.2), custom_call_target="tpu_custom_call" | custom-call | flops 1073741824 | bytes 4456448 | tf_op jit(solution)/shard_map/side_partial/pallas_call | solution.py:36
  27.1 0.0 copy-done.4
  27.1 0.0 copy-done.5
  27.1 0.9 %in_side.2.in_ref = bf16[2,1,256,1024]{3,2,1,0:T(8,128)(2,1)S(1)} custom-call(bf16[2,1,256,2048]{3,2,1,0:T(8,128)(2,1)S(1)} %copy-done.5, bf16[2,16,64,128]{3,2,1,0:T(8,128)(2,1)S(1)} %copy-done.4), custom_call_target="tpu_custom_call" | custom-call | flops 268435456 | bytes 3145728 | tf_op jit(solution)/shard_map/in_side/pallas_call | solution.py:72
  28.0 0.0 copy-done.3
  28.0 0.0 copy-done.6
  28.0 0.9 %query_ready.2.refs_0_ = f32[1,64,1024]{2,1,0:T(8,128)S(1)} custom-call(s32[1]{0:T(128)} %bitcast.layer_ref, f32[1,64,256]{2,1,0:T(8,128)S(1)} %add.37.side_ref, f32[1,1,256]{2,1,0:T(1,128)S(1)} %slice_bitcast_fusion.scale_ref, bf16[2,1,256,1024]{3,2,1,0:T(8,128)(2,1)S(1)} %in_side.2.in_ref, f32[2,64,64]{2,1,0:T(8,128)S(1)} %copy-done.6, ...), custom_call_target="tpu_custom_call" | custom-call | flops 335544320 | bytes 786432 | tf_op jit(solution)/shard_map/query_ready/pallas_call | solution.py:175
  29.0 1.5 %collective-permute-start.3 = (f32[1,64,1024]{2,1,0:T(8,128)S(1)}, f32[1,64,1024]{2,1,0:T(8,128)S(1)}, u32[]{:S(2)}, u32[]{:S(2)}) collective-permute-start(f32[1,64,1024]{2,1,0:T(8,128)S(1)} %query_ready.2.refs_0_), channel_id=1, source_target_pairs={{0,8},{8,0},{4,12},{12,4},{1,9},{9,1},{5,13},{13,5},{2,10},{10,2},... | collective-permute-start | bytes 786440 | tf_op jit(solution)/shard_map/ppermute | solution.py:264
  30.5 0.0 collective-permute-done.7.side_ref
  30.5 0.9 %query_ready.3.refs_5_ = f32[1,64,1024]{2,1,0:T(8,128)S(1)} custom-call(s32[1]{0:T(128)S(6)} %sub.3.layer_ref, f32[1,64,256]{2,1,0:T(8,128)S(1)} %collective-permute-done.7.side_ref, f32[1,1,256]{2,1,0:T(1,128)S(1)} %slice_bitcast_fusion.scale_ref, bf16[2,1,256,1024]{3,2,1,0:T(8,128)(2,1)S(1)} %in_side.2.in_ref, f32[2,64,64]{2,1,0:T(8,128)S(1)} %copy-done.6, ...), custom_call_target="tpu_custom_call" | custom-call | flops 335544320 | bytes 786432 | tf_op jit(solution)/shard_map/query_ready/pallas_call | solution.py:175
  31.5 0.6 collective-permute-start.9
  32.0 0.0 collective-permute-done.5
  32.1 3.2 %collective-permute-start.6 = (f32[4,64,256]{2,1,0:T(8,128)S(1)}, f32[4,64,256]{2,1,0:T(8,128)S(1)}, u32[]{:S(2)}, u32[]{:S(2)}) collective-permute-start(f32[4,64,256]{2,1,0:T(8,128)S(1)} %add.38), channel_id=1, source_target_pairs={{0,2},{2,0},{1,3},{3,1},{4,6},{6,4},{5,7},{7,5},{8,10},{10,8},{9,1... | collective-permute-start | bytes 786440 | tf_op jit(solution)/shard_map/ppermute | solution.py:264
  35.3 0.0 collective-permute-start.2
  35.3 0.5 collective-permute-start.8
  35.8 1.8 %collective-permute-done.3.refs_2_ = f32[1,64,1024]{2,1,0:T(8,128)S(1)} collective-permute-done((f32[1,64,1024]{2,1,0:T(8,128)S(1)}, f32[1,64,1024]{2,1,0:T(8,128)S(1)}, u32[]{:S(2)}, u32[]{:S(2)}) %collective-permute-start.3) | collective-permute-done | bytes 262176 | tf_op jit(solution)/shard_map/ppermute | solution.py:264
  37.7 0.0 collective-permute-start.4
  37.7 2.8 %collective-permute-done.9.refs_7_ = f32[1,64,1024]{2,1,0:T(8,128)S(1)} collective-permute-done((f32[1,64,1024]{2,1,0:T(8,128)S(1)}, f32[1,64,1024]{2,1,0:T(8,128)S(1)}, u32[]{:S(2)}, u32[]{:S(2)}) %collective-permute-start.9) | collective-permute-done | bytes 262176 | tf_op jit(solution)/shard_map/ppermute | solution.py:264
  40.5 0.0 collective-permute-start.10
  40.5 3.8 %collective-permute-done.6 = f32[4,64,256]{2,1,0:T(8,128)S(1)} collective-permute-done((f32[4,64,256]{2,1,0:T(8,128)S(1)}, f32[4,64,256]{2,1,0:T(8,128)S(1)}, u32[]{:S(2)}, u32[]{:S(2)}) %collective-permute-start.6) | collective-permute-done | bytes 262176 | tf_op jit(solution)/shard_map/ppermute | solution.py:264
  44.3 0.1 collective-permute-start.11
  44.4 7.4 %in_side.3.in_ref = bf16[2,4,256,1024]{3,2,1,0:T(8,128)(2,1)S(1)} custom-call(bf16[2,4,256,2048]{3,2,1,0:T(8,128)(2,1)} %acts_ref.3, bf16[2,16,64,128]{3,2,1,0:T(8,128)(2,1)S(1)} %copy-done.4), custom_call_target="tpu_custom_call" | custom-call | flops 1073741824 | bytes 12582912 | tf_op jit(solution)/shard_map/in_side/pallas_call | solution.py:72
  51.8 0.9 %train_blocks.2.refs_4_ = f32[4,64,1024]{2,1,0:T(8,128)S(1)} custom-call(s32[1]{0:T(128)} %bitcast.layer_ref, f32[4,64,256]{2,1,0:T(8,128)S(1)} %add.39.side_ref, f32[4,1,256]{2,1,0:T(1,128)S(1)} %reshape.33.scale_ref, bf16[2,4,256,1024]{3,2,1,0:T(8,128)(2,1)S(1)} %in_side.3.in_ref), custom_call_target="tpu_custom_call" | custom-call | flops 536870912 | bytes 3145728 | tf_op jit(solution)/shard_map/train_blocks/pallas_call | solution.py:134
  52.7 0.0 collective-permute-done.11.side_ref
  52.8 0.9 %train_blocks.3.refs_9_ = f32[4,64,1024]{2,1,0:T(8,128)S(1)} custom-call(s32[1]{0:T(128)S(6)} %sub.3.layer_ref, f32[4,64,256]{2,1,0:T(8,128)S(1)} %collective-permute-done.11.side_ref, f32[4,1,256]{2,1,0:T(1,128)S(1)} %reshape.33.scale_ref, bf16[2,4,256,1024]{3,2,1,0:T(8,128)(2,1)S(1)} %in_side.3.in_ref), custom_call_target="tpu_custom_call" | custom-call | flops 536870912 | bytes 3145728 | tf_op jit(solution)/shard_map/train_blocks/pallas_call | solution.py:134
  53.7 0.0 collective-permute-done.2.refs_1_
  53.7 0.0 collective-permute-done.8.refs_6_
  53.7 0.0 collective-permute-done.4.refs_3_
  53.7 0.0 collective-permute-done.10.refs_8_
  53.7 1.1 %score_terms.1 = f32[4,128]{1,0:T(4,128)S(1)} custom-call(f32[1,64,1024]{2,1,0:T(8,128)S(1)} %query_ready.2.refs_0_, f32[1,64,1024]{2,1,0:T(8,128)S(1)} %collective-permute-done.2.refs_1_, f32[1,64,1024]{2,1,0:T(8,128)S(1)} %collective-permute-done.3.refs_2_, f32[1,64,1024]{2,1,0:T(8,128)S(1)} %collective-permute-done.4.refs_3_, ...), custom_call_target="tpu_custom_call" | custom-call | flops 4194304 | bytes 4194304 | tf_op jit(solution)/shard_map/score_terms/pallas_call | solution.py:227
  54.9 0.6 gather_fusion
  55.4 2.0 %collective-permute-start.12 = (f32[4,128]{1,0:T(4,128)S(1)}, f32[4,128]{1,0:T(4,128)S(1)}, u32[]{:S(2)}, u32[]{:S(2)}) collective-permute-start(f32[4,128]{1,0:T(4,128)S(1)} %gather_fusion), channel_id=1, source_target_pairs={{0,1},{1,2},{2,3},{3,0},{4,5},{5,6},{6,7},{7,4},{8,9},{9,10},{10,1... | collective-permute-start | bytes 6152 | tf_op jit(solution)/shard_map/ppermute | solution.py:303
  57.5 1.3 %collective-permute-start.13 = (f32[4,128]{1,0:T(4,128)S(1)}, f32[4,128]{1,0:T(4,128)S(1)}, u32[]{:S(2)}, u32[]{:S(2)}) collective-permute-start(f32[4,128]{1,0:T(4,128)S(1)} %gather_fusion), channel_id=1, source_target_pairs={{0,2},{1,3},{2,0},{3,1},{4,6},{5,7},{6,4},{7,5},{8,10},{9,11},{10,... | collective-permute-start | bytes 6152 | tf_op jit(solution)/shard_map/ppermute | solution.py:303
  58.7 2.8 %collective-permute-start.14 = (f32[4,128]{1,0:T(4,128)S(1)}, f32[4,128]{1,0:T(4,128)S(1)}, u32[]{:S(2)}, u32[]{:S(2)}) collective-permute-start(f32[4,128]{1,0:T(4,128)S(1)} %gather_fusion), channel_id=1, source_target_pairs={{0,3},{1,0},{2,1},{3,2},{4,7},{5,4},{6,5},{7,6},{8,11},{9,8},{10,9... | collective-permute-start | bytes 6152 | tf_op jit(solution)/shard_map/ppermute | solution.py:303
  61.6 0.0 collective-permute-done.12
  61.6 0.4 collective-permute-done.13
  62.0 0.9 %collective-permute-done.14 = f32[4,128]{1,0:T(4,128)S(1)} collective-permute-done((f32[4,128]{1,0:T(4,128)S(1)}, f32[4,128]{1,0:T(4,128)S(1)}, u32[]{:S(2)}, u32[]{:S(2)}) %collective-permute-start.14) | collective-permute-done | bytes 2080 | tf_op jit(solution)/shard_map/ppermute | solution.py:303
  62.9 0.6 slice_multiply_fusion
  (11 shorter events, 0.1 us)
Async XLA Ops:
  0.0 1.0 %copy-start.1 = (bf16[2,64,2048]{2,1,0:T(8,128)(2,1)S(1)}, bf16[2,64,2048]{2,1,0:T(8,128)(2,1)}, u32[]{:S(2)}) copy-start(bf16[2,64,2048]{2,1,0:T(8,128)(2,1)} %proj_ref.10) | copy-start | bytes 1572868
  1.0 7.3 %copy-start = (bf16[2,1,256,2048]{3,2,1,0:T(8,128)(2,1)S(1)}, bf16[2,1,256,2048]{3,2,1,0:T(8,128)(2,1)}, u32[]{:S(2)}) copy-start(bf16[2,1,256,2048]{3,2,1,0:T(8,128)(2,1)} %grads_ref.5) | copy-start | bytes 6291460
  1.0 7.8 %copy-start.2 = (bf16[2,64,2048]{2,1,0:T(8,128)(2,1)S(1)}, bf16[2,64,2048]{2,1,0:T(8,128)(2,1)}, u32[]{:S(2)}) copy-start(bf16[2,64,2048]{2,1,0:T(8,128)(2,1)} %proj_ref.10) | copy-start | bytes 1572868
  5.2 4.2 %copy-start.8 = (s32[4,256]{1,0:T(4,128)S(1)}, s32[4,256]{1,0:T(4,128)}, u32[]{:S(2)}) copy-start(s32[4,256]{1,0:T(4,128)} %param.13) | copy-start | bytes 12292
  5.2 4.2 %copy-start.9 = (s32[1,256]{1,0:T(1,128)S(1)}, s32[1,256]{1,0:T(1,128)}, u32[]{:S(2)}) copy-start(s32[1,256]{1,0:T(1,128)} %param.16) | copy-start | bytes 3076
  5.2 4.2 %copy-start.7 = (f32[128256]{0:T(1024)S(1)}, f32[128256]{0:T(1024)}, u32[]{:S(2)}) copy-start(f32[128256]{0:T(1024)} %param.17) | copy-start | bytes 1539076
  5.2 26.8 %collective-permute-start.5 = (f32[4,64,256]{2,1,0:T(8,128)S(1)}, f32[4,64,256]{2,1,0:T(8,128)S(1)}, u32[]{:S(2)}, u32[]{:S(2)}) collective-permute-start(f32[4,64,256]{2,1,0:T(8,128)S(1)} %side_partial.7), channel_id=1, source_target_pairs={{0,1},{1,0},{2,3},{3,2},{4,5},{5,4},{6,7},{7,6},{8,9},{9,8},{10,11... | collective-permute-start | bytes 786440 | tf_op jit(solution)/shard_map/ppermute | solution.py:261
  8.8 7.2 %collective-permute-start = (f32[1,64,256]{2,1,0:T(8,128)S(1)}, f32[1,64,256]{2,1,0:T(8,128)S(1)}, u32[]{:S(2)}, u32[]{:S(2)}) collective-permute-start(f32[1,64,256]{2,1,0:T(8,128)S(1)} %side_partial.5), channel_id=1, source_target_pairs={{0,1},{1,0},{2,3},{3,2},{4,5},{5,4},{6,7},{7,6},{8,9},{9,8},{10,11... | collective-permute-start | bytes 196616 | tf_op jit(solution)/shard_map/ppermute | solution.py:261
  16.0 5.2 %collective-permute-start.1 = (f32[1,64,256]{2,1,0:T(8,128)S(1)}, f32[1,64,256]{2,1,0:T(8,128)S(1)}, u32[]{:S(2)}, u32[]{:S(2)}) collective-permute-start(f32[1,64,256]{2,1,0:T(8,128)S(1)} %add.36), channel_id=1, source_target_pairs={{0,2},{2,0},{1,3},{3,1},{4,6},{6,4},{5,7},{7,5},{8,10},{10,8},{9,1... | collective-permute-start | bytes 196616 | tf_op jit(solution)/shard_map/ppermute | solution.py:264
  21.3 5.8 %copy-start.4 = (bf16[2,16,64,128]{3,2,1,0:T(8,128)(2,1)S(1)}, bf16[2,16,64,128]{3,2,1,0:T(8,128)(2,1)}, u32[]{:S(2)}) copy-start(bf16[2,16,64,128]{3,2,1,0:T(8,128)(2,1)} %proj_ref.11) | copy-start | bytes 1572868
  21.3 5.8 %copy-start.5 = (bf16[2,1,256,2048]{3,2,1,0:T(8,128)(2,1)S(1)}, bf16[2,1,256,2048]{3,2,1,0:T(8,128)(2,1)}, u32[]{:S(2)}) copy-start(bf16[2,1,256,2048]{3,2,1,0:T(8,128)(2,1)} %acts_ref.2) | copy-start | bytes 6291460
  21.3 6.7 %copy-start.3 = (f32[2,16,64,64]{3,2,1,0:T(8,128)S(1)}, f32[2,16,64,64]{3,2,1,0:T(8,128)}, u32[]{:S(2)}) copy-start(f32[2,16,64,64]{3,2,1,0:T(8,128)} %in_factor_ref.3) | copy-start | bytes 1572868
  21.3 6.7 %copy-start.6 = (f32[2,64,64]{2,1,0:T(8,128)S(1)}, f32[2,64,64]{2,1,0:T(8,128)}, u32[]{:S(2)}) copy-start(f32[2,64,64]{2,1,0:T(8,128)} %out_factor_ref.3) | copy-start | bytes 98308
  21.3 9.2 %collective-permute-start.7 = (f32[1,64,256]{2,1,0:T(8,128)S(1)}, f32[1,64,256]{2,1,0:T(8,128)S(1)}, u32[]{:S(2)}, u32[]{:S(2)}) collective-permute-start(f32[1,64,256]{2,1,0:T(8,128)S(1)} %add.37.side_ref), channel_id=1, source_target_pairs={{0,1},{1,0},{2,3},{3,2},{4,5},{5,4},{6,7},{7,6},{8,9},{9,8},{10,11... | collective-permute-start | bytes 196616 | tf_op jit(solution)/shard_map/ppermute | solution.py:261
  29.0 8.7 %collective-permute-start.3 = (f32[1,64,1024]{2,1,0:T(8,128)S(1)}, f32[1,64,1024]{2,1,0:T(8,128)S(1)}, u32[]{:S(2)}, u32[]{:S(2)}) collective-permute-start(f32[1,64,1024]{2,1,0:T(8,128)S(1)} %query_ready.2.refs_0_), channel_id=1, source_target_pairs={{0,8},{8,0},{4,12},{12,4},{1,9},{9,1},{5,13},{13,5},{2,10},{10,2},... | collective-permute-start | bytes 786440 | tf_op jit(solution)/shard_map/ppermute | solution.py:264
  31.5 9.0 %collective-permute-start.9 = (f32[1,64,1024]{2,1,0:T(8,128)S(1)}, f32[1,64,1024]{2,1,0:T(8,128)S(1)}, u32[]{:S(2)}, u32[]{:S(2)}) collective-permute-start(f32[1,64,1024]{2,1,0:T(8,128)S(1)} %query_ready.3.refs_5_), channel_id=1, source_target_pairs={{0,8},{8,0},{4,12},{12,4},{1,9},{9,1},{5,13},{13,5},{2,10},{10,2},... | collective-permute-start | bytes 786440 | tf_op jit(solution)/shard_map/ppermute | solution.py:264
  32.1 12.2 %collective-permute-start.6 = (f32[4,64,256]{2,1,0:T(8,128)S(1)}, f32[4,64,256]{2,1,0:T(8,128)S(1)}, u32[]{:S(2)}, u32[]{:S(2)}) collective-permute-start(f32[4,64,256]{2,1,0:T(8,128)S(1)} %add.38), channel_id=1, source_target_pairs={{0,2},{2,0},{1,3},{3,1},{4,6},{6,4},{5,7},{7,5},{8,10},{10,8},{9,1... | collective-permute-start | bytes 786440 | tf_op jit(solution)/shard_map/ppermute | solution.py:264
  35.3 18.4 %collective-permute-start.2 = (f32[1,64,1024]{2,1,0:T(8,128)S(1)}, f32[1,64,1024]{2,1,0:T(8,128)S(1)}, u32[]{:S(2)}, u32[]{:S(2)}) collective-permute-start(f32[1,64,1024]{2,1,0:T(8,128)S(1)} %query_ready.2.refs_0_), channel_id=1, source_target_pairs={{0,4},{4,0},{8,12},{12,8},{1,5},{5,1},{9,13},{13,9},{2,6},{6,2},{1... | collective-permute-start | bytes 786440 | tf_op jit(solution)/shard_map/ppermute | solution.py:261
  35.3 18.4 %collective-permute-start.8 = (f32[1,64,1024]{2,1,0:T(8,128)S(1)}, f32[1,64,1024]{2,1,0:T(8,128)S(1)}, u32[]{:S(2)}, u32[]{:S(2)}) collective-permute-start(f32[1,64,1024]{2,1,0:T(8,128)S(1)} %query_ready.3.refs_5_), channel_id=1, source_target_pairs={{0,4},{4,0},{8,12},{12,8},{1,5},{5,1},{9,13},{13,9},{2,6},{6,2},{1... | collective-permute-start | bytes 786440 | tf_op jit(solution)/shard_map/ppermute | solution.py:261
  37.7 16.0 %collective-permute-start.4 = (f32[1,64,1024]{2,1,0:T(8,128)S(1)}, f32[1,64,1024]{2,1,0:T(8,128)S(1)}, u32[]{:S(2)}, u32[]{:S(2)}) collective-permute-start(f32[1,64,1024]{2,1,0:T(8,128)S(1)} %collective-permute-done.3.refs_2_), channel_id=1, source_target_pairs={{0,4},{4,0},{8,12},{12,8},{1,5},{5,1},{9,13},{13,9},{2,6},{6,2},{1... | collective-permute-start | bytes 786440 | tf_op jit(solution)/shard_map/ppermute | solution.py:261
  40.5 13.2 %collective-permute-start.10 = (f32[1,64,1024]{2,1,0:T(8,128)S(1)}, f32[1,64,1024]{2,1,0:T(8,128)S(1)}, u32[]{:S(2)}, u32[]{:S(2)}) collective-permute-start(f32[1,64,1024]{2,1,0:T(8,128)S(1)} %collective-permute-done.9.refs_7_), channel_id=1, source_target_pairs={{0,4},{4,0},{8,12},{12,8},{1,5},{5,1},{9,13},{13,9},{2,6},{6,2},{1... | collective-permute-start | bytes 786440 | tf_op jit(solution)/shard_map/ppermute | solution.py:261
  44.3 8.4 %collective-permute-start.11 = (f32[4,64,256]{2,1,0:T(8,128)S(1)}, f32[4,64,256]{2,1,0:T(8,128)S(1)}, u32[]{:S(2)}, u32[]{:S(2)}) collective-permute-start(f32[4,64,256]{2,1,0:T(8,128)S(1)} %add.39.side_ref), channel_id=1, source_target_pairs={{0,1},{1,0},{2,3},{3,2},{4,5},{5,4},{6,7},{7,6},{8,9},{9,8},{10,11... | collective-permute-start | bytes 786440 | tf_op jit(solution)/shard_map/ppermute | solution.py:261
  55.4 6.2 %collective-permute-start.12 = (f32[4,128]{1,0:T(4,128)S(1)}, f32[4,128]{1,0:T(4,128)S(1)}, u32[]{:S(2)}, u32[]{:S(2)}) collective-permute-start(f32[4,128]{1,0:T(4,128)S(1)} %gather_fusion), channel_id=1, source_target_pairs={{0,1},{1,2},{2,3},{3,0},{4,5},{5,6},{6,7},{7,4},{8,9},{9,10},{10,1... | collective-permute-start | bytes 6152 | tf_op jit(solution)/shard_map/ppermute | solution.py:303
  57.5 4.5 %collective-permute-start.13 = (f32[4,128]{1,0:T(4,128)S(1)}, f32[4,128]{1,0:T(4,128)S(1)}, u32[]{:S(2)}, u32[]{:S(2)}) collective-permute-start(f32[4,128]{1,0:T(4,128)S(1)} %gather_fusion), channel_id=1, source_target_pairs={{0,2},{1,3},{2,0},{3,1},{4,6},{5,7},{6,4},{7,5},{8,10},{9,11},{10,... | collective-permute-start | bytes 6152 | tf_op jit(solution)/shard_map/ppermute | solution.py:303
  58.7 4.2 %collective-permute-start.14 = (f32[4,128]{1,0:T(4,128)S(1)}, f32[4,128]{1,0:T(4,128)S(1)}, u32[]{:S(2)}, u32[]{:S(2)}) collective-permute-start(f32[4,128]{1,0:T(4,128)S(1)} %gather_fusion), channel_id=1, source_target_pairs={{0,3},{1,0},{2,1},{3,2},{4,7},{5,4},{6,5},{7,6},{8,11},{9,8},{10,9... | collective-permute-start | bytes 6152 | tf_op jit(solution)/shard_map/ppermute | solution.py:303

commit v2 on v1

v2 whole, which is shorter than its diff:
```python
import functools
import math

import jax
import jax.numpy as jnp
from jax import lax
from jax.experimental import pallas as pl
from jax.experimental.pallas import tpu as pltpu
from jax.sharding import PartitionSpec as P

HIGH = lax.Precision.HIGHEST
F32 = jnp.float32
BF16 = jnp.bfloat16
NT = (((1,), (1,)), ((), ()))
VMEM_LIMIT = 24 * 1024 * 1024
SCALE = 1.0

NEAR = [(0, 1), (1, 0), (2, 3), (3, 2)]
FAR = [(0, 2), (2, 0), (1, 3), (3, 1)]

WHOLE = pl.BlockSpec(memory_space=pltpu.VMEM)
IN_HBM = pl.BlockSpec(memory_space=pltpu.HBM)


def call(kernel, inputs, out_shape, name, *, micros, after=(), prefetch=(), grid=(1,),
         in_specs=None, out_specs=None, scratch=(), mebibytes=8):
    skip = len(prefetch) + len(inputs)

    def body(*refs):
        return kernel(*refs[:skip], *refs[skip + len(after) :])

    in_specs = in_specs or [WHOLE] * len(inputs)
    return pl.pallas_call(
        body,
        out_shape=out_shape,
        grid_spec=pltpu.PrefetchScalarGridSpec(
            num_scalar_prefetch=len(prefetch),
            grid=grid,
            in_specs=[*in_specs, *[pl.BlockSpec(memory_space=pl.ANY)] * len(after)],
            out_specs=out_specs or WHOLE,
            scratch_shapes=scratch,
        ),
        compiler_params=pltpu.CompilerParams(vmem_limit_bytes=mebibytes << 20),
        cost_estimate=pl.CostEstimate(
            flops=int(micros * SCALE * 1.1e9), bytes_accessed=0, transcendentals=0
        ),
        name=name,
    )(*prefetch, *inputs, *after)


def side_kernel(layer_ref, grads_ref, proj_ref, out_ref):
    side = lax.dot_general(grads_ref[0, 0], proj_ref[0], NT, preferred_element_type=F32)
    out_ref[0] = side.T


def side_partial(layer, grads, out_proj, micros, after=()):
    _, count, length, feats = grads.shape
    rank = out_proj.shape[1]
    return call(
        side_kernel,
        [grads, out_proj],
        jax.ShapeDtypeStruct((count, rank, length), F32),
        "side_partial",
        micros=micros,
        after=after,
        prefetch=[layer],
        grid=(count,),
        in_specs=[
            pl.BlockSpec((1, 1, length, feats), lambda i, l: (l[0], i, 0, 0)),
            pl.BlockSpec((1, rank, feats), lambda i, l: (l[0], 0, 0)),
        ],
        out_specs=pl.BlockSpec((1, rank, length), lambda i, l: (i, 0, 0)),
    )


def first_kernel(layer_ref, grads_hbm, proj_hbm, out_ref, grads, proj, sems):
    layer = layer_ref[0]
    copies = [
        pltpu.make_async_copy(grads_hbm.at[layer], grads, sems.at[0]),
        pltpu.make_async_copy(proj_hbm.at[layer], proj, sems.at[1]),
    ]
    for copy in copies:
        copy.start()
    for copy in copies:
        copy.wait()
    for seq in range(grads.shape[0]):
        out_ref[seq] = lax.dot_general(grads[seq], proj[...], NT, preferred_element_type=F32).T


def first_partial(layer, grads, out_proj, micros):
    _, count, length, feats = grads.shape
    rank = out_proj.shape[1]
    return call(
        first_kernel,
        [pltpu.with_memory_space_constraint(array, pltpu.HBM) for array in (grads, out_proj)],
        jax.ShapeDtypeStruct((count, rank, length), F32),
        "first_partial",
        micros=micros,
        prefetch=[layer],
        in_specs=[IN_HBM, IN_HBM],
        scratch=[
            pltpu.VMEM((count, length, feats), BF16),
            pltpu.VMEM((rank, feats), BF16),
            pltpu.SemaphoreType.DMA((2,)),
        ],
    )


def in_kernel(acts_ref, proj_ref, out_ref):
    heads, rank, width = proj_ref.shape[1:]
    none = jnp.zeros((rank, width), BF16)
    for pair in range(heads // 2):
        one, two = proj_ref[0, 2 * pair], proj_ref[0, 2 * pair + 1]
        both = jnp.concatenate(
            [jnp.concatenate([one, none], axis=1), jnp.concatenate([none, two], axis=1)], axis=0
        )
        acts = acts_ref[0, 0, :, 2 * width * pair : 2 * width * (pair + 1)]
        side = lax.dot_general(acts, both, NT, preferred_element_type=F32)
        out_ref[0, 0, :, 2 * rank * pair : 2 * rank * (pair + 1)] = side.astype(BF16)


def in_side(acts, in_proj, micros, after=()):
    layers, count, length, feats = acts.shape
    _, heads, rank, width = in_proj.shape
    return call(
        in_kernel,
        [acts, in_proj],
        jax.ShapeDtypeStruct((layers, count, length, heads * rank), BF16),
        "in_side",
        micros=micros,
        after=after,
        grid=(layers, count),
        in_specs=[
            pl.BlockSpec((1, 1, length, feats), lambda l, i: (l, i, 0, 0)),
            pl.BlockSpec((1, heads, rank, width), lambda l, i: (l, 0, 0, 0)),
        ],
        out_specs=pl.BlockSpec((1, 1, length, heads * rank), lambda l, i: (l, i, 0, 0)),
    )


def streamed_kernel(layer_ref, acts_hbm, proj_ref, one_ref, two_ref, tick_ref, acts, sems):
    layers, count = acts.shape[:2]
    order = [layer_ref[0], 1 - layer_ref[0]]
    heads, rank, width = proj_ref.shape[1:]
    steps = [(layer, seq) for layer in range(layers) for seq in range(count)]

    def copy(step):
        layer, seq = steps[step]
        return pltpu.make_async_copy(
            acts_hbm.at[order[layer], seq], acts.at[layer, seq], sems.at[step]
        )

    for step in range(len(steps)):
        copy(step).start()
    none = jnp.zeros((rank, width), BF16)
    for step, (layer, seq) in enumerate(steps):
        copy(step).wait()
        for pair in range(heads // 2):
            one, two = proj_ref[order[layer], 2 * pair], proj_ref[order[layer], 2 * pair + 1]
            both = jnp.concatenate(
                [jnp.concatenate([one, none], axis=1), jnp.concatenate([none, two], axis=1)],
                axis=0,
            )
            pair_acts = acts[layer, seq, :, 2 * width * pair : 2 * width * (pair + 1)]
            side = lax.dot_general(pair_acts, both, NT, preferred_element_type=F32)
            span = slice(2 * rank * pair, 2 * rank * (pair + 1))
            (one_ref, two_ref)[layer][0, seq, :, span] = side.astype(BF16)
    tick_ref[...] = jnp.zeros_like(tick_ref)


def in_side_streamed(layer, acts, in_proj, micros, after=()):
    layers, count, length, feats = acts.shape
    _, heads, rank, width = in_proj.shape
    return call(
        streamed_kernel,
        [pltpu.with_memory_space_constraint(acts, pltpu.HBM), in_proj],
        [
            jax.ShapeDtypeStruct((1, count, length, heads * rank), BF16),
            jax.ShapeDtypeStruct((1, count, length, heads * rank), BF16),
            jax.ShapeDtypeStruct((8, 128), F32),
        ],
        "in_side_streamed",
        micros=micros,
        mebibytes=20,
        prefetch=[layer],
        after=after,
        in_specs=[IN_HBM, WHOLE],
        out_specs=[WHOLE] * 3,
        scratch=[
            pltpu.VMEM(acts.shape, BF16),
            pltpu.SemaphoreType.DMA((layers * count,)),
        ],
    )


def settle_kernel(one_ref, two_ref, out_ref):
    out_ref[...] = one_ref[...] + two_ref[...]


def settle(one, two, after):
    return call(
        settle_kernel, [one, two], jax.ShapeDtypeStruct(one.shape, F32), "settle", micros=0.2,
        after=after,
    )


def token_kernel(ids_ref, table_ref, out_ref):
    table = table_ref[...]
    rows, lanes = table.shape
    high = table.astype(BF16)
    rest = table - high.astype(F32)
    mid = rest.astype(BF16)
    low = (rest - mid.astype(F32)).astype(BF16)
    turned = [part.T for part in (high, mid, low)]
    length = ids_ref.shape[1]
    for row in range(ids_ref.shape[0]):
        ids = ids_ref[row : row + 1, :]
        block = ids // lanes
        at = lax.broadcasted_iota(jnp.int32, (rows, length), 0) == block
        hot = jnp.where(at, 1.0, 0.0).astype(BF16)
        picked = sum(jnp.dot(part, hot, preferred_element_type=F32) for part in turned)
        lane = lax.broadcasted_iota(jnp.int32, (lanes, length), 0) == ids - block * lanes
        out_ref[row : row + 1, :] = jnp.sum(
            jnp.where(lane, picked, 0.0), axis=0, keepdims=True
        )


def token_scale(ids, token_weight, after=()):
    lanes = 128
    table = jnp.pad(token_weight, (0, -token_weight.shape[0] % lanes)).reshape(-1, lanes)
    return call(
        token_kernel,
        [ids, table],
        jax.ShapeDtypeStruct(ids.shape, F32),
        "token_scale",
        micros=1.5,
        after=after,
    )


def weighted_blocks(side, scale, in_side_seq, length):
    weighted = (side * scale).astype(BF16)
    return jnp.dot(weighted, in_side_seq, preferred_element_type=F32) * (1.0 / math.sqrt(length))


def blocks_kernel(side_ref, scale_ref, in_ref, out_ref):
    out_ref[0] = weighted_blocks(side_ref[0], scale_ref[0], in_ref[0, 0], side_ref.shape[2])


def train_blocks(side, scale, in_sides, after=()):
    count, rank, length = side.shape
    wide = in_sides.shape[3]
    return call(
        blocks_kernel,
        [side, scale.reshape(count, 1, length), in_sides],
        jax.ShapeDtypeStruct((count, rank, wide), F32),
        "train_blocks",
        micros=0.9,
        after=after,
        grid=(count,),
        in_specs=[
            pl.BlockSpec((1, rank, length), lambda i: (i, 0, 0)),
            pl.BlockSpec((1, 1, length), lambda i: (i, 0, 0)),
            pl.BlockSpec((1, 1, length, wide), lambda i: (0, i, 0, 0)),
        ],
        out_specs=pl.BlockSpec((1, rank, wide), lambda i: (i, 0, 0)),
    )


def query_kernel(terms_n, layer_ref, *refs):
    terms, refs = refs[:terms_n], refs[terms_n:]
    scale_ref, in_ref, out_factor_ref, in_factor_ref, out_ref, side_ref = refs
    heads, rank = in_factor_ref.shape[1], in_factor_ref.shape[2]
    side = sum(term[0] for term in terms)
    side_ref[0] = side
    blocks = weighted_blocks(side, scale_ref[0], in_ref[0, 0], side.shape[1])
    left = jnp.dot(out_factor_ref[0], blocks, precision=HIGH, preferred_element_type=F32)
    none = jnp.zeros((rank, rank), F32)
    for pair in range(heads // 2):
        one, two = in_factor_ref[0, 2 * pair], in_factor_ref[0, 2 * pair + 1]
        both = jnp.concatenate(
            [jnp.concatenate([one, none], axis=1), jnp.concatenate([none, two], axis=1)], axis=0
        )
        span = slice(2 * rank * pair, 2 * rank * (pair + 1))
        out_ref[0, :, span] = jnp.dot(
            left[:, span], both, precision=HIGH, preferred_element_type=F32
        )


def query_ready(layer, terms, scale, in_sides, out_factor, in_factor, after=()):
    count, rank, length = terms[0].shape
    wide = in_sides.shape[3]
    heads = in_factor.shape[1]
    side_spec = pl.BlockSpec((1, rank, length), lambda i, l: (i, 0, 0))
    return call(
        functools.partial(query_kernel, len(terms)),
        [*terms, scale.reshape(count, 1, length), in_sides, out_factor, in_factor],
        [
            jax.ShapeDtypeStruct((count, rank, wide), F32),
            jax.ShapeDtypeStruct((count, rank, length), F32),
        ],
        "query_ready",
        micros=0.9,
        after=after,
        prefetch=[layer],
        grid=(count,),
        in_specs=[
            *[side_spec] * len(terms),
            pl.BlockSpec((1, 1, length), lambda i, l: (i, 0, 0)),
            pl.BlockSpec((1, 1, length, wide), lambda i, l: (l[0], i, 0, 0)),
            pl.BlockSpec((1, rank, rank), lambda i, l: (l[0], 0, 0)),
            pl.BlockSpec((1, heads, rank, rank), lambda i, l: (l[0], 0, 0, 0)),
        ],
        out_specs=[pl.BlockSpec((1, rank, wide), lambda i, l: (i, 0, 0)), side_spec],
    )


def score_kernel(groups, norm, flip_ref, *refs):
    out_ref = refs[-1]
    rows, lanes = out_ref.shape
    row_at = lax.broadcasted_iota(jnp.int32, (rows, lanes), 0)
    lane_at = lax.broadcasted_iota(jnp.int32, (rows, lanes), 1)
    total = jnp.zeros((rows, lanes), F32)
    at = 0
    for queries_n in groups:
        query_refs = refs[at : at + queries_n]
        blocks_ref = refs[at + queries_n]
        at += queries_n + 1
        queries = [(ref, idx) for ref in query_refs for idx in range(ref.shape[0])]
        for row, (query_ref, idx) in enumerate(queries):
            mine = row_at == (row ^ flip_ref[0])
            query = query_ref[idx]
            for seq in range(blocks_ref.shape[0]):
                product = jnp.sum(query * blocks_ref[seq], axis=0, keepdims=True)
                value = jnp.sum(product, axis=1, keepdims=True) * norm
                total = total + jnp.where(mine & (lane_at == seq), value, 0.0)
    out_ref[...] = total


def score_terms(flip, norm, pairs):
    rows = sum(query.shape[0] for query in pairs[0][0])
    flat = [array for queries, blocks in pairs for array in (*queries, blocks)]
    groups = tuple(len(queries) for queries, _ in pairs)
    return call(
        lambda *refs: score_kernel(groups, norm, *refs),
        flat,
        jax.ShapeDtypeStruct((rows, 128), F32),
        "score_terms",
        micros=1.0,
        prefetch=[flip],
    )


def local(
    train_grads,
    train_acts,
    train_ids,
    query_grads,
    query_acts,
    query_ids,
    token_weight,
    out_proj,
    in_proj,
    out_factor,
    in_factor,
):
    layers, train_n = train_grads.shape[:2]
    query_n = query_ids.shape[0]
    heads, rank = in_proj.shape[1:3]
    n_head, n_dp = lax.axis_size("head"), lax.axis_size("dp")
    by_pairs = n_head == 4 and n_dp == 4 and layers == 2 and query_n == 1
    norm = 1.0 / math.sqrt(layers * heads * n_head * rank * rank)

    def scalar(idx):
        return jnp.asarray(idx, jnp.int32).reshape(1)

    def near(array, axis="head"):
        return lax.ppermute(array, axis, NEAR)

    def far(array, axis="head"):
        return lax.ppermute(array, axis, FAR)

    def ready(at, terms, after=()):
        return query_ready(at, terms, query_scale, query_in, out_factor, in_factor, after)

    if by_pairs:
        mine = scalar(lax.axis_index("head") % 2)
        other = 1 - mine
        query_out = first_partial(other, query_grads, out_proj, 5.0)
        query_got = near(query_out)
        query_keep = side_partial(mine, query_grads, out_proj, 0.5, [query_out])
        train_out = side_partial(other, train_grads, out_proj, 1.9, [query_keep])
        train_got = near(train_out)
        query_pair = query_keep + query_got
        query_far = far(query_pair)
        query_in = in_side(query_acts, in_proj, 0.9, [query_pair])
        query_scale = token_scale(query_ids, token_weight, [query_in])
        train_keep = side_partial(mine, train_grads, out_proj, 1.9, [query_scale])
        train_pair = train_keep + train_got
        ready_own, query_own = ready(mine, [query_pair, query_far], [train_pair])
        across_own = far(ready_own, "dp")
        ready_other, _ = ready(other, [near(query_own)], [ready_own])
        across_other = far(ready_other, "dp")
        train_scale = token_scale(train_ids, token_weight, [ready_other])
        train_own = train_pair + far(train_pair)
        train_other = near(train_own)
        *train_in, _ = in_side_streamed(mine, train_acts, in_proj, 5.0, [train_own])
        pairs = []
        for side, sides_in, query, across in (
            (train_own, train_in[0], ready_own, across_own),
            (train_other, train_in[1], ready_other, across_other),
        ):
            every = [query, near(query, "dp"), across, near(across, "dp")]
            pairs.append((every, train_blocks(side, train_scale, sides_in)))
        terms = score_terms(scalar(lax.axis_index("dp")), norm, pairs)
        total = terms
        for shift in range(1, 4):
            total = total + lax.ppermute(
                terms, "head", [(idx, (idx + shift) % 4) for idx in range(4)]
            )
    else:
        query_scale = token_scale(query_ids, token_weight)
        train_scale = token_scale(train_ids, token_weight)
        query_in = in_side(query_acts, in_proj, 0.9)
        train_in = in_side(train_acts, in_proj, 3.5)
        pairs = []
        for idx in range(layers):
            at = scalar(idx)
            query_side, train_side = lax.psum(
                (
                    side_partial(at, query_grads, out_proj, 0.5),
                    side_partial(at, train_grads, out_proj, 1.9),
                ),
                "head",
            )
            every = lax.all_gather(ready(at, [query_side])[0], "dp", axis=0, tiled=True)
            pairs.append(([every], train_blocks(train_side, train_scale, train_in[idx : idx + 1])))
        total = lax.psum(score_terms(scalar(0), norm, pairs), "head")
    return total[:, :train_n]


def solution(mesh):
    return jax.shard_map(
        local,
        mesh=mesh,
        in_specs=(
            P(None, ("groups", "dp"), None, "head"),
            P(None, ("groups", "dp"), None, "head"),
            P(("groups", "dp"), None),
            P(None, ("groups", "dp"), None, "head"),
            P(None, ("groups", "dp"), None, "head"),
            P(("groups", "dp"), None),
            P(),
            P(None, None, "head"),
            P(None, "head", None, None),
            P(),
            P(None, "head", None, None),
        ),
        out_specs=P(None, ("groups", "dp")),
        check_vma=False,
    )
```

time: 63.8 us -> 50.7 us (0.79)
  waiting for transfers between devices: 17.3 us -> 10.5 us
  Pallas kernels: 23.7 us -> 19.2 us
  local copies, waits for them, and re-layouts: 1.66 us -> 0.06 us
    pallas_call x12 -> x13, Pallas kernels: 23.7 us -> 19.2 us  [call(): pl.pallas_call(body, out_shape=out_shape, grid_spec=pltpu.PrefetchScalarG...]
    ppermute x4, waiting for transfers between devices: 10.8 us -> 6.93 us  [far(): return lax.ppermute(array, axis, FAR)]
    ppermute x8, starting transfers between devices: 5.57 us -> 8.64 us  [near(): return lax.ppermute(array, axis, NEAR)]
    ppermute x8, waiting for transfers between devices: 5.1 us -> 2.21 us  [near(): return lax.ppermute(array, axis, NEAR)]
    ppermute x4, starting transfers between devices: 8.16 us -> 6.63 us  [far(): return lax.ppermute(array, axis, FAR)]
    ppermute x3, starting transfers between devices: 6.15 us -> 4.62 us  [local(): lax.ppermute(terms, 'head', [(idx, (idx + shift) % 4) for idx in range(4)])]
    unnamed x20, local copies, waits for them, and re-layouts: 1.09 us -> 0.05 us
  transfers between devices with their start and end apart: 15 -> 15, of which waited for: 7 -> 7; matrix products, arithmetic and copies ran while one was open for 0% -> 0% of each run, Pallas kernels for 29% -> 30%
where the time goes in v2:
time: 50.7 us; the launch traced here: 50.5 us
  starting transfers between devices  19.9 us (39%)
  Pallas kernels  19.2 us (38%)
  waiting for transfers between devices  10.5 us (21%)
  other arithmetic  0.67 us (1%)
    pallas_call x13, Pallas kernels, call(): pl.pallas_call(body, out_shape=out_shape, grid_spec=pltpu.PrefetchScalarG...  19.2 us
    ppermute x8, starting transfers between devices, near(): return lax.ppermute(array, axis, NEAR)  8.64 us
    ppermute x4, waiting for transfers between devices, far(): return lax.ppermute(array, axis, FAR)  6.93 us
    ppermute x4, starting transfers between devices, far(): return lax.ppermute(array, axis, FAR)  6.63 us
    ppermute x3, starting transfers between devices, local(): lax.ppermute(terms, 'head', [(idx, (idx + shift) % 4) for idx in range(4)])  4.62 us
    ppermute x8, waiting for transfers between devices, near(): return lax.ppermute(array, axis, NEAR)  2.21 us
    ppermute x3, waiting for transfers between devices, local(): lax.ppermute(terms, 'head', [(idx, (idx + shift) % 4) for idx in range(4)])  1.34 us
  transfers between devices with their start and end apart: 15, of which 7 were waited for; matrix products, arithmetic and copies ran while one was open for 0% of the time, Pallas kernels for 30%

profile of v2, /device:TPU:0, one launch (start us, length us, event | category | flops | bytes accessed | tf_op | source)
XLA Modules:
  0.0 50.5 jit_solution(12517365626520032391)
XLA Ops:
  0.0 0.0 copy-start.1
  0.0 0.0 copy-start.3
  0.0 0.0 copy-start
  0.0 1.9 %first_partial.1.refs_3_ = f32[1,64,256]{2,1,0:T(8,128)S(1)} custom-call(s32[1]{0:T(128)S(6)} %sub.3.refs_0_, bf16[2,1,256,2048]{3,2,1,0:T(8,128)(2,1)} %refs_1_.7, bf16[2,64,2048]{2,1,0:T(8,128)(2,1)} %refs_2_.8), custom_call_target="tpu_custom_call" | custom-call | flops 5500000256 | tf_op jit(solution)/shard_map/first_partial/pallas_call | solution.py:33
  1.9 3.1 %collective-permute-start = (f32[1,64,256]{2,1,0:T(8,128)S(1)}, f32[1,64,256]{2,1,0:T(8,128)S(1)}, u32[]{:S(2)}, u32[]{:S(2)}) collective-permute-start(f32[1,64,256]{2,1,0:T(8,128)S(1)} %first_partial.1.refs_3_), channel_id=1, source_target_pairs={{0,1},{1,0},{2,3},{3,2},{4,5},{5,4},{6,7},{7,6},{8,9},{9,8},{10,11... | collective-permute-start | bytes 196616 | tf_op jit(solution)/shard_map/ppermute | solution.py:378
  5.0 0.0 copy-done.1
  5.0 0.0 copy-done.3
  5.0 0.5 side_partial.3.refs_3_
  5.5 0.0 copy-done
  5.5 0.0 copy-start.2
  5.5 0.0 copy-start.4
  5.5 1.9 %side_partial.5 = f32[4,64,256]{2,1,0:T(8,128)S(1)} custom-call(s32[1]{0:T(128)S(6)} %sub.3.refs_0_, bf16[2,4,256,2048]{3,2,1,0:T(8,128)(2,1)S(1)} %copy-done, bf16[2,64,2048]{2,1,0:T(8,128)(2,1)S(1)} %copy-done.1, f32[1,64,256]{2,1,0:T(8,128)S(1)} %side_partial.3.refs_3_), custom_call_target="tpu_custom_call" | custom-call | flops 2090000000 | tf_op jit(solution)/shard_map/side_partial/pallas_call | solution.py:33
  7.4 0.0 copy-start.6
  7.5 0.0 copy-start.9
  7.5 2.1 %collective-permute-start.2 = (f32[4,64,256]{2,1,0:T(8,128)S(1)}, f32[4,64,256]{2,1,0:T(8,128)S(1)}, u32[]{:S(2)}, u32[]{:S(2)}) collective-permute-start(f32[4,64,256]{2,1,0:T(8,128)S(1)} %side_partial.5), channel_id=1, source_target_pairs={{0,1},{1,0},{2,3},{3,2},{4,5},{5,4},{6,7},{7,6},{8,9},{9,8},{10,11... | collective-permute-start | bytes 786440 | tf_op jit(solution)/shard_map/ppermute | solution.py:378
  9.6 0.0 collective-permute-done
  9.6 2.7 %collective-permute-start.1 = (f32[1,64,256]{2,1,0:T(8,128)S(1)}, f32[1,64,256]{2,1,0:T(8,128)S(1)}, u32[]{:S(2)}, u32[]{:S(2)}) collective-permute-start(f32[1,64,256]{2,1,0:T(8,128)S(1)} %add.23.refs_2_.refs_1_), channel_id=1, source_target_pairs={{0,2},{2,0},{1,3},{3,1},{4,6},{6,4},{5,7},{7,5},{8,10},{10,8},{9,1... | collective-permute-start | bytes 196616 | tf_op jit(solution)/shard_map/ppermute | solution.py:381
  12.3 0.0 copy-done.2
  12.3 0.0 copy-done.4
  12.3 0.9 %in_side.1.refs_2_.refs_4_.refs_3_ = bf16[2,1,256,1024]{3,2,1,0:T(8,128)(2,1)S(1)} custom-call(bf16[2,1,256,2048]{3,2,1,0:T(8,128)(2,1)S(1)} %copy-done.2, bf16[2,16,64,128]{3,2,1,0:T(8,128)(2,1)S(1)} %copy-done.4, f32[1,64,256]{2,1,0:T(8,128)S(1)} %add.23.refs_2_.refs_1_), custom_call_target="tpu_custom_call" | custom-call | flops 990000000 | tf_op jit(solution)/shard_map/in_side/pallas_call | solution.py:33
  13.2 0.0 copy-done.6
  13.2 0.0 copy-done.9
  13.2 0.5 token_scale.2.refs_3_
  13.7 0.0 copy-start.5
  13.7 0.0 copy-start.7
  13.7 1.9 %side_partial.4 = f32[4,64,256]{2,1,0:T(8,128)S(1)} custom-call(s32[1]{0:T(128)} %bitcast.1.refs_0_, bf16[2,4,256,2048]{3,2,1,0:T(8,128)(2,1)S(1)} %copy-done, bf16[2,64,2048]{2,1,0:T(8,128)(2,1)S(1)} %copy-done.1, f32[1,256]{1,0:T(1,128)S(1)} %token_scale.2.refs_3_), custom_call_target="tpu_custom_call" | custom-call | flops 2090000000 | tf_op jit(solution)/shard_map/side_partial/pallas_call | solution.py:33
  15.6 1.7 %collective-permute-done.2 = f32[4,64,256]{2,1,0:T(8,128)S(1)} collective-permute-done((f32[4,64,256]{2,1,0:T(8,128)S(1)}, f32[4,64,256]{2,1,0:T(8,128)S(1)}, u32[]{:S(2)}, u32[]{:S(2)}) %collective-permute-start.2) | collective-permute-done | bytes 262176 | tf_op jit(solution)/shard_map/ppermute | solution.py:378
  17.4 0.0 collective-permute-done.1.refs_2_
  17.4 0.0 copy-done.5
  17.4 0.0 copy-done.7
  17.4 1.0 %query_ready.2 = (f32[1,64,1024]{2,1,0:T(8,128)S(1)}, f32[1,64,256]{2,1,0:T(8,128)S(1)}) custom-call(s32[1]{0:T(128)} %bitcast.1.refs_0_, f32[1,64,256]{2,1,0:T(8,128)S(1)} %add.23.refs_2_.refs_1_, f32[1,64,256]{2,1,0:T(8,128)S(1)} %collective-permute-done.1.refs_2_, f32[1,1,256]{2,1,0:T(1,128)S(1)} %bitcast.5, ...), custom_call_target="tpu_custom_call" | custom-call | flops 990000000 | tf_op jit(solution)/shard_map/query_ready/pallas_call | solution.py:33
  18.3 0.0 copy-start.8
  18.4 2.7 %collective-permute-start.7 = (f32[1,64,256]{2,1,0:T(8,128)S(1)}, f32[1,64,256]{2,1,0:T(8,128)S(1)}, u32[]{:S(2)}, u32[]{:S(2)}) collective-permute-start(f32[1,64,256]{2,1,0:T(8,128)S(1)} %get-tuple-element.11), channel_id=1, source_target_pairs={{0,1},{1,0},{2,3},{3,2},{4,5},{5,4},{6,7},{7,6},{8,9},{9,8},{10,11... | collective-permute-start | bytes 196616 | tf_op jit(solution)/shard_map/ppermute | solution.py:378
  21.1 1.6 %collective-permute-start.6 = (f32[4,64,256]{2,1,0:T(8,128)S(1)}, f32[4,64,256]{2,1,0:T(8,128)S(1)}, u32[]{:S(2)}, u32[]{:S(2)}) collective-permute-start(f32[4,64,256]{2,1,0:T(8,128)S(1)} %add.24.refs_7_), channel_id=1, source_target_pairs={{0,2},{2,0},{1,3},{3,1},{4,6},{6,4},{5,7},{7,5},{8,10},{10,8},{9,1... | collective-permute-start | bytes 786440 | tf_op jit(solution)/shard_map/ppermute | solution.py:381
  22.7 1.5 %collective-permute-start.4 = (f32[1,64,1024]{2,1,0:T(8,128)S(1)}, f32[1,64,1024]{2,1,0:T(8,128)S(1)}, u32[]{:S(2)}, u32[]{:S(2)}) collective-permute-start(f32[1,64,1024]{2,1,0:T(8,128)S(1)} %get-tuple-element.10.refs_6_.refs_1_), channel_id=1, source_target_pairs={{0,8},{8,0},{4,12},{12,4},{1,9},{9,1},{5,13},{13,5},{2,10},{10,2},... | collective-permute-start | bytes 786440 | tf_op jit(solution)/shard_map/ppermute | solution.py:381
  24.2 0.0 collective-permute-done.7.refs_1_
  24.2 0.9 %query_ready.3 = (f32[1,64,1024]{2,1,0:T(8,128)S(1)}, f32[1,64,256]{2,1,0:T(8,128)}) custom-call(s32[1]{0:T(128)S(6)} %sub.3.refs_0_, f32[1,64,256]{2,1,0:T(8,128)S(1)} %collective-permute-done.7.refs_1_, f32[1,1,256]{2,1,0:T(1,128)S(1)} %bitcast.6, bf16[2,1,256,1024]{3,2,1,0:T(8,128)(2,1)S(1)} %in_side.1.refs_2_.refs_4_.refs_3_, ...), custom_call_target="tpu_custom_call" | custom-call | flops 990000000 | tf_op jit(solution)/shard_map/query_ready/pallas_call | solution.py:33
  25.2 0.8 %collective-permute-start.9 = (f32[1,64,1024]{2,1,0:T(8,128)S(1)}, f32[1,64,1024]{2,1,0:T(8,128)S(1)}, u32[]{:S(2)}, u32[]{:S(2)}) collective-permute-start(f32[1,64,1024]{2,1,0:T(8,128)S(1)} %get-tuple-element.12.refs_2_.refs_6_), channel_id=1, source_target_pairs={{0,8},{8,0},{4,12},{12,4},{1,9},{9,1},{5,13},{13,5},{2,10},{10,2},... | collective-permute-start | bytes 786440 | tf_op jit(solution)/shard_map/ppermute | solution.py:381
  26.0 0.0 collective-permute-start.3
  26.0 0.5 %collective-permute-start.8 = (f32[1,64,1024]{2,1,0:T(8,128)S(1)}, f32[1,64,1024]{2,1,0:T(8,128)S(1)}, u32[]{:S(2)}, u32[]{:S(2)}) collective-permute-start(f32[1,64,1024]{2,1,0:T(8,128)S(1)} %get-tuple-element.12.refs_2_.refs_6_), channel_id=1, source_target_pairs={{0,4},{4,0},{8,12},{12,8},{1,5},{5,1},{9,13},{13,9},{2,6},{6,2},{1... | collective-permute-start | bytes 786440 | tf_op jit(solution)/shard_map/ppermute | solution.py:378
  26.6 0.0 copy-done.8
  26.6 1.3 %token_scale.3 = f32[4,256]{1,0:T(4,128)S(1)} custom-call(s32[4,256]{1,0:T(4,128)S(1)} %copy-done.8, f32[1002,128]{1,0:T(8,128)S(1)} %bitcast.8, f32[1,64,1024]{2,1,0:T(8,128)S(1)} %get-tuple-element.12.refs_2_.refs_6_), custom_call_target="tpu_custom_call" | custom-call | flops 1650000000 | tf_op jit(solution)/shard_map/token_scale/pallas_call | solution.py:33
  27.8 6.2 %collective-permute-done.6 = f32[4,64,256]{2,1,0:T(8,128)S(1)} collective-permute-done((f32[4,64,256]{2,1,0:T(8,128)S(1)}, f32[4,64,256]{2,1,0:T(8,128)S(1)}, u32[]{:S(2)}, u32[]{:S(2)}) %collective-permute-start.6) | collective-permute-done | bytes 262176 | tf_op jit(solution)/shard_map/ppermute | solution.py:381
  34.0 0.1 collective-permute-start.11
  34.1 0.0 collective-permute-done.4.refs_3_
  34.1 0.1 collective-permute-start.5
  34.2 0.8 %collective-permute-done.9.refs_8_ = f32[1,64,1024]{2,1,0:T(8,128)S(1)} collective-permute-done((f32[1,64,1024]{2,1,0:T(8,128)S(1)}, f32[1,64,1024]{2,1,0:T(8,128)S(1)}, u32[]{:S(2)}, u32[]{:S(2)}) %collective-permute-start.9) | collective-permute-done | bytes 262176 | tf_op jit(solution)/shard_map/ppermute | solution.py:381
  35.0 0.0 collective-permute-start.10
  35.0 5.3 %in_side_streamed.1 = (bf16[1,4,256,1024]{3,2,1,0:T(8,128)(2,1)S(1)}, bf16[1,4,256,1024]{3,2,1,0:T(8,128)(2,1)S(1)}, f32[8,128]{1,0:T(8,128)}) custom-call(s32[1]{0:T(128)} %bitcast.1.refs_0_, bf16[2,4,256,2048]{3,2,1,0:T(8,128)(2,1)} %refs_1_.11, bf16[2,16,64,128]{3,2,1,0:T(8,128)(2,1)S(1)} %copy-done.4, f32[4,64,256]{2,1,0:T(8,128)S(1)} %add.25.refs_3_.refs_0_), custom_call_target="tpu_custom_call" | custom-call | flops 5500000256 | tf_op jit(solution)/shard_map/in_side_streamed/pallas_call | solution.py:33
  40.3 0.9 %train_blocks.2.refs_5_ = f32[4,64,1024]{2,1,0:T(8,128)S(1)} custom-call(f32[4,64,256]{2,1,0:T(8,128)S(1)} %add.25.refs_3_.refs_0_, f32[4,1,256]{2,1,0:T(1,128)S(1)} %reshape.22.refs_1_, bf16[1,4,256,1024]{3,2,1,0:T(8,128)(2,1)S(1)} %get-tuple-element.13.refs_2_), custom_call_target="tpu_custom_call" | custom-call | flops 990000000 | tf_op jit(solution)/shard_map/train_blocks/pallas_call | solution.py:33
  41.2 0.5 collective-permute-done.11.refs_0_
  41.7 0.9 %train_blocks.3.refs_10_ = f32[4,64,1024]{2,1,0:T(8,128)S(1)} custom-call(f32[4,64,256]{2,1,0:T(8,128)S(1)} %collective-permute-done.11.refs_0_, f32[4,1,256]{2,1,0:T(1,128)S(1)} %reshape.22.refs_1_, bf16[1,4,256,1024]{3,2,1,0:T(8,128)(2,1)S(1)} %get-tuple-element.14.refs_2_), custom_call_target="tpu_custom_call" | custom-call | flops 990000000 | tf_op jit(solution)/shard_map/train_blocks/pallas_call | solution.py:33
  42.5 0.0 collective-permute-done.3.refs_2_
  42.6 0.0 collective-permute-done.8.refs_7_
  42.6 0.0 collective-permute-done.5.refs_4_
  42.6 0.0 collective-permute-done.10.refs_9_
  42.6 1.4 %score_terms.1 = f32[4,128]{1,0:T(4,128)S(1)} custom-call(s32[1]{0:T(128)} %bitcast.refs_0_, f32[1,64,1024]{2,1,0:T(8,128)S(1)} %get-tuple-element.10.refs_6_.refs_1_, f32[1,64,1024]{2,1,0:T(8,128)S(1)} %collective-permute-done.3.refs_2_, f32[1,64,1024]{2,1,0:T(8,128)S(1)} %collective-permute-done.4.refs_3_, ...), custom_call_target="tpu_custom_call" | custom-call | flops 1100000000 | tf_op jit(solution)/shard_map/score_terms/pallas_call | solution.py:33
  44.0 1.2 %collective-permute-start.12 = (f32[4,128]{1,0:T(4,128)S(1)}, f32[4,128]{1,0:T(4,128)S(1)}, u32[]{:S(2)}, u32[]{:S(2)}) collective-permute-start(f32[4,128]{1,0:T(4,128)S(1)} %score_terms.1), channel_id=1, source_target_pairs={{0,1},{1,2},{2,3},{3,0},{4,5},{5,6},{6,7},{7,4},{8,9},{9,10},{10,1... | collective-permute-start | bytes 6152 | tf_op jit(solution)/shard_map/ppermute | solution.py:418
  45.2 0.7 %collective-permute-start.13 = (f32[4,128]{1,0:T(4,128)S(1)}, f32[4,128]{1,0:T(4,128)S(1)}, u32[]{:S(2)}, u32[]{:S(2)}) collective-permute-start(f32[4,128]{1,0:T(4,128)S(1)} %score_terms.1), channel_id=1, source_target_pairs={{0,2},{1,3},{2,0},{3,1},{4,6},{5,7},{6,4},{7,5},{8,10},{9,11},{10,... | collective-permute-start | bytes 6152 | tf_op jit(solution)/shard_map/ppermute | solution.py:418
  45.9 2.8 %collective-permute-start.14 = (f32[4,128]{1,0:T(4,128)S(1)}, f32[4,128]{1,0:T(4,128)S(1)}, u32[]{:S(2)}, u32[]{:S(2)}) collective-permute-start(f32[4,128]{1,0:T(4,128)S(1)} %score_terms.1), channel_id=1, source_target_pairs={{0,3},{1,0},{2,1},{3,2},{4,7},{5,4},{6,5},{7,6},{8,11},{9,8},{10,9... | collective-permute-start | bytes 6152 | tf_op jit(solution)/shard_map/ppermute | solution.py:418
  48.6 0.8 %collective-permute-done.12 = f32[4,128]{1,0:T(4,128)S(1)} collective-permute-done((f32[4,128]{1,0:T(4,128)S(1)}, f32[4,128]{1,0:T(4,128)S(1)}, u32[]{:S(2)}, u32[]{:S(2)}) %collective-permute-start.12) | collective-permute-done | bytes 2080 | tf_op jit(solution)/shard_map/ppermute | solution.py:418
  49.4 0.3 collective-permute-done.13
  49.7 0.3 collective-permute-done.14
  50.0 0.6 %add_add_fusion = f32[4,128]{1,0:T(4,128)} fusion(f32[4,128]{1,0:T(4,128)S(1)} %collective-permute-done.14, f32[4,128]{1,0:T(4,128)S(1)} %collective-permute-done.13, f32[4,128]{1,0:T(4,128)S(1)} %score_terms.1, f32[4,128]{1,0:T(4,128)S(1)} %collective-permute-done.12), kind=kLoop, calls=%fused_computation | loop fusion | flops 1536 | bytes 10240 | tf_op jit(solution)/shard_map/add | solution.py:418
  (4 shorter events, 0.1 us)
Async XLA Ops:
  0.0 5.0 %copy-start.1 = (bf16[2,64,2048]{2,1,0:T(8,128)(2,1)S(1)}, bf16[2,64,2048]{2,1,0:T(8,128)(2,1)}, u32[]{:S(2)}) copy-start(bf16[2,64,2048]{2,1,0:T(8,128)(2,1)} %refs_2_.8) | copy-start | bytes 1572868
  0.0 5.0 %copy-start.3 = (bf16[2,1,256,2048]{3,2,1,0:T(8,128)(2,1)S(1)}, bf16[2,1,256,2048]{3,2,1,0:T(8,128)(2,1)}, u32[]{:S(2)}) copy-start(bf16[2,1,256,2048]{3,2,1,0:T(8,128)(2,1)} %refs_1_.7) | copy-start | bytes 6291460
  0.0 5.5 %copy-start = (bf16[2,4,256,2048]{3,2,1,0:T(8,128)(2,1)S(1)}, bf16[2,4,256,2048]{3,2,1,0:T(8,128)(2,1)}, u32[]{:S(2)}) copy-start(bf16[2,4,256,2048]{3,2,1,0:T(8,128)(2,1)} %refs_1_.10) | copy-start | bytes 25165828
  1.9 7.7 %collective-permute-start = (f32[1,64,256]{2,1,0:T(8,128)S(1)}, f32[1,64,256]{2,1,0:T(8,128)S(1)}, u32[]{:S(2)}, u32[]{:S(2)}) collective-permute-start(f32[1,64,256]{2,1,0:T(8,128)S(1)} %first_partial.1.refs_3_), channel_id=1, source_target_pairs={{0,1},{1,0},{2,3},{3,2},{4,5},{5,4},{6,7},{7,6},{8,9},{9,8},{10,11... | collective-permute-start | bytes 196616 | tf_op jit(solution)/shard_map/ppermute | solution.py:378
  5.5 6.8 %copy-start.2 = (bf16[2,1,256,2048]{3,2,1,0:T(8,128)(2,1)S(1)}, bf16[2,1,256,2048]{3,2,1,0:T(8,128)(2,1)}, u32[]{:S(2)}) copy-start(bf16[2,1,256,2048]{3,2,1,0:T(8,128)(2,1)} %refs_0_.3) | copy-start | bytes 6291460
  5.5 6.8 %copy-start.4 = (bf16[2,16,64,128]{3,2,1,0:T(8,128)(2,1)S(1)}, bf16[2,16,64,128]{3,2,1,0:T(8,128)(2,1)}, u32[]{:S(2)}) copy-start(bf16[2,16,64,128]{3,2,1,0:T(8,128)(2,1)} %refs_2_.9) | copy-start | bytes 1572868
  7.4 5.7 %copy-start.6 = (f32[128256]{0:T(1024)S(1)}, f32[128256]{0:T(1024)}, u32[]{:S(2)}) copy-start(f32[128256]{0:T(1024)} %param.17) | copy-start | bytes 1539076
  7.5 5.7 %copy-start.9 = (s32[1,256]{1,0:T(1,128)S(1)}, s32[1,256]{1,0:T(1,128)}, u32[]{:S(2)}) copy-start(s32[1,256]{1,0:T(1,128)} %refs_0_.4) | copy-start | bytes 3076
  7.5 9.9 %collective-permute-start.2 = (f32[4,64,256]{2,1,0:T(8,128)S(1)}, f32[4,64,256]{2,1,0:T(8,128)S(1)}, u32[]{:S(2)}, u32[]{:S(2)}) collective-permute-start(f32[4,64,256]{2,1,0:T(8,128)S(1)} %side_partial.5), channel_id=1, source_target_pairs={{0,1},{1,0},{2,3},{3,2},{4,5},{5,4},{6,7},{7,6},{8,9},{9,8},{10,11... | collective-permute-start | bytes 786440 | tf_op jit(solution)/shard_map/ppermute | solution.py:378
  9.6 7.7 %collective-permute-start.1 = (f32[1,64,256]{2,1,0:T(8,128)S(1)}, f32[1,64,256]{2,1,0:T(8,128)S(1)}, u32[]{:S(2)}, u32[]{:S(2)}) collective-permute-start(f32[1,64,256]{2,1,0:T(8,128)S(1)} %add.23.refs_2_.refs_1_), channel_id=1, source_target_pairs={{0,2},{2,0},{1,3},{3,1},{4,6},{6,4},{5,7},{7,5},{8,10},{10,8},{9,1... | collective-permute-start | bytes 196616 | tf_op jit(solution)/shard_map/ppermute | solution.py:381
  13.7 3.7 %copy-start.5 = (f32[2,16,64,64]{3,2,1,0:T(8,128)S(1)}, f32[2,16,64,64]{3,2,1,0:T(8,128)}, u32[]{:S(2)}) copy-start(f32[2,16,64,64]{3,2,1,0:T(8,128)} %refs_5_.3) | copy-start | bytes 1572868
  13.7 3.7 %copy-start.7 = (f32[2,64,64]{2,1,0:T(8,128)S(1)}, f32[2,64,64]{2,1,0:T(8,128)}, u32[]{:S(2)}) copy-start(f32[2,64,64]{2,1,0:T(8,128)} %refs_4_.1) | copy-start | bytes 98308
  18.3 8.2 %copy-start.8 = (s32[4,256]{1,0:T(4,128)S(1)}, s32[4,256]{1,0:T(4,128)}, u32[]{:S(2)}) copy-start(s32[4,256]{1,0:T(4,128)} %refs_0_.5) | copy-start | bytes 12292
  18.4 5.9 %collective-permute-start.7 = (f32[1,64,256]{2,1,0:T(8,128)S(1)}, f32[1,64,256]{2,1,0:T(8,128)S(1)}, u32[]{:S(2)}, u32[]{:S(2)}) collective-permute-start(f32[1,64,256]{2,1,0:T(8,128)S(1)} %get-tuple-element.11), channel_id=1, source_target_pairs={{0,1},{1,0},{2,3},{3,2},{4,5},{5,4},{6,7},{7,6},{8,9},{9,8},{10,11... | collective-permute-start | bytes 196616 | tf_op jit(solution)/shard_map/ppermute | solution.py:378
  21.1 12.9 %collective-permute-start.6 = (f32[4,64,256]{2,1,0:T(8,128)S(1)}, f32[4,64,256]{2,1,0:T(8,128)S(1)}, u32[]{:S(2)}, u32[]{:S(2)}) collective-permute-start(f32[4,64,256]{2,1,0:T(8,128)S(1)} %add.24.refs_7_), channel_id=1, source_target_pairs={{0,2},{2,0},{1,3},{3,1},{4,6},{6,4},{5,7},{7,5},{8,10},{10,8},{9,1... | collective-permute-start | bytes 786440 | tf_op jit(solution)/shard_map/ppermute | solution.py:381
  22.7 11.4 %collective-permute-start.4 = (f32[1,64,1024]{2,1,0:T(8,128)S(1)}, f32[1,64,1024]{2,1,0:T(8,128)S(1)}, u32[]{:S(2)}, u32[]{:S(2)}) collective-permute-start(f32[1,64,1024]{2,1,0:T(8,128)S(1)} %get-tuple-element.10.refs_6_.refs_1_), channel_id=1, source_target_pairs={{0,8},{8,0},{4,12},{12,4},{1,9},{9,1},{5,13},{13,5},{2,10},{10,2},... | collective-permute-start | bytes 786440 | tf_op jit(solution)/shard_map/ppermute | solution.py:381
  25.2 9.8 %collective-permute-start.9 = (f32[1,64,1024]{2,1,0:T(8,128)S(1)}, f32[1,64,1024]{2,1,0:T(8,128)S(1)}, u32[]{:S(2)}, u32[]{:S(2)}) collective-permute-start(f32[1,64,1024]{2,1,0:T(8,128)S(1)} %get-tuple-element.12.refs_2_.refs_6_), channel_id=1, source_target_pairs={{0,8},{8,0},{4,12},{12,4},{1,9},{9,1},{5,13},{13,5},{2,10},{10,2},... | collective-permute-start | bytes 786440 | tf_op jit(solution)/shard_map/ppermute | solution.py:381
  26.0 16.5 %collective-permute-start.3 = (f32[1,64,1024]{2,1,0:T(8,128)S(1)}, f32[1,64,1024]{2,1,0:T(8,128)S(1)}, u32[]{:S(2)}, u32[]{:S(2)}) collective-permute-start(f32[1,64,1024]{2,1,0:T(8,128)S(1)} %get-tuple-element.10.refs_6_.refs_1_), channel_id=1, source_target_pairs={{0,4},{4,0},{8,12},{12,8},{1,5},{5,1},{9,13},{13,9},{2,6},{6,2},{1... | collective-permute-start | bytes 786440 | tf_op jit(solution)/shard_map/ppermute | solution.py:378
  26.0 16.5 %collective-permute-start.8 = (f32[1,64,1024]{2,1,0:T(8,128)S(1)}, f32[1,64,1024]{2,1,0:T(8,128)S(1)}, u32[]{:S(2)}, u32[]{:S(2)}) collective-permute-start(f32[1,64,1024]{2,1,0:T(8,128)S(1)} %get-tuple-element.12.refs_2_.refs_6_), channel_id=1, source_target_pairs={{0,4},{4,0},{8,12},{12,8},{1,5},{5,1},{9,13},{13,9},{2,6},{6,2},{1... | collective-permute-start | bytes 786440 | tf_op jit(solution)/shard_map/ppermute | solution.py:378
  34.0 7.6 %collective-permute-start.11 = (f32[4,64,256]{2,1,0:T(8,128)S(1)}, f32[4,64,256]{2,1,0:T(8,128)S(1)}, u32[]{:S(2)}, u32[]{:S(2)}) collective-permute-start(f32[4,64,256]{2,1,0:T(8,128)S(1)} %add.25.refs_3_.refs_0_), channel_id=1, source_target_pairs={{0,1},{1,0},{2,3},{3,2},{4,5},{5,4},{6,7},{7,6},{8,9},{9,8},{10,11... | collective-permute-start | bytes 786440 | tf_op jit(solution)/shard_map/ppermute | solution.py:378
  34.1 8.4 %collective-permute-start.5 = (f32[1,64,1024]{2,1,0:T(8,128)S(1)}, f32[1,64,1024]{2,1,0:T(8,128)S(1)}, u32[]{:S(2)}, u32[]{:S(2)}) collective-permute-start(f32[1,64,1024]{2,1,0:T(8,128)S(1)} %collective-permute-done.4.refs_3_), channel_id=1, source_target_pairs={{0,4},{4,0},{8,12},{12,8},{1,5},{5,1},{9,13},{13,9},{2,6},{6,2},{1... | collective-permute-start | bytes 786440 | tf_op jit(solution)/shard_map/ppermute | solution.py:378
  35.0 7.6 %collective-permute-start.10 = (f32[1,64,1024]{2,1,0:T(8,128)S(1)}, f32[1,64,1024]{2,1,0:T(8,128)S(1)}, u32[]{:S(2)}, u32[]{:S(2)}) collective-permute-start(f32[1,64,1024]{2,1,0:T(8,128)S(1)} %collective-permute-done.9.refs_8_), channel_id=1, source_target_pairs={{0,4},{4,0},{8,12},{12,8},{1,5},{5,1},{9,13},{13,9},{2,6},{6,2},{1... | collective-permute-start | bytes 786440 | tf_op jit(solution)/shard_map/ppermute | solution.py:378
  44.0 5.4 %collective-permute-start.12 = (f32[4,128]{1,0:T(4,128)S(1)}, f32[4,128]{1,0:T(4,128)S(1)}, u32[]{:S(2)}, u32[]{:S(2)}) collective-permute-start(f32[4,128]{1,0:T(4,128)S(1)} %score_terms.1), channel_id=1, source_target_pairs={{0,1},{1,2},{2,3},{3,0},{4,5},{5,6},{6,7},{7,4},{8,9},{9,10},{10,1... | collective-permute-start | bytes 6152 | tf_op jit(solution)/shard_map/ppermute | solution.py:418
  45.2 4.5 %collective-permute-start.13 = (f32[4,128]{1,0:T(4,128)S(1)}, f32[4,128]{1,0:T(4,128)S(1)}, u32[]{:S(2)}, u32[]{:S(2)}) collective-permute-start(f32[4,128]{1,0:T(4,128)S(1)} %score_terms.1), channel_id=1, source_target_pairs={{0,2},{1,3},{2,0},{3,1},{4,6},{5,7},{6,4},{7,5},{8,10},{9,11},{10,... | collective-permute-start | bytes 6152 | tf_op jit(solution)/shard_map/ppermute | solution.py:418
  45.9 4.1 %collective-permute-start.14 = (f32[4,128]{1,0:T(4,128)S(1)}, f32[4,128]{1,0:T(4,128)S(1)}, u32[]{:S(2)}, u32[]{:S(2)}) collective-permute-start(f32[4,128]{1,0:T(4,128)S(1)} %score_terms.1), channel_id=1, source_target_pairs={{0,3},{1,0},{2,1},{3,2},{4,7},{5,4},{6,5},{7,6},{8,11},{9,8},{10,9... | collective-permute-start | bytes 6152 | tf_op jit(solution)/shard_map/ppermute | solution.py:418

commit v3 on v2

v3 whole, which is shorter than its diff:
```python
import functools
import math

import jax
import jax.numpy as jnp
from jax import lax
from jax.experimental import pallas as pl
from jax.experimental.pallas import tpu as pltpu
from jax.sharding import PartitionSpec as P

HIGH = lax.Precision.HIGHEST
F32 = jnp.float32
BF16 = jnp.bfloat16
NT = (((1,), (1,)), ((), ()))

NEAR = [(0, 1), (1, 0), (2, 3), (3, 2)]
FAR = [(0, 2), (2, 0), (1, 3), (3, 1)]

WHOLE = pl.BlockSpec(memory_space=pltpu.VMEM)
IN_HBM = pl.BlockSpec(memory_space=pltpu.HBM)


def call(kernel, inputs, out_shape, name, *, micros, after=(), prefetch=(), grid=(1,),
         in_specs=None, out_specs=None, scratch=(), mebibytes=8):
    skip = len(prefetch) + len(inputs)

    def body(*refs):
        return kernel(*refs[:skip], *refs[skip + len(after) :])

    in_specs = in_specs or [WHOLE] * len(inputs)
    return pl.pallas_call(
        body,
        out_shape=out_shape,
        grid_spec=pltpu.PrefetchScalarGridSpec(
            num_scalar_prefetch=len(prefetch),
            grid=grid,
            in_specs=[*in_specs, *[pl.BlockSpec(memory_space=pl.ANY)] * len(after)],
            out_specs=out_specs or WHOLE,
            scratch_shapes=scratch,
        ),
        compiler_params=pltpu.CompilerParams(vmem_limit_bytes=mebibytes << 20),
        cost_estimate=pl.CostEstimate(
            flops=int(micros * 1.1e9), bytes_accessed=0, transcendentals=0
        ),
        name=name,
    )(*prefetch, *inputs, *after)


def stage(layer):
    return pl.when(layer >= 0)


def in_hbm(array):
    return pltpu.with_memory_space_constraint(array, pltpu.HBM)


def hold(array, after):
    return pl.pallas_call(
        lambda *refs: None,
        out_shape=jax.ShapeDtypeStruct(array.shape, array.dtype),
        in_specs=[WHOLE, *[pl.BlockSpec(memory_space=pl.ANY)] * len(after)],
        out_specs=WHOLE,
        input_output_aliases={0: 0},
        compiler_params=pltpu.CompilerParams(vmem_limit_bytes=1 << 20),
        cost_estimate=pl.CostEstimate(flops=0, bytes_accessed=0, transcendentals=0),
        name="hold",
    )(array, *after)


def side_kernel(layer_ref, grads_ref, proj_ref, out_ref):
    side = lax.dot_general(grads_ref[0, 0], proj_ref[0], NT, preferred_element_type=F32)
    out_ref[0] = side.T


def side_partial(layer, grads, out_proj, micros, after=()):
    _, count, length, feats = grads.shape
    rank = out_proj.shape[1]
    return call(
        side_kernel,
        [grads, out_proj],
        jax.ShapeDtypeStruct((count, rank, length), F32),
        "side_partial",
        micros=micros,
        after=after,
        prefetch=[layer],
        grid=(count,),
        in_specs=[
            pl.BlockSpec((1, 1, length, feats), lambda i, l: (l[0], i, 0, 0)),
            pl.BlockSpec((1, rank, feats), lambda i, l: (l[0], 0, 0)),
        ],
        out_specs=pl.BlockSpec((1, rank, length), lambda i, l: (i, 0, 0)),
    )


def sides_of(layer, grads_ref, proj_ref, out_ref):
    for seq in range(out_ref.shape[0]):
        out_ref[seq] = lax.dot_general(
            grads_ref[layer, seq], proj_ref[layer], NT, preferred_element_type=F32
        ).T


def sides_kernel(layer_ref, grads_ref, proj_ref, out_ref):
    sides_of(layer_ref[0], grads_ref, proj_ref, out_ref)


def sides_partial(layer, grads, out_proj, micros, after=()):
    _, count, length, feats = grads.shape
    return call(
        sides_kernel,
        [grads, out_proj],
        jax.ShapeDtypeStruct((count, out_proj.shape[1], length), F32),
        "sides_partial",
        micros=micros,
        after=after,
        prefetch=[layer],
        mebibytes=4,
    )


def both_kernel(
    layer_ref, ids_ref, acts_ref, in_proj_ref, table_ref, grads_ref, proj_ref,
    in_ref, scale_ref, out_ref,
):
    for at in range(acts_ref.shape[0]):
        for seq in range(acts_ref.shape[1]):
            in_side_of(acts_ref.at[at, seq], in_proj_ref.at[at], in_ref, (at, seq))
    token_kernel(ids_ref, table_ref, scale_ref)
    sides_of(layer_ref[0], grads_ref, proj_ref, out_ref)


def query_in_and_side(
    layer, ids, acts, in_proj, token_weight, grads, out_proj, micros, after=()
):
    layers, acts_n, length, feats = acts.shape
    _, heads, rank, width = in_proj.shape
    count = grads.shape[1]
    return call(
        both_kernel,
        [ids, acts, in_proj, token_table(token_weight), grads, out_proj],
        [
            jax.ShapeDtypeStruct((layers, acts_n, length, heads * rank), BF16),
            jax.ShapeDtypeStruct(ids.shape, F32),
            jax.ShapeDtypeStruct((count, rank, length), F32),
        ],
        "query_in_and_side",
        micros=micros,
        after=after,
        mebibytes=8,
        prefetch=[layer],
        out_specs=[WHOLE] * 3,
    )


def first_kernel(layer_ref, grads_hbm, proj_hbm, out_ref, grads, proj, sems):
    layer = layer_ref[0]
    copies = [
        pltpu.make_async_copy(proj_hbm.at[layer], proj, sems.at[0]),
        pltpu.make_async_copy(grads_hbm.at[layer], grads, sems.at[1]),
    ]
    for copy in copies:
        copy.start()
    for copy in copies:
        copy.wait()

    @stage(layer)
    def _():
        for seq in range(grads.shape[0]):
            out_ref[seq] = lax.dot_general(
                grads[seq], proj[...], NT, preferred_element_type=F32
            ).T


def first_partial(layer, grads, out_proj, micros):
    _, count, length, feats = grads.shape
    rank = out_proj.shape[1]
    return call(
        first_kernel,
        [in_hbm(grads), in_hbm(out_proj)],
        jax.ShapeDtypeStruct((count, rank, length), F32),
        "first_partial",
        micros=micros,
        prefetch=[layer],
        in_specs=[IN_HBM, IN_HBM],
        scratch=[
            pltpu.VMEM((count, length, feats), BF16),
            pltpu.VMEM((rank, feats), BF16),
            pltpu.SemaphoreType.DMA((2,)),
        ],
    )


def in_side_of(acts, proj, out_ref, at):
    heads, rank, width = proj.shape
    none = jnp.zeros((rank, width), BF16)
    for pair in range(heads // 2):
        one, two = proj[2 * pair], proj[2 * pair + 1]
        both = jnp.concatenate(
            [jnp.concatenate([one, none], axis=1), jnp.concatenate([none, two], axis=1)], axis=0
        )
        pair_acts = acts[:, 2 * width * pair : 2 * width * (pair + 1)]
        side = lax.dot_general(pair_acts, both, NT, preferred_element_type=F32)
        out_ref[(*at, slice(None), slice(2 * rank * pair, 2 * rank * (pair + 1)))] = side.astype(
            BF16
        )


def in_kernel(acts_ref, proj_ref, out_ref):
    in_side_of(acts_ref.at[0, 0], proj_ref.at[0], out_ref, (0, 0))


def in_side(acts, in_proj, micros, after=()):
    layers, count, length, feats = acts.shape
    _, heads, rank, width = in_proj.shape
    return call(
        in_kernel,
        [acts, in_proj],
        jax.ShapeDtypeStruct((layers, count, length, heads * rank), BF16),
        "in_side",
        micros=micros,
        after=after,
        grid=(layers, count),
        in_specs=[
            pl.BlockSpec((1, 1, length, feats), lambda l, i: (l, i, 0, 0)),
            pl.BlockSpec((1, heads, rank, width), lambda l, i: (l, 0, 0, 0)),
        ],
        out_specs=pl.BlockSpec((1, 1, length, heads * rank), lambda l, i: (l, i, 0, 0)),
    )


def streamed_kernel(layer_ref, acts_hbm, proj_ref, one_ref, two_ref, acts, sems):
    layers, count = acts.shape[:2]
    order = [layer_ref[0], 1 - layer_ref[0]]
    steps = [(layer, seq) for layer in range(layers) for seq in range(count)]

    def copy(step):
        layer, seq = steps[step]
        return pltpu.make_async_copy(
            acts_hbm.at[order[layer], seq], acts.at[layer, seq], sems.at[step]
        )

    for step in range(len(steps)):
        copy(step).start()
    for step, (layer, seq) in enumerate(steps):
        copy(step).wait()

        @stage(layer_ref[0])
        def _():
            in_side_of(
                acts.at[layer, seq], proj_ref.at[order[layer]], (one_ref, two_ref)[layer], (seq,)
            )


def in_side_streamed(layer, acts, in_proj, micros, after=()):
    layers, count, length, feats = acts.shape
    _, heads, rank, width = in_proj.shape
    return call(
        streamed_kernel,
        [in_hbm(acts), in_proj],
        [jax.ShapeDtypeStruct((count, length, heads * rank), BF16)] * 2,
        "in_side_streamed",
        micros=micros,
        mebibytes=20,
        prefetch=[layer],
        after=after,
        in_specs=[IN_HBM, WHOLE],
        out_specs=[WHOLE] * 2,
        scratch=[
            pltpu.VMEM(acts.shape, BF16),
            pltpu.SemaphoreType.DMA((layers * count,)),
        ],
    )


def settle_kernel(one_ref, two_ref, out_ref):
    out_ref[...] = one_ref[...] + two_ref[...]


def settle(one, two, after):
    return call(
        settle_kernel, [one, two], jax.ShapeDtypeStruct(one.shape, F32), "settle", micros=0.1,
        after=after,
    )


def token_kernel(ids_ref, table_ref, out_ref):
    table = table_ref[...]
    rows, lanes = table.shape
    high = table.astype(BF16)
    rest = table - high.astype(F32)
    mid = rest.astype(BF16)
    low = (rest - mid.astype(F32)).astype(BF16)
    turned = [part.T for part in (high, mid, low)]
    length = ids_ref.shape[1]
    for row in range(ids_ref.shape[0]):
        ids = ids_ref[row : row + 1, :]
        block = ids // lanes
        at = lax.broadcasted_iota(jnp.int32, (rows, length), 0) == block
        hot = jnp.where(at, 1.0, 0.0).astype(BF16)
        picked = sum(jnp.dot(part, hot, preferred_element_type=F32) for part in turned)
        lane = lax.broadcasted_iota(jnp.int32, (lanes, length), 0) == ids - block * lanes
        out_ref[row : row + 1, :] = jnp.sum(
            jnp.where(lane, picked, 0.0), axis=0, keepdims=True
        )


def token_table(token_weight):
    lanes = 128
    return jnp.pad(token_weight, (0, -token_weight.shape[0] % lanes)).reshape(-1, lanes)


def token_scale(ids, token_weight, micros, after=()):
    table = token_table(token_weight)
    return call(
        token_kernel,
        [ids, table],
        jax.ShapeDtypeStruct(ids.shape, F32),
        "token_scale",
        micros=micros,
        after=after,
    )


def blocks_of(side, scale, in_side_seq):
    weighted = (side * scale).astype(BF16)
    product = jnp.dot(weighted, in_side_seq, preferred_element_type=F32)
    return product * (1.0 / math.sqrt(side.shape[1]))


def ready_kernel(layer_ref, own_ref, other_ref, scale_ref, in_ref, *refs):
    out_factor_ref, in_factor_ref, *out_refs = refs
    layers, heads, rank, _ = in_factor_ref.shape
    none = jnp.zeros((rank, rank), F32)
    for layer in range(layers):
        lefts = []
        for seq in range(out_refs[layer].shape[0]):
            side = jnp.where(layer_ref[0] == layer, own_ref[seq], other_ref[seq])
            blocks = blocks_of(side, scale_ref[seq : seq + 1, :], in_ref[layer, seq])
            lefts.append(
                jnp.dot(out_factor_ref[layer], blocks, precision=HIGH, preferred_element_type=F32)
            )
        for pair in range(heads // 2):
            one, two = in_factor_ref[layer, 2 * pair], in_factor_ref[layer, 2 * pair + 1]
            both = jnp.concatenate(
                [jnp.concatenate([one, none], axis=1), jnp.concatenate([none, two], axis=1)],
                axis=0,
            )
            span = slice(2 * rank * pair, 2 * rank * (pair + 1))
            for seq, left in enumerate(lefts):
                out_refs[layer][seq, :, span] = jnp.dot(
                    left[:, span], both, precision=HIGH, preferred_element_type=F32
                )


def query_ready(layer, own, other, scale, in_sides, out_factor, in_factor, after=()):
    layers, count, _, wide = in_sides.shape
    rank = own.shape[1]
    return call(
        ready_kernel,
        [own, other, scale, in_sides, out_factor, in_factor],
        [jax.ShapeDtypeStruct((count, rank, wide), F32)] * layers,
        "query_ready",
        micros=0.1,
        prefetch=[layer],
        after=after,
        out_specs=[WHOLE] * layers,
    )


def score_kernel(layers, queries_n, sides_n, first, norm, at_ref, *refs):
    query_refs, refs = refs[:queries_n], refs[queries_n:]
    side_refs, refs = refs[:sides_n], refs[sides_n:]
    scale_ref, in_ref, *before_refs, out_ref = refs
    rows, lanes = out_ref.shape
    row_at = lax.broadcasted_iota(jnp.int32, (rows, lanes), 0)
    lane_at = lax.broadcasted_iota(jnp.int32, (rows, lanes), 1)
    total = jnp.zeros((rows, lanes), F32)
    for ref in before_refs:
        total = total + ref[...]
    queries = [(refs, idx) for refs in zip(*[iter(query_refs)] * layers) for idx in range(refs[0].shape[0])]
    sides = [(ref, idx) for ref in side_refs for idx in range(ref.shape[0])]
    for seq, (side_ref, side_idx) in enumerate(sides, first):
        blocks = blocks_of(side_ref[side_idx], scale_ref[seq : seq + 1, :], in_ref[seq])
        for row, (layer_refs, idx) in enumerate(queries):
            query = layer_refs[0][idx]
            for layer in range(1, layers):
                query = jnp.where(at_ref[0] == layer, layer_refs[layer][idx], query)
            product = jnp.sum(query * blocks, axis=0, keepdims=True)
            value = jnp.sum(product, axis=1, keepdims=True) * norm
            here = (row_at == (row ^ at_ref[1])) & (lane_at == seq)
            total = total + jnp.where(here, value, 0.0)
    out_ref[...] = total


def score_terms(layer, flip, norm, queries, sides, scale, in_sides, before=(), first=0, micros=1.5):
    layers = len(queries[0])
    rows = sum(query[0].shape[0] for query in queries)
    flat = [array for query in queries for array in query]
    return call(
        functools.partial(score_kernel, layers, len(flat), len(sides), first, norm),
        [*flat, *sides, scale, in_sides, *before],
        jax.ShapeDtypeStruct((rows, 128), F32),
        "score_terms",
        micros=micros,
        prefetch=[jnp.concatenate([layer, flip])],
    )


def local(
    train_grads,
    train_acts,
    train_ids,
    query_grads,
    query_acts,
    query_ids,
    token_weight,
    out_proj,
    in_proj,
    out_factor,
    in_factor,
):
    layers, train_n = train_grads.shape[:2]
    query_n = query_ids.shape[0]
    heads, rank = in_proj.shape[1:3]
    n_head, n_dp = lax.axis_size("head"), lax.axis_size("dp")
    by_pairs = n_head == 4 and n_dp == 4 and layers == 2 and query_n == 1
    norm = 1.0 / math.sqrt(layers * heads * n_head * rank * rank)

    def scalar(idx):
        return jnp.asarray(idx, jnp.int32).reshape(1)

    def near(array, axis="head"):
        return lax.ppermute(array, axis, NEAR)

    def far(array, axis="head"):
        return lax.ppermute(array, axis, FAR)

    if by_pairs:
        mine = scalar(lax.axis_index("head") % 2)
        other = 1 - mine
        flip = scalar(lax.axis_index("dp"))
        query_out = first_partial(other, query_grads, out_proj, 8.0)
        query_got = near(query_out)
        train_out = sides_partial(other, train_grads, out_proj, 2.0, [query_out])
        query_keep = sides_partial(mine, query_grads, out_proj, 0.5, [train_out])
        query_pair = query_keep + query_got
        query_far = far(query_pair)
        train_got = near(train_out)
        query_in, query_scale, train_keep = query_in_and_side(
            mine, query_ids, query_acts, in_proj, token_weight, train_grads, out_proj, 3.0,
            [query_pair],
        )
        query_own = settle(query_pair, query_far, [query_scale])
        query_other = near(query_own)
        parts = [(i * train_n // 1, (i + 1) * train_n // 1) for i in range(1)]
        pairs = [train_keep[a:b] + train_got[a:b] for a, b in parts]
        ready = query_ready(
            mine, query_own, query_other, query_scale, query_in, out_factor, in_factor, pairs
        )
        across = [far(one, "dp") for one in ready]
        train_scale = token_scale(train_ids, token_weight, 0.1, ready[-1:])
        owns = [pair + far(pair) for pair in pairs]
        others = [near(own) for own in owns]
        across = [hold(one, owns[-1:]) for one in across]
        every = [
            ready,
            [near(one, "dp") for one in ready],
            across,
            [near(one, "dp") for one in across],
        ]
        in_own, in_other = in_side_streamed(mine, train_acts, in_proj, 5.0, owns)
        terms = score_terms(mine, flip, norm, every, owns, train_scale, in_own)
        for (first, _), part in zip(parts, others):
            terms = score_terms(
                other, flip, norm, every, [part], train_scale, in_other, [terms], first
            )
        total = terms
        for shift in range(1, 4):
            total = total + lax.ppermute(
                terms, "head", [(idx, (idx + shift) % 4) for idx in range(4)]
            )
    else:
        query_scale = token_scale(query_ids, token_weight, 0.5)
        train_scale = token_scale(train_ids, token_weight, 1.5)
        query_in = in_side(query_acts, in_proj, 0.9)
        train_in = in_side(train_acts, in_proj, 3.5)
        at = [scalar(idx) for idx in range(layers)]
        query_sides, train_sides = lax.psum(
            (
                [side_partial(idx, query_grads, out_proj, 0.5) for idx in at],
                [side_partial(idx, train_grads, out_proj, 1.9) for idx in at],
            ),
            "head",
        )
        ready = query_ready(
            at[0], *query_sides, query_scale, query_in, out_factor, in_factor
        )
        every = [[lax.all_gather(one, "dp", axis=0, tiled=True) for one in ready]]
        terms = []
        for layer, idx in enumerate(at):
            sides, in_sides = train_sides[layer], train_in[layer]
            before = terms[-1:]
            terms.append(
                score_terms(idx, scalar(0), norm, every, [sides], train_scale, in_sides, before)
            )
        total = lax.psum(terms[-1], "head")
    return total[:, :train_n]


def solution(mesh):
    return jax.shard_map(
        local,
        mesh=mesh,
        in_specs=(
            P(None, ("groups", "dp"), None, "head"),
            P(None, ("groups", "dp"), None, "head"),
            P(("groups", "dp"), None),
            P(None, ("groups", "dp"), None, "head"),
            P(None, ("groups", "dp"), None, "head"),
            P(("groups", "dp"), None),
            P(),
            P(None, None, "head"),
            P(None, "head", None, None),
            P(),
            P(None, "head", None, None),
        ),
        out_specs=P(None, ("groups", "dp")),
        check_vma=False,
    )
```

time: 50.7 us -> 49.3 us (0.972)
  Pallas kernels: 19.2 us -> 16.6 us
  waiting for transfers between devices: 10.5 us -> 12.9 us
  starting transfers between devices: 19.9 us -> 18.5 us
    pallas_call x13 -> x10, Pallas kernels: 19.2 us -> 16.6 us  [call(): pl.pallas_call(body, out_shape=out_shape, grid_spec=pltpu.PrefetchScalarG...]
    ppermute x4, waiting for transfers between devices: 6.93 us -> 8.79 us  [far(): return lax.ppermute(array, axis, FAR)]
    ppermute x4, starting transfers between devices: 6.63 us -> 4.79 us  [far(): return lax.ppermute(array, axis, FAR)]
    ppermute x8, starting transfers between devices: 8.64 us -> 9.15 us  [near(): return lax.ppermute(array, axis, NEAR)]
  transfers between devices with their start and end apart: 15 -> 15, of which waited for: 7 -> 6; matrix products, arithmetic and copies ran while one was open for 0% -> 0% of each run, Pallas kernels for 30% -> 27%
where the time goes in v3:
time: 49.3 us; the launch traced here: 49.2 us
  starting transfers between devices  18.5 us (38%)
  Pallas kernels  16.6 us (34%)
  waiting for transfers between devices  12.9 us (26%)
  other arithmetic  0.82 us (2%)
    pallas_call x10, Pallas kernels, call(): pl.pallas_call(body, out_shape=out_shape, grid_spec=pltpu.PrefetchScalarG...  16.6 us
    ppermute x8, starting transfers between devices, near(): return lax.ppermute(array, axis, NEAR)  9.15 us
    ppermute x4, waiting for transfers between devices, far(): return lax.ppermute(array, axis, FAR)  8.79 us
    ppermute x4, starting transfers between devices, far(): return lax.ppermute(array, axis, FAR)  4.79 us
    ppermute x3, starting transfers between devices, local(): lax.ppermute(terms, 'head', [(idx, (idx + shift) % 4) for idx in range(4)])  4.6 us
    ppermute x8, waiting for transfers between devices, near(): return lax.ppermute(array, axis, NEAR)  2.45 us
    ppermute x3, waiting for transfers between devices, local(): lax.ppermute(terms, 'head', [(idx, (idx + shift) % 4) for idx in range(4)])  1.68 us
  transfers between devices with their start and end apart: 15, of which 6 were waited for; matrix products, arithmetic and copies ran while one was open for 0% of the time, Pallas kernels for 27%

profile of v3, /device:TPU:0, one launch (start us, length us, event | category | flops | bytes accessed | tf_op | source)
XLA Modules:
  0.0 49.2 jit_solution(7007815407573251554)
XLA Ops:
  0.0 0.0 copy-start
  0.0 0.0 copy-start.1
  0.0 1.9 %first_partial.1.refs_3_ = f32[1,64,256]{2,1,0:T(8,128)S(1)} custom-call(s32[1]{0:T(128)S(6)} %sub.3.refs_0_, bf16[2,1,256,2048]{3,2,1,0:T(8,128)(2,1)} %refs_1_.7, bf16[2,64,2048]{2,1,0:T(8,128)(2,1)} %refs_6_.2), custom_call_target="tpu_custom_call" | custom-call | flops 8800000000 | tf_op jit(solution)/shard_map/first_partial/pallas_call | solution.py:31
  2.0 0.0 copy-start.2
  2.0 3.1 %collective-permute-start = (f32[1,64,256]{2,1,0:T(8,128)S(1)}, f32[1,64,256]{2,1,0:T(8,128)S(1)}, u32[]{:S(2)}, u32[]{:S(2)}) collective-permute-start(f32[1,64,256]{2,1,0:T(8,128)S(1)} %first_partial.1.refs_3_), channel_id=1, source_target_pairs={{0,1},{1,0},{2,3},{3,2},{4,5},{5,4},{6,7},{7,6},{8,9},{9,8},{10,11... | collective-permute-start | bytes 196616 | tf_op jit(solution)/shard_map/ppermute | solution.py:432
  5.1 0.0 copy-done
  5.1 0.0 copy-done.1
  5.1 1.3 %sides_partial.2.refs_3_ = f32[4,64,256]{2,1,0:T(8,128)S(1)} custom-call(s32[1]{0:T(128)S(6)} %sub.3.refs_0_, bf16[2,4,256,2048]{3,2,1,0:T(8,128)(2,1)S(1)} %copy-done, bf16[2,64,2048]{2,1,0:T(8,128)(2,1)S(1)} %copy-done.1, f32[1,64,256]{2,1,0:T(8,128)S(1)} %first_partial.1.refs_3_), custom_call_target="tpu_custom_call" | custom-call | flops 2200000000 | tf_op jit(solution)/shard_map/sides_partial/pallas_call | solution.py:31
  6.4 0.0 copy-start.4
  6.4 0.0 copy-start.7
  6.4 0.0 copy-start.8
  6.4 0.0 copy-start.9
  6.4 1.8 %collective-permute-start.3 = (f32[4,64,256]{2,1,0:T(8,128)S(1)}, f32[4,64,256]{2,1,0:T(8,128)S(1)}, u32[]{:S(2)}, u32[]{:S(2)}) collective-permute-start(f32[4,64,256]{2,1,0:T(8,128)S(1)} %sides_partial.2.refs_3_), channel_id=1, source_target_pairs={{0,1},{1,0},{2,3},{3,2},{4,5},{5,4},{6,7},{7,6},{8,9},{9,8},{10,11... | collective-permute-start | bytes 786440 | tf_op jit(solution)/shard_map/ppermute | solution.py:432
  8.3 0.0 copy-done.2
  8.3 0.5 sides_partial.3
  8.7 0.0 collective-permute-done
  8.8 2.7 %collective-permute-start.1 = (f32[1,64,256]{2,1,0:T(8,128)S(1)}, f32[1,64,256]{2,1,0:T(8,128)S(1)}, u32[]{:S(2)}, u32[]{:S(2)}) collective-permute-start(f32[1,64,256]{2,1,0:T(8,128)S(1)} %add.23.refs_7_.refs_0_), channel_id=1, source_target_pairs={{0,2},{2,0},{1,3},{3,1},{4,6},{6,4},{5,7},{7,5},{8,10},{10,8},{9,1... | collective-permute-start | bytes 196616 | tf_op jit(solution)/shard_map/ppermute | solution.py:435
  11.4 0.0 copy-done.4
  11.4 0.0 copy-done.7
  11.4 0.0 copy-done.8
  11.4 0.0 copy-done.9
  11.4 0.0 copy-start.3
  11.4 0.0 copy-start.5
  11.4 2.1 %query_in_and_side.1 = (bf16[2,1,256,1024]{3,2,1,0:T(8,128)(2,1)S(1)}, f32[1,256]{1,0:T(1,128)S(1)}, f32[4,64,256]{2,1,0:T(8,128)S(1)}) custom-call(s32[1]{0:T(128)} %bitcast.refs_0_, s32[1,256]{1,0:T(1,128)S(1)} %copy-done.9, bf16[2,1,256,2048]{3,2,1,0:T(8,128)(2,1)S(1)} %copy-done.7, bf16[2,16,64,128]{3,2,1,0:T(8,128)(2,1)S(1)} %copy-done.8, ...), custom_call_target="tpu_custom_call" | custom-call | flops 3300000000 | tf_op jit(solution)/shard_map/query_in_and_side/pallas_call | solution.py:31
  13.6 0.0 copy-start.6
  13.6 1.7 %collective-permute-done.1.refs_1_ = f32[1,64,256]{2,1,0:T(8,128)S(1)} collective-permute-done((f32[1,64,256]{2,1,0:T(8,128)S(1)}, f32[1,64,256]{2,1,0:T(8,128)S(1)}, u32[]{:S(2)}, u32[]{:S(2)}) %collective-permute-start.1) | collective-permute-done | bytes 65568 | tf_op jit(solution)/shard_map/ppermute | solution.py:435
  15.2 3.6 %collective-permute-start.2 = (f32[1,64,256]{2,1,0:T(8,128)S(1)}, f32[1,64,256]{2,1,0:T(8,128)S(1)}, u32[]{:S(2)}, u32[]{:S(2)}) collective-permute-start(f32[1,64,256]{2,1,0:T(8,128)S(1)} %settle.1.refs_1_), channel_id=1, source_target_pairs={{0,1},{1,0},{2,3},{3,2},{4,5},{5,4},{6,7},{7,6},{8,9},{9,8},{10,11... | collective-permute-start | bytes 196616 | tf_op jit(solution)/shard_map/ppermute | solution.py:432
  18.8 0.0 collective-permute-done.3
  18.8 0.1 collective-permute-start.7
  18.9 2.4 %collective-permute-done.2.refs_2_ = f32[1,64,256]{2,1,0:T(8,128)S(1)} collective-permute-done((f32[1,64,256]{2,1,0:T(8,128)S(1)}, f32[1,64,256]{2,1,0:T(8,128)S(1)}, u32[]{:S(2)}, u32[]{:S(2)}) %collective-permute-start.2) | collective-permute-done | bytes 65568 | tf_op jit(solution)/shard_map/ppermute | solution.py:432
  21.4 0.0 copy-done.3
  21.4 0.0 copy-done.5
  21.4 1.8 %query_ready.1 = (f32[1,64,1024]{2,1,0:T(8,128)S(1)}, f32[1,64,1024]{2,1,0:T(8,128)S(1)}) custom-call(s32[1]{0:T(128)} %bitcast.refs_0_, f32[1,64,256]{2,1,0:T(8,128)S(1)} %settle.1.refs_1_, f32[1,64,256]{2,1,0:T(8,128)S(1)} %collective-permute-done.2.refs_2_, f32[1,256]{1,0:T(1,128)S(1)} %get-tuple-element.12.refs_2_.refs_3_, ...), custom_call_target="tpu_custom_call" | custom-call | flops 110000000 | tf_op jit(solution)/shard_map/query_ready/pallas_call | solution.py:31
  23.2 1.5 %collective-permute-start.8 = (f32[1,64,1024]{2,1,0:T(8,128)S(1)}, f32[1,64,1024]{2,1,0:T(8,128)S(1)}, u32[]{:S(2)}, u32[]{:S(2)}) collective-permute-start(f32[1,64,1024]{2,1,0:T(8,128)S(1)} %get-tuple-element.16.refs_2_), channel_id=1, source_target_pairs={{0,8},{8,0},{4,12},{12,4},{1,9},{9,1},{5,13},{13,5},{2,10},{10,2},... | collective-permute-start | bytes 786440 | tf_op jit(solution)/shard_map/ppermute | solution.py:435
  24.7 0.5 %collective-permute-start.6 = (f32[1,64,1024]{2,1,0:T(8,128)S(1)}, f32[1,64,1024]{2,1,0:T(8,128)S(1)}, u32[]{:S(2)}, u32[]{:S(2)}) collective-permute-start(f32[1,64,1024]{2,1,0:T(8,128)S(1)} %get-tuple-element.15.refs_1_), channel_id=1, source_target_pairs={{0,8},{8,0},{4,12},{12,4},{1,9},{9,1},{5,13},{13,5},{2,10},{10,2},... | collective-permute-start | bytes 786440 | tf_op jit(solution)/shard_map/ppermute | solution.py:435
  25.2 0.1 pad_add_fusion.1.refs_0_
  25.3 0.1 pad_add_fusion.refs_0_
  25.4 0.0 collective-permute-start.4
  25.4 0.5 %collective-permute-start.5 = (f32[1,64,1024]{2,1,0:T(8,128)S(1)}, f32[1,64,1024]{2,1,0:T(8,128)S(1)}, u32[]{:S(2)}, u32[]{:S(2)}) collective-permute-start(f32[1,64,1024]{2,1,0:T(8,128)S(1)} %get-tuple-element.16.refs_2_), channel_id=1, source_target_pairs={{0,4},{4,0},{8,12},{12,8},{1,5},{5,1},{9,13},{13,9},{2,6},{6,2},{1... | collective-permute-start | bytes 786440 | tf_op jit(solution)/shard_map/ppermute | solution.py:432
  25.9 0.0 copy-done.6
  25.9 1.3 %token_scale.1.refs_10_ = f32[4,256]{1,0:T(4,128)S(1)} custom-call(s32[4,256]{1,0:T(4,128)S(1)} %copy-done.6, f32[1002,128]{1,0:T(8,128)S(1)} %bitcast.5, f32[1,64,1024]{2,1,0:T(8,128)S(1)} %get-tuple-element.16.refs_2_), custom_call_target="tpu_custom_call" | custom-call | flops 110000000 | tf_op jit(solution)/shard_map/token_scale/pallas_call | solution.py:31
  27.2 4.6 %collective-permute-done.7 = f32[4,64,256]{2,1,0:T(8,128)S(1)} collective-permute-done((f32[4,64,256]{2,1,0:T(8,128)S(1)}, f32[4,64,256]{2,1,0:T(8,128)S(1)}, u32[]{:S(2)}, u32[]{:S(2)}) %collective-permute-start.7) | collective-permute-done | bytes 262176 | tf_op jit(solution)/shard_map/ppermute | solution.py:435
  31.8 0.1 collective-permute-start.11
  31.9 0.0 collective-permute-done.8.refs_0_
  31.9 0.1 collective-permute-start.10
  32.0 2.5 %collective-permute-done.6.refs_0_ = f32[1,64,1024]{2,1,0:T(8,128)S(1)} collective-permute-done((f32[1,64,1024]{2,1,0:T(8,128)S(1)}, f32[1,64,1024]{2,1,0:T(8,128)S(1)}, u32[]{:S(2)}, u32[]{:S(2)}) %collective-permute-start.6) | collective-permute-done | bytes 262176 | tf_op jit(solution)/shard_map/ppermute | solution.py:435
  34.5 0.0 collective-permute-start.9
  34.5 4.8 %in_side_streamed.1 = (bf16[4,256,1024]{2,1,0:T(8,128)(2,1)S(1)}, bf16[4,256,1024]{2,1,0:T(8,128)(2,1)S(1)}) custom-call(s32[1]{0:T(128)} %bitcast.refs_0_, bf16[2,4,256,2048]{3,2,1,0:T(8,128)(2,1)} %refs_1_.9, bf16[2,16,64,128]{3,2,1,0:T(8,128)(2,1)S(1)} %copy-done.8, f32[4,64,256]{2,1,0:T(8,128)S(1)} %add.25.refs_1_.refs_3_.refs_9_), custom_call_target="tpu_custom_call" | custom-call | flops 5500000256 | tf_op jit(solution)/shard_map/in_side_streamed/pallas_call | solution.py:31
  39.3 0.0 collective-permute-done.4.refs_3_
  39.4 0.0 collective-permute-done.5.refs_4_
  39.4 0.0 collective-permute-done.10.refs_8_
  39.4 0.0 collective-permute-done.9.refs_7_
  39.4 1.5 %score_terms.2.refs_12_ = f32[4,128]{1,0:T(4,128)S(1)} custom-call(s32[2]{0:T(128)S(1)} %pad_add_fusion.1.refs_0_, f32[1,64,1024]{2,1,0:T(8,128)S(1)} %get-tuple-element.15.refs_1_, f32[1,64,1024]{2,1,0:T(8,128)S(1)} %get-tuple-element.16.refs_2_, f32[1,64,1024]{2,1,0:T(8,128)S(1)} %collective-permute-done.4.refs_3_, ...), custom_call_target="tpu_custom_call" | custom-call | flops 1650000000 | tf_op jit(solution)/shard_map/score_terms/pallas_call | solution.py:31
  40.9 0.0 collective-permute-done.11.refs_9_
  40.9 1.5 %score_terms.3 = f32[4,128]{1,0:T(4,128)S(1)} custom-call(s32[2]{0:T(128)S(1)} %pad_add_fusion.refs_0_, f32[1,64,1024]{2,1,0:T(8,128)S(1)} %get-tuple-element.15.refs_1_, f32[1,64,1024]{2,1,0:T(8,128)S(1)} %get-tuple-element.16.refs_2_, f32[1,64,1024]{2,1,0:T(8,128)S(1)} %collective-permute-done.4.refs_3_, ...), custom_call_target="tpu_custom_call" | custom-call | flops 1650000000 | tf_op jit(solution)/shard_map/score_terms/pallas_call | solution.py:31
  42.3 1.8 %collective-permute-start.12 = (f32[4,128]{1,0:T(4,128)S(1)}, f32[4,128]{1,0:T(4,128)S(1)}, u32[]{:S(2)}, u32[]{:S(2)}) collective-permute-start(f32[4,128]{1,0:T(4,128)S(1)} %score_terms.3), channel_id=1, source_target_pairs={{0,1},{1,2},{2,3},{3,0},{4,5},{5,6},{6,7},{7,4},{8,9},{9,10},{10,1... | collective-permute-start | bytes 6152 | tf_op jit(solution)/shard_map/ppermute | solution.py:478
  44.1 0.2 collective-permute-start.13
  44.4 2.6 %collective-permute-start.14 = (f32[4,128]{1,0:T(4,128)S(1)}, f32[4,128]{1,0:T(4,128)S(1)}, u32[]{:S(2)}, u32[]{:S(2)}) collective-permute-start(f32[4,128]{1,0:T(4,128)S(1)} %score_terms.3), channel_id=1, source_target_pairs={{0,3},{1,0},{2,1},{3,2},{4,7},{5,4},{6,5},{7,6},{8,11},{9,8},{10,9... | collective-permute-start | bytes 6152 | tf_op jit(solution)/shard_map/ppermute | solution.py:478
  46.9 0.8 %collective-permute-done.12 = f32[4,128]{1,0:T(4,128)S(1)} collective-permute-done((f32[4,128]{1,0:T(4,128)S(1)}, f32[4,128]{1,0:T(4,128)S(1)}, u32[]{:S(2)}, u32[]{:S(2)}) %collective-permute-start.12) | collective-permute-done | bytes 2080 | tf_op jit(solution)/shard_map/ppermute | solution.py:478
  47.8 0.8 %collective-permute-done.13 = f32[4,128]{1,0:T(4,128)S(1)} collective-permute-done((f32[4,128]{1,0:T(4,128)S(1)}, f32[4,128]{1,0:T(4,128)S(1)}, u32[]{:S(2)}, u32[]{:S(2)}) %collective-permute-start.13) | collective-permute-done | bytes 2080 | tf_op jit(solution)/shard_map/ppermute | solution.py:478
  48.6 0.0 collective-permute-done.14
  48.6 0.6 %add_add_fusion = f32[4,128]{1,0:T(4,128)} fusion(f32[4,128]{1,0:T(4,128)S(1)} %collective-permute-done.14, f32[4,128]{1,0:T(4,128)S(1)} %collective-permute-done.13, f32[4,128]{1,0:T(4,128)S(1)} %score_terms.3, f32[4,128]{1,0:T(4,128)S(1)} %collective-permute-done.12), kind=kLoop, calls=%fused_computation | loop fusion | flops 1536 | bytes 10240 | tf_op jit(solution)/shard_map/add | solution.py:478
  (6 shorter events, 0.1 us)
Async XLA Ops:
  0.0 5.1 %copy-start = (bf16[2,4,256,2048]{3,2,1,0:T(8,128)(2,1)S(1)}, bf16[2,4,256,2048]{3,2,1,0:T(8,128)(2,1)}, u32[]{:S(2)}) copy-start(bf16[2,4,256,2048]{3,2,1,0:T(8,128)(2,1)} %refs_5_.2) | copy-start | bytes 25165828
  0.0 5.1 %copy-start.1 = (bf16[2,64,2048]{2,1,0:T(8,128)(2,1)S(1)}, bf16[2,64,2048]{2,1,0:T(8,128)(2,1)}, u32[]{:S(2)}) copy-start(bf16[2,64,2048]{2,1,0:T(8,128)(2,1)} %refs_6_.2) | copy-start | bytes 1572868
  2.0 6.3 %copy-start.2 = (bf16[2,1,256,2048]{3,2,1,0:T(8,128)(2,1)S(1)}, bf16[2,1,256,2048]{3,2,1,0:T(8,128)(2,1)}, u32[]{:S(2)}) copy-start(bf16[2,1,256,2048]{3,2,1,0:T(8,128)(2,1)} %refs_1_.7) | copy-start | bytes 6291460
  2.0 6.8 %collective-permute-start = (f32[1,64,256]{2,1,0:T(8,128)S(1)}, f32[1,64,256]{2,1,0:T(8,128)S(1)}, u32[]{:S(2)}, u32[]{:S(2)}) collective-permute-start(f32[1,64,256]{2,1,0:T(8,128)S(1)} %first_partial.1.refs_3_), channel_id=1, source_target_pairs={{0,1},{1,0},{2,3},{3,2},{4,5},{5,4},{6,7},{7,6},{8,9},{9,8},{10,11... | collective-permute-start | bytes 196616 | tf_op jit(solution)/shard_map/ppermute | solution.py:432
  6.4 5.0 %copy-start.4 = (f32[128256]{0:T(1024)S(1)}, f32[128256]{0:T(1024)}, u32[]{:S(2)}) copy-start(f32[128256]{0:T(1024)} %param.17) | copy-start | bytes 1539076
  6.4 5.0 %copy-start.7 = (bf16[2,1,256,2048]{3,2,1,0:T(8,128)(2,1)S(1)}, bf16[2,1,256,2048]{3,2,1,0:T(8,128)(2,1)}, u32[]{:S(2)}) copy-start(bf16[2,1,256,2048]{3,2,1,0:T(8,128)(2,1)} %refs_2_.8) | copy-start | bytes 6291460
  6.4 5.0 %copy-start.8 = (bf16[2,16,64,128]{3,2,1,0:T(8,128)(2,1)S(1)}, bf16[2,16,64,128]{3,2,1,0:T(8,128)(2,1)}, u32[]{:S(2)}) copy-start(bf16[2,16,64,128]{3,2,1,0:T(8,128)(2,1)} %refs_2_.9) | copy-start | bytes 1572868
  6.4 5.0 %copy-start.9 = (s32[1,256]{1,0:T(1,128)S(1)}, s32[1,256]{1,0:T(1,128)}, u32[]{:S(2)}) copy-start(s32[1,256]{1,0:T(1,128)} %refs_1_.8) | copy-start | bytes 3076
  6.4 12.4 %collective-permute-start.3 = (f32[4,64,256]{2,1,0:T(8,128)S(1)}, f32[4,64,256]{2,1,0:T(8,128)S(1)}, u32[]{:S(2)}, u32[]{:S(2)}) collective-permute-start(f32[4,64,256]{2,1,0:T(8,128)S(1)} %sides_partial.2.refs_3_), channel_id=1, source_target_pairs={{0,1},{1,0},{2,3},{3,2},{4,5},{5,4},{6,7},{7,6},{8,9},{9,8},{10,11... | collective-permute-start | bytes 786440 | tf_op jit(solution)/shard_map/ppermute | solution.py:432
  8.8 6.5 %collective-permute-start.1 = (f32[1,64,256]{2,1,0:T(8,128)S(1)}, f32[1,64,256]{2,1,0:T(8,128)S(1)}, u32[]{:S(2)}, u32[]{:S(2)}) collective-permute-start(f32[1,64,256]{2,1,0:T(8,128)S(1)} %add.23.refs_7_.refs_0_), channel_id=1, source_target_pairs={{0,2},{2,0},{1,3},{3,1},{4,6},{6,4},{5,7},{7,5},{8,10},{10,8},{9,1... | collective-permute-start | bytes 196616 | tf_op jit(solution)/shard_map/ppermute | solution.py:435
  11.4 9.9 %copy-start.3 = (f32[2,16,64,64]{3,2,1,0:T(8,128)S(1)}, f32[2,16,64,64]{3,2,1,0:T(8,128)}, u32[]{:S(2)}) copy-start(f32[2,16,64,64]{3,2,1,0:T(8,128)} %refs_6_.3) | copy-start | bytes 1572868
  11.4 9.9 %copy-start.5 = (f32[2,64,64]{2,1,0:T(8,128)S(1)}, f32[2,64,64]{2,1,0:T(8,128)}, u32[]{:S(2)}) copy-start(f32[2,64,64]{2,1,0:T(8,128)} %refs_5_.3) | copy-start | bytes 98308
  13.6 12.3 %copy-start.6 = (s32[4,256]{1,0:T(4,128)S(1)}, s32[4,256]{1,0:T(4,128)}, u32[]{:S(2)}) copy-start(s32[4,256]{1,0:T(4,128)} %refs_0_.1) | copy-start | bytes 12292
  15.2 6.1 %collective-permute-start.2 = (f32[1,64,256]{2,1,0:T(8,128)S(1)}, f32[1,64,256]{2,1,0:T(8,128)S(1)}, u32[]{:S(2)}, u32[]{:S(2)}) collective-permute-start(f32[1,64,256]{2,1,0:T(8,128)S(1)} %settle.1.refs_1_), channel_id=1, source_target_pairs={{0,1},{1,0},{2,3},{3,2},{4,5},{5,4},{6,7},{7,6},{8,9},{9,8},{10,11... | collective-permute-start | bytes 196616 | tf_op jit(solution)/shard_map/ppermute | solution.py:432
  18.8 12.9 %collective-permute-start.7 = (f32[4,64,256]{2,1,0:T(8,128)S(1)}, f32[4,64,256]{2,1,0:T(8,128)S(1)}, u32[]{:S(2)}, u32[]{:S(2)}) collective-permute-start(f32[4,64,256]{2,1,0:T(8,128)S(1)} %add.24.refs_7_), channel_id=1, source_target_pairs={{0,2},{2,0},{1,3},{3,1},{4,6},{6,4},{5,7},{7,5},{8,10},{10,8},{9,1... | collective-permute-start | bytes 786440 | tf_op jit(solution)/shard_map/ppermute | solution.py:435
  23.2 8.7 %collective-permute-start.8 = (f32[1,64,1024]{2,1,0:T(8,128)S(1)}, f32[1,64,1024]{2,1,0:T(8,128)S(1)}, u32[]{:S(2)}, u32[]{:S(2)}) collective-permute-start(f32[1,64,1024]{2,1,0:T(8,128)S(1)} %get-tuple-element.16.refs_2_), channel_id=1, source_target_pairs={{0,8},{8,0},{4,12},{12,4},{1,9},{9,1},{5,13},{13,5},{2,10},{10,2},... | collective-permute-start | bytes 786440 | tf_op jit(solution)/shard_map/ppermute | solution.py:435
  24.7 9.8 %collective-permute-start.6 = (f32[1,64,1024]{2,1,0:T(8,128)S(1)}, f32[1,64,1024]{2,1,0:T(8,128)S(1)}, u32[]{:S(2)}, u32[]{:S(2)}) collective-permute-start(f32[1,64,1024]{2,1,0:T(8,128)S(1)} %get-tuple-element.15.refs_1_), channel_id=1, source_target_pairs={{0,8},{8,0},{4,12},{12,4},{1,9},{9,1},{5,13},{13,5},{2,10},{10,2},... | collective-permute-start | bytes 786440 | tf_op jit(solution)/shard_map/ppermute | solution.py:435
  25.4 14.0 %collective-permute-start.4 = (f32[1,64,1024]{2,1,0:T(8,128)S(1)}, f32[1,64,1024]{2,1,0:T(8,128)S(1)}, u32[]{:S(2)}, u32[]{:S(2)}) collective-permute-start(f32[1,64,1024]{2,1,0:T(8,128)S(1)} %get-tuple-element.15.refs_1_), channel_id=1, source_target_pairs={{0,4},{4,0},{8,12},{12,8},{1,5},{5,1},{9,13},{13,9},{2,6},{6,2},{1... | collective-permute-start | bytes 786440 | tf_op jit(solution)/shard_map/ppermute | solution.py:432
  25.4 14.0 %collective-permute-start.5 = (f32[1,64,1024]{2,1,0:T(8,128)S(1)}, f32[1,64,1024]{2,1,0:T(8,128)S(1)}, u32[]{:S(2)}, u32[]{:S(2)}) collective-permute-start(f32[1,64,1024]{2,1,0:T(8,128)S(1)} %get-tuple-element.16.refs_2_), channel_id=1, source_target_pairs={{0,4},{4,0},{8,12},{12,8},{1,5},{5,1},{9,13},{13,9},{2,6},{6,2},{1... | collective-permute-start | bytes 786440 | tf_op jit(solution)/shard_map/ppermute | solution.py:432
  31.8 9.1 %collective-permute-start.11 = (f32[4,64,256]{2,1,0:T(8,128)S(1)}, f32[4,64,256]{2,1,0:T(8,128)S(1)}, u32[]{:S(2)}, u32[]{:S(2)}) collective-permute-start(f32[4,64,256]{2,1,0:T(8,128)S(1)} %add.25.refs_1_.refs_3_.refs_9_), channel_id=1, source_target_pairs={{0,1},{1,0},{2,3},{3,2},{4,5},{5,4},{6,7},{7,6},{8,9},{9,8},{10,11... | collective-permute-start | bytes 786440 | tf_op jit(solution)/shard_map/ppermute | solution.py:432
  31.9 7.5 %collective-permute-start.10 = (f32[1,64,1024]{2,1,0:T(8,128)S(1)}, f32[1,64,1024]{2,1,0:T(8,128)S(1)}, u32[]{:S(2)}, u32[]{:S(2)}) collective-permute-start(f32[1,64,1024]{2,1,0:T(8,128)S(1)} %hold.3.refs_6_), channel_id=1, source_target_pairs={{0,4},{4,0},{8,12},{12,8},{1,5},{5,1},{9,13},{13,9},{2,6},{6,2},{1... | collective-permute-start | bytes 786440 | tf_op jit(solution)/shard_map/ppermute | solution.py:432
  34.5 4.9 %collective-permute-start.9 = (f32[1,64,1024]{2,1,0:T(8,128)S(1)}, f32[1,64,1024]{2,1,0:T(8,128)S(1)}, u32[]{:S(2)}, u32[]{:S(2)}) collective-permute-start(f32[1,64,1024]{2,1,0:T(8,128)S(1)} %hold.2.refs_5_), channel_id=1, source_target_pairs={{0,4},{4,0},{8,12},{12,8},{1,5},{5,1},{9,13},{13,9},{2,6},{6,2},{1... | collective-permute-start | bytes 786440 | tf_op jit(solution)/shard_map/ppermute | solution.py:432
  42.3 5.4 %collective-permute-start.12 = (f32[4,128]{1,0:T(4,128)S(1)}, f32[4,128]{1,0:T(4,128)S(1)}, u32[]{:S(2)}, u32[]{:S(2)}) collective-permute-start(f32[4,128]{1,0:T(4,128)S(1)} %score_terms.3), channel_id=1, source_target_pairs={{0,1},{1,2},{2,3},{3,0},{4,5},{5,6},{6,7},{7,4},{8,9},{9,10},{10,1... | collective-permute-start | bytes 6152 | tf_op jit(solution)/shard_map/ppermute | solution.py:478
  44.1 4.5 %collective-permute-start.13 = (f32[4,128]{1,0:T(4,128)S(1)}, f32[4,128]{1,0:T(4,128)S(1)}, u32[]{:S(2)}, u32[]{:S(2)}) collective-permute-start(f32[4,128]{1,0:T(4,128)S(1)} %score_terms.3), channel_id=1, source_target_pairs={{0,2},{1,3},{2,0},{3,1},{4,6},{5,7},{6,4},{7,5},{8,10},{9,11},{10,... | collective-permute-start | bytes 6152 | tf_op jit(solution)/shard_map/ppermute | solution.py:478
  44.4 4.3 %collective-permute-start.14 = (f32[4,128]{1,0:T(4,128)S(1)}, f32[4,128]{1,0:T(4,128)S(1)}, u32[]{:S(2)}, u32[]{:S(2)}) collective-permute-start(f32[4,128]{1,0:T(4,128)S(1)} %score_terms.3), channel_id=1, source_target_pairs={{0,3},{1,0},{2,1},{3,2},{4,7},{5,4},{6,5},{7,6},{8,11},{9,8},{10,9... | collective-permute-start | bytes 6152 | tf_op jit(solution)/shard_map/ppermute | solution.py:478

commit v4 on v3

--- a/solution.py
+++ b/solution.py
@@ -227,47 +227,53 @@
     )
 
 
-def streamed_kernel(layer_ref, acts_hbm, proj_ref, one_ref, two_ref, acts, sems):
-    layers, count = acts.shape[:2]
-    order = [layer_ref[0], 1 - layer_ref[0]]
-    steps = [(layer, seq) for layer in range(layers) for seq in range(count)]
-
-    def copy(step):
-        layer, seq = steps[step]
-        return pltpu.make_async_copy(
-            acts_hbm.at[order[layer], seq], acts.at[layer, seq], sems.at[step]
-        )
-
-    for step in range(len(steps)):
-        copy(step).start()
-    for step, (layer, seq) in enumerate(steps):
-        copy(step).wait()
-
-        @stage(layer_ref[0])
-        def _():
-            in_side_of(
-                acts.at[layer, seq], proj_ref.at[order[layer]], (one_ref, two_ref)[layer], (seq,)
-            )
-
-
-def in_side_streamed(layer, acts, in_proj, micros, after=()):
-    layers, count, length, feats = acts.shape
-    _, heads, rank, width = in_proj.shape
-    return call(
-        streamed_kernel,
-        [in_hbm(acts), in_proj],
-        [jax.ShapeDtypeStruct((count, length, heads * rank), BF16)] * 2,
-        "in_side_streamed",
-        micros=micros,
-        mebibytes=20,
-        prefetch=[layer],
-        after=after,
-        in_specs=[IN_HBM, WHOLE],
+def layer_in_kernel(layer_ref, acts_ref, proj_ref, out_ref):
+    layer = layer_ref[0]
+    for seq in range(out_ref.shape[0]):
+        in_side_of(acts_ref.at[layer, seq], proj_ref.at[layer], out_ref, (seq,))
+
+
+def in_side_of_layer(layer, acts, in_proj, micros, after=()):
+    _, count, length, _ = acts.shape
+    _, heads, rank, _ = in_proj.shape
+    return call(
+        layer_in_kernel,
+        [acts, in_proj],
+        jax.ShapeDtypeStruct((count, length, heads * rank), BF16),
+        "in_side_of_layer",
+        micros=micros,
+        prefetch=[layer],
+        after=after,
+    )
+
+
+def stage_kernel(acts_hbm, out_ref, tick_ref, sems):
+    layers, count = out_ref.shape[:2]
+    copies = [
+        pltpu.make_async_copy(
+            acts_hbm.at[layer, seq], out_ref.at[layer, seq], sems.at[layer * count + seq]
+        )
+        for layer in range(layers)
+        for seq in range(count)
+    ]
+    for copy in copies:
+        copy.start()
+    tick_ref[...] = jnp.zeros_like(tick_ref)
+    for copy in copies:
+        copy.wait()
+
+
+def staged(acts, after):
+    return call(
+        stage_kernel,
+        [in_hbm(acts)],
+        [jax.ShapeDtypeStruct(acts.shape, BF16), jax.ShapeDtypeStruct((8, 128), F32)],
+        "staged",
+        micros=0.1,
+        after=after,
+        in_specs=[IN_HBM],
         out_specs=[WHOLE] * 2,
-        scratch=[
-            pltpu.VMEM(acts.shape, BF16),
-            pltpu.SemaphoreType.DMA((layers * count,)),
-        ],
+        scratch=[pltpu.SemaphoreType.DMA((acts.shape[0] * acts.shape[1],))],
     )
 
 
@@ -405,6 +411,61 @@
     )
 
 
+def lever_kernel(layers, queries_n, layer_ref, *refs):
+    query_refs, (in_ref, out_ref) = refs[:queries_n], refs[queries_n:]
+    rows = []
+    for layer_refs in zip(*[iter(query_refs)] * layers):
+        for idx in range(layer_refs[0].shape[0]):
+            query = layer_refs[0][idx]
+            for layer in range(1, layers):
+                query = jnp.where(layer_ref[0] == layer, layer_refs[layer][idx], query)
+            rows.append(query.astype(BF16))
+    stacked = jnp.concatenate(rows, axis=0)
+    for seq in range(in_ref.shape[0]):
+        out_ref[seq] = lax.dot_general(stacked, in_ref[seq], NT, preferred_element_type=F32)
+
+
+def query_levers(layer, queries, in_sides):
+    flat = [array for query in queries for array in query]
+    rows = sum(query[0].shape[0] * query[0].shape[1] for query in queries)
+    count, length, _ = in_sides.shape
+    return call(
+        functools.partial(lever_kernel, len(queries[0]), len(flat)),
+        [*flat, in_sides],
+        jax.ShapeDtypeStruct((count, rows, length), F32),
+        "query_levers",
+        micros=1.5,
+        prefetch=[layer],
+    )
+
+
+def lever_score_kernel(norm, flip_ref, lever_ref, side_ref, scale_ref, before_ref, out_ref):
+    rows, lanes = out_ref.shape
+    rank = side_ref.shape[1]
+    row_at = lax.broadcasted_iota(jnp.int32, (rows, lanes), 0)
+    lane_at = lax.broadcasted_iota(jnp.int32, (rows, lanes), 1)
+    total = before_ref[...]
+    for seq in range(side_ref.shape[0]):
+        weighted = (side_ref[seq] * scale_ref[seq : seq + 1, :]).astype(BF16).astype(F32)
+        for row in range(rows):
+            product = lever_ref[seq, rank * row : rank * (row + 1), :] * weighted
+            value = jnp.sum(jnp.sum(product, axis=0, keepdims=True), axis=1, keepdims=True)
+            here = (row_at == (row ^ flip_ref[0])) & (lane_at == seq)
+            total = total + jnp.where(here, value * norm, 0.0)
+    out_ref[...] = total
+
+
+def lever_scores(flip, norm, levers, side, scale, before):
+    return call(
+        functools.partial(lever_score_kernel, norm / math.sqrt(side.shape[2])),
+        [levers, side, scale, before],
+        jax.ShapeDtypeStruct(before.shape, F32),
+        "lever_scores",
+        micros=0.5,
+        prefetch=[flip],
+    )
+
+
 def local(
     train_grads,
     train_acts,
@@ -458,21 +519,21 @@
         )
         across = [far(one, "dp") for one in ready]
         train_scale = token_scale(train_ids, token_weight, 0.1, ready[-1:])
-        owns = [pair + far(pair) for pair in pairs]
+        acts, tick = staged(train_acts, [train_scale])
+        owns = [pair + hold(far(pair), [tick]) for pair in pairs]
         others = [near(own) for own in owns]
-        across = [hold(one, owns[-1:]) for one in across]
+        in_other = in_side_of_layer(other, acts, in_proj, 2.5, owns)
+        across = [hold(across[0], [owns[0]]), hold(across[1], [owns[0]])]
+        in_own = in_side_of_layer(mine, acts, in_proj, 6.0, [in_other])
         every = [
             ready,
             [near(one, "dp") for one in ready],
             across,
             [near(one, "dp") for one in across],
         ]
-        in_own, in_other = in_side_streamed(mine, train_acts, in_proj, 5.0, owns)
         terms = score_terms(mine, flip, norm, every, owns, train_scale, in_own)
-        for (first, _), part in zip(parts, others):
-            terms = score_terms(
-                other, flip, norm, every, [part], train_scale, in_other, [terms], first
-            )
+        levers = query_levers(other, every, in_other)
+        terms = lever_scores(flip, norm, levers, others[0], train_scale, terms)
         total = terms
         for shift in range(1, 4):
             total = total + lax.ppermute(

time: 49.3 us -> 46.9 us (0.951)
  waiting for transfers between devices: 12.9 us -> 8.11 us
  starting transfers between devices: 18.5 us -> 20.3 us
  Pallas kernels: 16.6 us -> 17.3 us
    ppermute x4, waiting for transfers between devices: 8.79 us -> 2.92 us  [far(): return lax.ppermute(array, axis, FAR)]
    ppermute x8, starting transfers between devices: 9.15 us -> 10.9 us  [near(): return lax.ppermute(array, axis, NEAR)]
    ppermute x8, waiting for transfers between devices: 2.45 us -> 3.48 us  [near(): return lax.ppermute(array, axis, NEAR)]
    pallas_call x10 -> x13, Pallas kernels: 16.6 us -> 17.3 us  [call(): pl.pallas_call(body, out_shape=out_shape, grid_spec=pltpu.PrefetchScalarG...]
  transfers between devices with their start and end apart: 15 -> 15, of which waited for: 6 -> 7; matrix products, arithmetic and copies ran while one was open for 0% -> 0% of each run, Pallas kernels for 27% -> 33%
where the time goes in v4:
time: 46.9 us; the launch traced here: 46.7 us
  starting transfers between devices  20.3 us (43%)
  Pallas kernels  17.3 us (37%)
  waiting for transfers between devices  8.11 us (17%)
  other arithmetic  0.74 us (2%)
    pallas_call x13, Pallas kernels, call(): pl.pallas_call(body, out_shape=out_shape, grid_spec=pltpu.PrefetchScalarG...  17.3 us
    ppermute x8, starting transfers between devices, near(): return lax.ppermute(array, axis, NEAR)  10.9 us
    ppermute x4, starting transfers between devices, far(): return lax.ppermute(array, axis, FAR)  4.79 us
    ppermute x3, starting transfers between devices, local(): lax.ppermute(terms, 'head', [(idx, (idx + shift) % 4) for idx in range(4)])  4.56 us
    ppermute x8, waiting for transfers between devices, near(): return lax.ppermute(array, axis, NEAR)  3.48 us
    ppermute x4, waiting for transfers between devices, far(): return lax.ppermute(array, axis, FAR)  2.92 us
    ppermute x3, waiting for transfers between devices, local(): lax.ppermute(terms, 'head', [(idx, (idx + shift) % 4) for idx in range(4)])  1.72 us
  transfers between devices with their start and end apart: 15, of which 7 were waited for; matrix products, arithmetic and copies ran while one was open for 0% of the time, Pallas kernels for 33%

profile of v4, /device:TPU:0, one launch (start us, length us, event | category | flops | bytes accessed | tf_op | source)
XLA Modules:
  0.0 46.7 jit_solution(3476148579580880837)
XLA Ops:
  0.0 0.0 copy-start
  0.0 0.0 copy-start.1
  0.0 1.9 %first_partial.1.refs_3_ = f32[1,64,256]{2,1,0:T(8,128)S(1)} custom-call(s32[1]{0:T(128)S(6)} %sub.3.refs_0_, bf16[2,1,256,2048]{3,2,1,0:T(8,128)(2,1)} %refs_1_.6, bf16[2,64,2048]{2,1,0:T(8,128)(2,1)} %refs_6_.2), custom_call_target="tpu_custom_call" | custom-call | flops 8800000000 | tf_op jit(solution)/shard_map/first_partial/pallas_call | solution.py:31
  2.0 0.0 copy-start.2
  2.0 3.1 %collective-permute-start = (f32[1,64,256]{2,1,0:T(8,128)S(1)}, f32[1,64,256]{2,1,0:T(8,128)S(1)}, u32[]{:S(2)}, u32[]{:S(2)}) collective-permute-start(f32[1,64,256]{2,1,0:T(8,128)S(1)} %first_partial.1.refs_3_), channel_id=1, source_target_pairs={{0,1},{1,0},{2,3},{3,2},{4,5},{5,4},{6,7},{7,6},{8,9},{9,8},{10,11... | collective-permute-start | bytes 196616 | tf_op jit(solution)/shard_map/ppermute | solution.py:493
  5.1 0.0 copy-done
  5.1 0.0 copy-done.1
  5.1 1.3 %sides_partial.2.refs_3_ = f32[4,64,256]{2,1,0:T(8,128)S(1)} custom-call(s32[1]{0:T(128)S(6)} %sub.3.refs_0_, bf16[2,4,256,2048]{3,2,1,0:T(8,128)(2,1)S(1)} %copy-done, bf16[2,64,2048]{2,1,0:T(8,128)(2,1)S(1)} %copy-done.1, f32[1,64,256]{2,1,0:T(8,128)S(1)} %first_partial.1.refs_3_), custom_call_target="tpu_custom_call" | custom-call | flops 2200000000 | tf_op jit(solution)/shard_map/sides_partial/pallas_call | solution.py:31
  6.4 0.0 copy-start.4
  6.4 0.0 copy-start.5
  6.4 0.0 copy-start.8
  6.4 0.0 copy-start.9
  6.4 1.8 %collective-permute-start.3 = (f32[4,64,256]{2,1,0:T(8,128)S(1)}, f32[4,64,256]{2,1,0:T(8,128)S(1)}, u32[]{:S(2)}, u32[]{:S(2)}) collective-permute-start(f32[4,64,256]{2,1,0:T(8,128)S(1)} %sides_partial.2.refs_3_), channel_id=1, source_target_pairs={{0,1},{1,0},{2,3},{3,2},{4,5},{5,4},{6,7},{7,6},{8,9},{9,8},{10,11... | collective-permute-start | bytes 786440 | tf_op jit(solution)/shard_map/ppermute | solution.py:493
  8.3 0.0 copy-done.2
  8.3 0.5 sides_partial.3
  8.7 0.0 collective-permute-done
  8.8 2.7 %collective-permute-start.1 = (f32[1,64,256]{2,1,0:T(8,128)S(1)}, f32[1,64,256]{2,1,0:T(8,128)S(1)}, u32[]{:S(2)}, u32[]{:S(2)}) collective-permute-start(f32[1,64,256]{2,1,0:T(8,128)S(1)} %add.23.refs_7_.refs_0_), channel_id=1, source_target_pairs={{0,2},{2,0},{1,3},{3,1},{4,6},{6,4},{5,7},{7,5},{8,10},{10,8},{9,1... | collective-permute-start | bytes 196616 | tf_op jit(solution)/shard_map/ppermute | solution.py:496
  11.4 0.0 copy-done.4
  11.4 0.0 copy-done.5
  11.4 0.0 copy-done.8
  11.4 0.0 copy-done.9
  11.4 0.0 copy-start.3
  11.4 0.0 copy-start.6
  11.4 2.1 %query_in_and_side.1 = (bf16[2,1,256,1024]{3,2,1,0:T(8,128)(2,1)S(1)}, f32[1,256]{1,0:T(1,128)S(1)}, f32[4,64,256]{2,1,0:T(8,128)S(1)}) custom-call(s32[1]{0:T(128)} %bitcast.1.refs_0_, s32[1,256]{1,0:T(1,128)S(1)} %copy-done.9, bf16[2,1,256,2048]{3,2,1,0:T(8,128)(2,1)S(1)} %copy-done.8, bf16[2,16,64,128]{3,2,1,0:T(8,128)(2,1)S(1)} %copy-done.4, ...), custom_call_target="tpu_custom_call" | custom-call | flops 3300000000 | tf_op jit(solution)/shard_map/query_in_and_side/pallas_call | solution.py:31
  13.6 0.0 copy-start.7
  13.6 1.7 %collective-permute-done.1.refs_1_ = f32[1,64,256]{2,1,0:T(8,128)S(1)} collective-permute-done((f32[1,64,256]{2,1,0:T(8,128)S(1)}, f32[1,64,256]{2,1,0:T(8,128)S(1)}, u32[]{:S(2)}, u32[]{:S(2)}) %collective-permute-start.1) | collective-permute-done | bytes 65568 | tf_op jit(solution)/shard_map/ppermute | solution.py:496
  15.2 3.6 %collective-permute-start.2 = (f32[1,64,256]{2,1,0:T(8,128)S(1)}, f32[1,64,256]{2,1,0:T(8,128)S(1)}, u32[]{:S(2)}, u32[]{:S(2)}) collective-permute-start(f32[1,64,256]{2,1,0:T(8,128)S(1)} %settle.1.refs_1_), channel_id=1, source_target_pairs={{0,1},{1,0},{2,3},{3,2},{4,5},{5,4},{6,7},{7,6},{8,9},{9,8},{10,11... | collective-permute-start | bytes 196616 | tf_op jit(solution)/shard_map/ppermute | solution.py:493
  18.8 0.0 collective-permute-done.3
  18.8 0.1 collective-permute-start.7
  18.9 2.4 %collective-permute-done.2.refs_2_ = f32[1,64,256]{2,1,0:T(8,128)S(1)} collective-permute-done((f32[1,64,256]{2,1,0:T(8,128)S(1)}, f32[1,64,256]{2,1,0:T(8,128)S(1)}, u32[]{:S(2)}, u32[]{:S(2)}) %collective-permute-start.2) | collective-permute-done | bytes 65568 | tf_op jit(solution)/shard_map/ppermute | solution.py:493
  21.4 0.0 copy-done.3
  21.4 0.0 copy-done.6
  21.4 1.8 %query_ready.1 = (f32[1,64,1024]{2,1,0:T(8,128)S(1)}, f32[1,64,1024]{2,1,0:T(8,128)S(1)}) custom-call(s32[1]{0:T(128)} %bitcast.1.refs_0_, f32[1,64,256]{2,1,0:T(8,128)S(1)} %settle.1.refs_1_, f32[1,64,256]{2,1,0:T(8,128)S(1)} %collective-permute-done.2.refs_2_, f32[1,256]{1,0:T(1,128)S(1)} %get-tuple-element.12.refs_2_.refs_3_, ...), custom_call_target="tpu_custom_call" | custom-call | flops 110000000 | tf_op jit(solution)/shard_map/query_ready/pallas_call | solution.py:31
  23.2 1.5 %collective-permute-start.8 = (f32[1,64,1024]{2,1,0:T(8,128)S(1)}, f32[1,64,1024]{2,1,0:T(8,128)S(1)}, u32[]{:S(2)}, u32[]{:S(2)}) collective-permute-start(f32[1,64,1024]{2,1,0:T(8,128)S(1)} %get-tuple-element.16.refs_2_), channel_id=1, source_target_pairs={{0,8},{8,0},{4,12},{12,4},{1,9},{9,1},{5,13},{13,5},{2,10},{10,2},... | collective-permute-start | bytes 786440 | tf_op jit(solution)/shard_map/ppermute | solution.py:496
  24.7 0.1 pad_add_fusion.refs_0_
  24.8 0.5 %collective-permute-start.6 = (f32[1,64,1024]{2,1,0:T(8,128)S(1)}, f32[1,64,1024]{2,1,0:T(8,128)S(1)}, u32[]{:S(2)}, u32[]{:S(2)}) collective-permute-start(f32[1,64,1024]{2,1,0:T(8,128)S(1)} %get-tuple-element.15.refs_1_), channel_id=1, source_target_pairs={{0,8},{8,0},{4,12},{12,4},{1,9},{9,1},{5,13},{13,5},{2,10},{10,2},... | collective-permute-start | bytes 786440 | tf_op jit(solution)/shard_map/ppermute | solution.py:496
  25.3 0.0 collective-permute-start.4
  25.3 0.5 %collective-permute-start.5 = (f32[1,64,1024]{2,1,0:T(8,128)S(1)}, f32[1,64,1024]{2,1,0:T(8,128)S(1)}, u32[]{:S(2)}, u32[]{:S(2)}) collective-permute-start(f32[1,64,1024]{2,1,0:T(8,128)S(1)} %get-tuple-element.16.refs_2_), channel_id=1, source_target_pairs={{0,4},{4,0},{8,12},{12,8},{1,5},{5,1},{9,13},{13,9},{2,6},{6,2},{1... | collective-permute-start | bytes 786440 | tf_op jit(solution)/shard_map/ppermute | solution.py:493
  25.8 0.0 copy-done.7
  25.8 1.3 %token_scale.1.refs_1_.refs_10_.refs_3_ = f32[4,256]{1,0:T(4,128)S(1)} custom-call(s32[4,256]{1,0:T(4,128)S(1)} %copy-done.7, f32[1002,128]{1,0:T(8,128)S(1)} %bitcast.5, f32[1,64,1024]{2,1,0:T(8,128)S(1)} %get-tuple-element.16.refs_2_), custom_call_target="tpu_custom_call" | custom-call | flops 110000000 | tf_op jit(solution)/shard_map/token_scale/pallas_call | solution.py:31
  27.1 3.5 %staged.1 = (bf16[2,4,256,2048]{3,2,1,0:T(8,128)(2,1)S(1)}, f32[8,128]{1,0:T(8,128)S(1)}) custom-call(bf16[2,4,256,2048]{3,2,1,0:T(8,128)(2,1)} %refs_0_.3, f32[4,256]{1,0:T(4,128)S(1)} %token_scale.1.refs_1_.refs_10_.refs_3_), custom_call_target="tpu_custom_call" | custom-call | flops 110000000 | tf_op jit(solution)/shard_map/staged/pallas_call | solution.py:31
  30.6 1.2 %collective-permute-done.7.refs_0_ = f32[4,64,256]{2,1,0:T(8,128)S(1)} collective-permute-done((f32[4,64,256]{2,1,0:T(8,128)S(1)}, f32[4,64,256]{2,1,0:T(8,128)S(1)}, u32[]{:S(2)}, u32[]{:S(2)}) %collective-permute-start.7) | collective-permute-done | bytes 262176 | tf_op jit(solution)/shard_map/ppermute | solution.py:496
  31.8 1.4 %collective-permute-start.11 = (f32[4,64,256]{2,1,0:T(8,128)S(1)}, f32[4,64,256]{2,1,0:T(8,128)S(1)}, u32[]{:S(2)}, u32[]{:S(2)}) collective-permute-start(f32[4,64,256]{2,1,0:T(8,128)S(1)} %add.25.refs_1_.refs_3_.refs_9_), channel_id=1, source_target_pairs={{0,1},{1,0},{2,3},{3,2},{4,5},{5,4},{6,7},{7,6},{8,9},{9,8},{10,11... | collective-permute-start | bytes 786440 | tf_op jit(solution)/shard_map/ppermute | solution.py:493
  33.2 0.0 collective-permute-done.8.refs_0_
  33.2 0.0 collective-permute-start.10
  33.2 1.3 %in_side_of_layer.2.refs_9_.refs_3_ = bf16[4,256,1024]{2,1,0:T(8,128)(2,1)S(1)} custom-call(s32[1]{0:T(128)S(6)} %sub.3.refs_0_, bf16[2,4,256,2048]{3,2,1,0:T(8,128)(2,1)S(1)} %get-tuple-element.18.refs_1_, bf16[2,16,64,128]{3,2,1,0:T(8,128)(2,1)S(1)} %copy-done.4, f32[4,64,256]{2,1,0:T(8,128)S(1)} %add.25.refs_1_.refs_3_.refs_9_), custom_call_target="tpu_custom_call" | custom-call | flops 2750000128 | tf_op jit(solution)/shard_map/in_side_of_layer/pallas_call | solution.py:31
  34.5 0.1 collective-permute-done.6.refs_0_
  34.5 0.5 %collective-permute-start.9 = (f32[1,64,1024]{2,1,0:T(8,128)S(1)}, f32[1,64,1024]{2,1,0:T(8,128)S(1)}, u32[]{:S(2)}, u32[]{:S(2)}) collective-permute-start(f32[1,64,1024]{2,1,0:T(8,128)S(1)} %hold.4.refs_5_), channel_id=1, source_target_pairs={{0,4},{4,0},{8,12},{12,8},{1,5},{5,1},{9,13},{13,9},{2,6},{6,2},{1... | collective-permute-start | bytes 786440 | tf_op jit(solution)/shard_map/ppermute | solution.py:493
  35.1 1.3 %in_side_of_layer.3.refs_11_ = bf16[4,256,1024]{2,1,0:T(8,128)(2,1)S(1)} custom-call(s32[1]{0:T(128)} %bitcast.1.refs_0_, bf16[2,4,256,2048]{3,2,1,0:T(8,128)(2,1)S(1)} %get-tuple-element.18.refs_1_, bf16[2,16,64,128]{3,2,1,0:T(8,128)(2,1)S(1)} %copy-done.4, bf16[4,256,1024]{2,1,0:T(8,128)(2,1)S(1)} %in_side_of_layer.2.refs_9_.refs_3_), custom_call_target="tpu_custom_call" | custom-call | flops 6600000000 | tf_op jit(solution)/shard_map/in_side_of_layer/pallas_call | solution.py:31
  36.3 0.0 collective-permute-done.4.refs_3_
  36.3 0.0 collective-permute-done.5.refs_4_
  36.3 0.0 collective-permute-done.10.refs_8_
  36.4 0.0 collective-permute-done.9.refs_7_
  36.4 0.8 %query_levers.1.refs_1_ = f32[4,256,256]{2,1,0:T(8,128)S(1)} custom-call(s32[1]{0:T(128)S(6)} %sub.3.refs_0_, f32[1,64,1024]{2,1,0:T(8,128)S(1)} %get-tuple-element.15.refs_1_, f32[1,64,1024]{2,1,0:T(8,128)S(1)} %get-tuple-element.16.refs_2_, f32[1,64,1024]{2,1,0:T(8,128)S(1)} %collective-permute-done.4.refs_3_, ...), custom_call_target="tpu_custom_call" | custom-call | flops 1650000000 | tf_op jit(solution)/shard_map/query_levers/pallas_call | solution.py:31
  37.2 1.5 %score_terms.1.refs_4_ = f32[4,128]{1,0:T(4,128)S(1)} custom-call(s32[2]{0:T(128)S(1)} %pad_add_fusion.refs_0_, f32[1,64,1024]{2,1,0:T(8,128)S(1)} %get-tuple-element.15.refs_1_, f32[1,64,1024]{2,1,0:T(8,128)S(1)} %get-tuple-element.16.refs_2_, f32[1,64,1024]{2,1,0:T(8,128)S(1)} %collective-permute-done.4.refs_3_, ...), custom_call_target="tpu_custom_call" | custom-call | flops 1650000000 | tf_op jit(solution)/shard_map/score_terms/pallas_call | solution.py:31
  38.6 1.0 %collective-permute-done.11.refs_2_ = f32[4,64,256]{2,1,0:T(8,128)S(1)} collective-permute-done((f32[4,64,256]{2,1,0:T(8,128)S(1)}, f32[4,64,256]{2,1,0:T(8,128)S(1)}, u32[]{:S(2)}, u32[]{:S(2)}) %collective-permute-start.11) | collective-permute-done | bytes 262176 | tf_op jit(solution)/shard_map/ppermute | solution.py:493
  39.7 0.2 lever_scores.1
  39.9 1.8 %collective-permute-start.12 = (f32[4,128]{1,0:T(4,128)S(1)}, f32[4,128]{1,0:T(4,128)S(1)}, u32[]{:S(2)}, u32[]{:S(2)}) collective-permute-start(f32[4,128]{1,0:T(4,128)S(1)} %lever_scores.1), channel_id=1, source_target_pairs={{0,1},{1,2},{2,3},{3,0},{4,5},{5,6},{6,7},{7,4},{8,9},{9,10},{10,1... | collective-permute-start | bytes 6152 | tf_op jit(solution)/shard_map/ppermute | solution.py:539
  41.6 0.5 %collective-permute-start.13 = (f32[4,128]{1,0:T(4,128)S(1)}, f32[4,128]{1,0:T(4,128)S(1)}, u32[]{:S(2)}, u32[]{:S(2)}) collective-permute-start(f32[4,128]{1,0:T(4,128)S(1)} %lever_scores.1), channel_id=1, source_target_pairs={{0,2},{1,3},{2,0},{3,1},{4,6},{5,7},{6,4},{7,5},{8,10},{9,11},{10,... | collective-permute-start | bytes 6152 | tf_op jit(solution)/shard_map/ppermute | solution.py:539
  42.2 2.3 %collective-permute-start.14 = (f32[4,128]{1,0:T(4,128)S(1)}, f32[4,128]{1,0:T(4,128)S(1)}, u32[]{:S(2)}, u32[]{:S(2)}) collective-permute-start(f32[4,128]{1,0:T(4,128)S(1)} %lever_scores.1), channel_id=1, source_target_pairs={{0,3},{1,0},{2,1},{3,2},{4,7},{5,4},{6,5},{7,6},{8,11},{9,8},{10,9... | collective-permute-start | bytes 6152 | tf_op jit(solution)/shard_map/ppermute | solution.py:539
  44.4 0.9 %collective-permute-done.12 = f32[4,128]{1,0:T(4,128)S(1)} collective-permute-done((f32[4,128]{1,0:T(4,128)S(1)}, f32[4,128]{1,0:T(4,128)S(1)}, u32[]{:S(2)}, u32[]{:S(2)}) %collective-permute-start.12) | collective-permute-done | bytes 2080 | tf_op jit(solution)/shard_map/ppermute | solution.py:539
  45.3 0.8 %collective-permute-done.13 = f32[4,128]{1,0:T(4,128)S(1)} collective-permute-done((f32[4,128]{1,0:T(4,128)S(1)}, f32[4,128]{1,0:T(4,128)S(1)}, u32[]{:S(2)}, u32[]{:S(2)}) %collective-permute-start.13) | collective-permute-done | bytes 2080 | tf_op jit(solution)/shard_map/ppermute | solution.py:539
  46.1 0.0 collective-permute-done.14
  46.1 0.6 %add_add_fusion = f32[4,128]{1,0:T(4,128)} fusion(f32[4,128]{1,0:T(4,128)S(1)} %collective-permute-done.14, f32[4,128]{1,0:T(4,128)S(1)} %collective-permute-done.13, f32[4,128]{1,0:T(4,128)S(1)} %lever_scores.1, f32[4,128]{1,0:T(4,128)S(1)} %collective-permute-done.12), kind=kLoop, calls=%fused_computation | loop fusion | flops 1536 | bytes 10240 | tf_op jit(solution)/shard_map/add | solution.py:539
  (7 shorter events, 0.1 us)
Async XLA Ops:
  0.0 5.1 %copy-start = (bf16[2,4,256,2048]{3,2,1,0:T(8,128)(2,1)S(1)}, bf16[2,4,256,2048]{3,2,1,0:T(8,128)(2,1)}, u32[]{:S(2)}) copy-start(bf16[2,4,256,2048]{3,2,1,0:T(8,128)(2,1)} %refs_5_.2) | copy-start | bytes 25165828
  0.0 5.1 %copy-start.1 = (bf16[2,64,2048]{2,1,0:T(8,128)(2,1)S(1)}, bf16[2,64,2048]{2,1,0:T(8,128)(2,1)}, u32[]{:S(2)}) copy-start(bf16[2,64,2048]{2,1,0:T(8,128)(2,1)} %refs_6_.2) | copy-start | bytes 1572868
  2.0 6.3 %copy-start.2 = (bf16[2,1,256,2048]{3,2,1,0:T(8,128)(2,1)S(1)}, bf16[2,1,256,2048]{3,2,1,0:T(8,128)(2,1)}, u32[]{:S(2)}) copy-start(bf16[2,1,256,2048]{3,2,1,0:T(8,128)(2,1)} %refs_1_.6) | copy-start | bytes 6291460
  2.0 6.8 %collective-permute-start = (f32[1,64,256]{2,1,0:T(8,128)S(1)}, f32[1,64,256]{2,1,0:T(8,128)S(1)}, u32[]{:S(2)}, u32[]{:S(2)}) collective-permute-start(f32[1,64,256]{2,1,0:T(8,128)S(1)} %first_partial.1.refs_3_), channel_id=1, source_target_pairs={{0,1},{1,0},{2,3},{3,2},{4,5},{5,4},{6,7},{7,6},{8,9},{9,8},{10,11... | collective-permute-start | bytes 196616 | tf_op jit(solution)/shard_map/ppermute | solution.py:493
  6.4 5.0 %copy-start.4 = (bf16[2,16,64,128]{3,2,1,0:T(8,128)(2,1)S(1)}, bf16[2,16,64,128]{3,2,1,0:T(8,128)(2,1)}, u32[]{:S(2)}) copy-start(bf16[2,16,64,128]{3,2,1,0:T(8,128)(2,1)} %refs_2_.11) | copy-start | bytes 1572868
  6.4 5.0 %copy-start.5 = (f32[128256]{0:T(1024)S(1)}, f32[128256]{0:T(1024)}, u32[]{:S(2)}) copy-start(f32[128256]{0:T(1024)} %param.17) | copy-start | bytes 1539076
  6.4 5.0 %copy-start.8 = (bf16[2,1,256,2048]{3,2,1,0:T(8,128)(2,1)S(1)}, bf16[2,1,256,2048]{3,2,1,0:T(8,128)(2,1)}, u32[]{:S(2)}) copy-start(bf16[2,1,256,2048]{3,2,1,0:T(8,128)(2,1)} %refs_2_.9) | copy-start | bytes 6291460
  6.4 5.0 %copy-start.9 = (s32[1,256]{1,0:T(1,128)S(1)}, s32[1,256]{1,0:T(1,128)}, u32[]{:S(2)}) copy-start(s32[1,256]{1,0:T(1,128)} %refs_1_.7) | copy-start | bytes 3076
  6.4 12.4 %collective-permute-start.3 = (f32[4,64,256]{2,1,0:T(8,128)S(1)}, f32[4,64,256]{2,1,0:T(8,128)S(1)}, u32[]{:S(2)}, u32[]{:S(2)}) collective-permute-start(f32[4,64,256]{2,1,0:T(8,128)S(1)} %sides_partial.2.refs_3_), channel_id=1, source_target_pairs={{0,1},{1,0},{2,3},{3,2},{4,5},{5,4},{6,7},{7,6},{8,9},{9,8},{10,11... | collective-permute-start | bytes 786440 | tf_op jit(solution)/shard_map/ppermute | solution.py:493
  8.8 6.5 %collective-permute-start.1 = (f32[1,64,256]{2,1,0:T(8,128)S(1)}, f32[1,64,256]{2,1,0:T(8,128)S(1)}, u32[]{:S(2)}, u32[]{:S(2)}) collective-permute-start(f32[1,64,256]{2,1,0:T(8,128)S(1)} %add.23.refs_7_.refs_0_), channel_id=1, source_target_pairs={{0,2},{2,0},{1,3},{3,1},{4,6},{6,4},{5,7},{7,5},{8,10},{10,8},{9,1... | collective-permute-start | bytes 196616 | tf_op jit(solution)/shard_map/ppermute | solution.py:496
  11.4 9.9 %copy-start.3 = (f32[2,16,64,64]{3,2,1,0:T(8,128)S(1)}, f32[2,16,64,64]{3,2,1,0:T(8,128)}, u32[]{:S(2)}) copy-start(f32[2,16,64,64]{3,2,1,0:T(8,128)} %refs_6_.3) | copy-start | bytes 1572868
  11.4 9.9 %copy-start.6 = (f32[2,64,64]{2,1,0:T(8,128)S(1)}, f32[2,64,64]{2,1,0:T(8,128)}, u32[]{:S(2)}) copy-start(f32[2,64,64]{2,1,0:T(8,128)} %refs_5_.3) | copy-start | bytes 98308
  13.6 12.3 %copy-start.7 = (s32[4,256]{1,0:T(4,128)S(1)}, s32[4,256]{1,0:T(4,128)}, u32[]{:S(2)}) copy-start(s32[4,256]{1,0:T(4,128)} %refs_0_.2) | copy-start | bytes 12292
  15.2 6.1 %collective-permute-start.2 = (f32[1,64,256]{2,1,0:T(8,128)S(1)}, f32[1,64,256]{2,1,0:T(8,128)S(1)}, u32[]{:S(2)}, u32[]{:S(2)}) collective-permute-start(f32[1,64,256]{2,1,0:T(8,128)S(1)} %settle.1.refs_1_), channel_id=1, source_target_pairs={{0,1},{1,0},{2,3},{3,2},{4,5},{5,4},{6,7},{7,6},{8,9},{9,8},{10,11... | collective-permute-start | bytes 196616 | tf_op jit(solution)/shard_map/ppermute | solution.py:493
  18.8 12.9 %collective-permute-start.7 = (f32[4,64,256]{2,1,0:T(8,128)S(1)}, f32[4,64,256]{2,1,0:T(8,128)S(1)}, u32[]{:S(2)}, u32[]{:S(2)}) collective-permute-start(f32[4,64,256]{2,1,0:T(8,128)S(1)} %add.24.refs_7_), channel_id=1, source_target_pairs={{0,2},{2,0},{1,3},{3,1},{4,6},{6,4},{5,7},{7,5},{8,10},{10,8},{9,1... | collective-permute-start | bytes 786440 | tf_op jit(solution)/shard_map/ppermute | solution.py:496
  23.2 10.0 %collective-permute-start.8 = (f32[1,64,1024]{2,1,0:T(8,128)S(1)}, f32[1,64,1024]{2,1,0:T(8,128)S(1)}, u32[]{:S(2)}, u32[]{:S(2)}) collective-permute-start(f32[1,64,1024]{2,1,0:T(8,128)S(1)} %get-tuple-element.16.refs_2_), channel_id=1, source_target_pairs={{0,8},{8,0},{4,12},{12,4},{1,9},{9,1},{5,13},{13,5},{2,10},{10,2},... | collective-permute-start | bytes 786440 | tf_op jit(solution)/shard_map/ppermute | solution.py:496
  24.8 9.8 %collective-permute-start.6 = (f32[1,64,1024]{2,1,0:T(8,128)S(1)}, f32[1,64,1024]{2,1,0:T(8,128)S(1)}, u32[]{:S(2)}, u32[]{:S(2)}) collective-permute-start(f32[1,64,1024]{2,1,0:T(8,128)S(1)} %get-tuple-element.15.refs_1_), channel_id=1, source_target_pairs={{0,8},{8,0},{4,12},{12,4},{1,9},{9,1},{5,13},{13,5},{2,10},{10,2},... | collective-permute-start | bytes 786440 | tf_op jit(solution)/shard_map/ppermute | solution.py:496
  25.3 11.0 %collective-permute-start.4 = (f32[1,64,1024]{2,1,0:T(8,128)S(1)}, f32[1,64,1024]{2,1,0:T(8,128)S(1)}, u32[]{:S(2)}, u32[]{:S(2)}) collective-permute-start(f32[1,64,1024]{2,1,0:T(8,128)S(1)} %get-tuple-element.15.refs_1_), channel_id=1, source_target_pairs={{0,4},{4,0},{8,12},{12,8},{1,5},{5,1},{9,13},{13,9},{2,6},{6,2},{1... | collective-permute-start | bytes 786440 | tf_op jit(solution)/shard_map/ppermute | solution.py:493
  25.3 11.0 %collective-permute-start.5 = (f32[1,64,1024]{2,1,0:T(8,128)S(1)}, f32[1,64,1024]{2,1,0:T(8,128)S(1)}, u32[]{:S(2)}, u32[]{:S(2)}) collective-permute-start(f32[1,64,1024]{2,1,0:T(8,128)S(1)} %get-tuple-element.16.refs_2_), channel_id=1, source_target_pairs={{0,4},{4,0},{8,12},{12,8},{1,5},{5,1},{9,13},{13,9},{2,6},{6,2},{1... | collective-permute-start | bytes 786440 | tf_op jit(solution)/shard_map/ppermute | solution.py:493
  31.8 7.8 %collective-permute-start.11 = (f32[4,64,256]{2,1,0:T(8,128)S(1)}, f32[4,64,256]{2,1,0:T(8,128)S(1)}, u32[]{:S(2)}, u32[]{:S(2)}) collective-permute-start(f32[4,64,256]{2,1,0:T(8,128)S(1)} %add.25.refs_1_.refs_3_.refs_9_), channel_id=1, source_target_pairs={{0,1},{1,0},{2,3},{3,2},{4,5},{5,4},{6,7},{7,6},{8,9},{9,8},{10,11... | collective-permute-start | bytes 786440 | tf_op jit(solution)/shard_map/ppermute | solution.py:493
  33.2 3.2 %collective-permute-start.10 = (f32[1,64,1024]{2,1,0:T(8,128)S(1)}, f32[1,64,1024]{2,1,0:T(8,128)S(1)}, u32[]{:S(2)}, u32[]{:S(2)}) collective-permute-start(f32[1,64,1024]{2,1,0:T(8,128)S(1)} %hold.5.refs_6_), channel_id=1, source_target_pairs={{0,4},{4,0},{8,12},{12,8},{1,5},{5,1},{9,13},{13,9},{2,6},{6,2},{1... | collective-permute-start | bytes 786440 | tf_op jit(solution)/shard_map/ppermute | solution.py:493
  34.5 1.8 %collective-permute-start.9 = (f32[1,64,1024]{2,1,0:T(8,128)S(1)}, f32[1,64,1024]{2,1,0:T(8,128)S(1)}, u32[]{:S(2)}, u32[]{:S(2)}) collective-permute-start(f32[1,64,1024]{2,1,0:T(8,128)S(1)} %hold.4.refs_5_), channel_id=1, source_target_pairs={{0,4},{4,0},{8,12},{12,8},{1,5},{5,1},{9,13},{13,9},{2,6},{6,2},{1... | collective-permute-start | bytes 786440 | tf_op jit(solution)/shard_map/ppermute | solution.py:493
  39.9 5.4 %collective-permute-start.12 = (f32[4,128]{1,0:T(4,128)S(1)}, f32[4,128]{1,0:T(4,128)S(1)}, u32[]{:S(2)}, u32[]{:S(2)}) collective-permute-start(f32[4,128]{1,0:T(4,128)S(1)} %lever_scores.1), channel_id=1, source_target_pairs={{0,1},{1,2},{2,3},{3,0},{4,5},{5,6},{6,7},{7,4},{8,9},{9,10},{10,1... | collective-permute-start | bytes 6152 | tf_op jit(solution)/shard_map/ppermute | solution.py:539
  41.6 4.5 %collective-permute-start.13 = (f32[4,128]{1,0:T(4,128)S(1)}, f32[4,128]{1,0:T(4,128)S(1)}, u32[]{:S(2)}, u32[]{:S(2)}) collective-permute-start(f32[4,128]{1,0:T(4,128)S(1)} %lever_scores.1), channel_id=1, source_target_pairs={{0,2},{1,3},{2,0},{3,1},{4,6},{5,7},{6,4},{7,5},{8,10},{9,11},{10,... | collective-permute-start | bytes 6152 | tf_op jit(solution)/shard_map/ppermute | solution.py:539
  42.2 4.0 %collective-permute-start.14 = (f32[4,128]{1,0:T(4,128)S(1)}, f32[4,128]{1,0:T(4,128)S(1)}, u32[]{:S(2)}, u32[]{:S(2)}) collective-permute-start(f32[4,128]{1,0:T(4,128)S(1)} %lever_scores.1), channel_id=1, source_target_pairs={{0,3},{1,0},{2,1},{3,2},{4,7},{5,4},{6,5},{7,6},{8,11},{9,8},{10,9... | collective-permute-start | bytes 6152 | tf_op jit(solution)/shard_map/ppermute | solution.py:539

commit v5 on v4

--- a/solution.py
+++ b/solution.py
@@ -505,7 +505,7 @@
         query_keep = sides_partial(mine, query_grads, out_proj, 0.5, [train_out])
         query_pair = query_keep + query_got
         query_far = far(query_pair)
-        train_got = near(train_out)
+        train_got = near(hold(train_out, [query_pair]))
         query_in, query_scale, train_keep = query_in_and_side(
             mine, query_ids, query_acts, in_proj, token_weight, train_grads, out_proj, 3.0,
             [query_pair],

time: 46.9 us -> 46.1 us (0.983)
  starting transfers between devices: 20.3 us -> 16.5 us
  waiting for transfers between devices: 8.11 us -> 11 us
    ppermute x8, starting transfers between devices: 10.9 us -> 6.56 us  [near(): return lax.ppermute(array, axis, NEAR)]
    ppermute x8, waiting for transfers between devices: 3.48 us -> 5.42 us  [near(): return lax.ppermute(array, axis, NEAR)]
    ppermute x4, starting transfers between devices: 4.79 us -> 6.1 us  [far(): return lax.ppermute(array, axis, FAR)]
    ppermute x3, starting transfers between devices: 4.56 us -> 3.87 us  [local(): lax.ppermute(terms, 'head', [(idx, (idx + shift) % 4) for idx in range(4)])]
    ppermute x3, waiting for transfers between devices: 1.72 us -> 2.21 us  [local(): lax.ppermute(terms, 'head', [(idx, (idx + shift) % 4) for idx in range(4)])]
  transfers between devices with their start and end apart: 15 -> 15, of which waited for: 7 -> 8; matrix products, arithmetic and copies ran while one was open for 0% -> 0% of each run, Pallas kernels for 33% -> 33%
where the time goes in v5:
time: 46.1 us; the launch traced here: 45.9 us
  Pallas kernels  17.4 us (38%)
  starting transfers between devices  16.5 us (36%)
  waiting for transfers between devices  11 us (24%)
  other arithmetic  0.74 us (2%)
    pallas_call x13, Pallas kernels, call(): pl.pallas_call(body, out_shape=out_shape, grid_spec=pltpu.PrefetchScalarG...  17.4 us
    ppermute x8, starting transfers between devices, near(): return lax.ppermute(array, axis, NEAR)  6.56 us
    ppermute x4, starting transfers between devices, far(): return lax.ppermute(array, axis, FAR)  6.1 us
    ppermute x8, waiting for transfers between devices, near(): return lax.ppermute(array, axis, NEAR)  5.42 us
    ppermute x3, starting transfers between devices, local(): lax.ppermute(terms, 'head', [(idx, (idx + shift) % 4) for idx in range(4)])  3.87 us
    ppermute x4, waiting for transfers between devices, far(): return lax.ppermute(array, axis, FAR)  3.38 us
    ppermute x3, waiting for transfers between devices, local(): lax.ppermute(terms, 'head', [(idx, (idx + shift) % 4) for idx in range(4)])  2.21 us
  transfers between devices with their start and end apart: 15, of which 8 were waited for; matrix products, arithmetic and copies ran while one was open for 0% of the time, Pallas kernels for 33%

profile of v5, /device:TPU:0, one launch (start us, length us, event | category | flops | bytes accessed | tf_op | source)
XLA Modules:
  0.0 45.9 jit_solution(17915015595522944393)
XLA Ops:
  0.0 0.0 copy-start
  0.0 0.0 copy-start.1
  0.0 1.9 %first_partial.1.refs_3_ = f32[1,64,256]{2,1,0:T(8,128)S(1)} custom-call(s32[1]{0:T(128)S(6)} %sub.3.refs_0_, bf16[2,1,256,2048]{3,2,1,0:T(8,128)(2,1)} %refs_1_.6, bf16[2,64,2048]{2,1,0:T(8,128)(2,1)} %refs_6_.2), custom_call_target="tpu_custom_call" | custom-call | flops 8800000000 | tf_op jit(solution)/shard_map/first_partial/pallas_call | solution.py:31
  2.0 0.0 copy-start.2
  2.0 3.1 %collective-permute-start = (f32[1,64,256]{2,1,0:T(8,128)S(1)}, f32[1,64,256]{2,1,0:T(8,128)S(1)}, u32[]{:S(2)}, u32[]{:S(2)}) collective-permute-start(f32[1,64,256]{2,1,0:T(8,128)S(1)} %first_partial.1.refs_3_), channel_id=1, source_target_pairs={{0,1},{1,0},{2,3},{3,2},{4,5},{5,4},{6,7},{7,6},{8,9},{9,8},{10,11... | collective-permute-start | bytes 196616 | tf_op jit(solution)/shard_map/ppermute | solution.py:493
  5.1 0.0 copy-done
  5.1 0.0 copy-done.1
  5.1 1.3 %sides_partial.2.refs_3_.refs_0_ = f32[4,64,256]{2,1,0:T(8,128)S(1)} custom-call(s32[1]{0:T(128)S(6)} %sub.3.refs_0_, bf16[2,4,256,2048]{3,2,1,0:T(8,128)(2,1)S(1)} %copy-done, bf16[2,64,2048]{2,1,0:T(8,128)(2,1)S(1)} %copy-done.1, f32[1,64,256]{2,1,0:T(8,128)S(1)} %first_partial.1.refs_3_), custom_call_target="tpu_custom_call" | custom-call | flops 2200000000 | tf_op jit(solution)/shard_map/sides_partial/pallas_call | solution.py:31
  6.4 0.0 copy-done.2
  6.4 0.0 copy-start.4
  6.4 0.0 copy-start.5
  6.4 0.0 copy-start.8
  6.4 0.0 copy-start.9
  6.4 0.5 %sides_partial.3 = f32[1,64,256]{2,1,0:T(8,128)S(1)} custom-call(s32[1]{0:T(128)} %bitcast.1.refs_0_, bf16[2,1,256,2048]{3,2,1,0:T(8,128)(2,1)S(1)} %copy-done.2, bf16[2,64,2048]{2,1,0:T(8,128)(2,1)S(1)} %copy-done.1, f32[4,64,256]{2,1,0:T(8,128)S(1)} %sides_partial.2.refs_3_.refs_0_), custom_call_target="tpu_custom_call" | custom-call | flops 550000000 | tf_op jit(solution)/shard_map/sides_partial/pallas_call | solution.py:31
  6.9 0.4 collective-permute-done
  7.3 3.1 %collective-permute-start.1 = (f32[1,64,256]{2,1,0:T(8,128)S(1)}, f32[1,64,256]{2,1,0:T(8,128)S(1)}, u32[]{:S(2)}, u32[]{:S(2)}) collective-permute-start(f32[1,64,256]{2,1,0:T(8,128)S(1)} %add.23.refs_7_.refs_0_.refs_1_), channel_id=1, source_target_pairs={{0,2},{2,0},{1,3},{3,1},{4,6},{6,4},{5,7},{7,5},{8,10},{10,8},{9,1... | collective-permute-start | bytes 196616 | tf_op jit(solution)/shard_map/ppermute | solution.py:496
  10.4 1.6 %collective-permute-start.3 = (f32[4,64,256]{2,1,0:T(8,128)S(1)}, f32[4,64,256]{2,1,0:T(8,128)S(1)}, u32[]{:S(2)}, u32[]{:S(2)}) collective-permute-start(f32[4,64,256]{2,1,0:T(8,128)S(1)} %hold.4), channel_id=1, source_target_pairs={{0,1},{1,0},{2,3},{3,2},{4,5},{5,4},{6,7},{7,6},{8,9},{9,8},{10,11... | collective-permute-start | bytes 786440 | tf_op jit(solution)/shard_map/ppermute | solution.py:493
  12.0 0.0 copy-done.4
  12.0 0.0 copy-done.5
  12.0 0.0 copy-done.8
  12.0 0.0 copy-done.9
  12.0 0.0 copy-start.3
  12.0 0.0 copy-start.6
  12.0 2.1 %query_in_and_side.1 = (bf16[2,1,256,1024]{3,2,1,0:T(8,128)(2,1)S(1)}, f32[1,256]{1,0:T(1,128)S(1)}, f32[4,64,256]{2,1,0:T(8,128)S(1)}) custom-call(s32[1]{0:T(128)} %bitcast.1.refs_0_, s32[1,256]{1,0:T(1,128)S(1)} %copy-done.9, bf16[2,1,256,2048]{3,2,1,0:T(8,128)(2,1)S(1)} %copy-done.8, bf16[2,16,64,128]{3,2,1,0:T(8,128)(2,1)S(1)} %copy-done.4, ...), custom_call_target="tpu_custom_call" | custom-call | flops 3300000000 | tf_op jit(solution)/shard_map/query_in_and_side/pallas_call | solution.py:31
  14.1 0.0 copy-start.7
  14.2 0.0 collective-permute-done.1.refs_1_
  14.2 1.2 %collective-permute-start.2 = (f32[1,64,256]{2,1,0:T(8,128)S(1)}, f32[1,64,256]{2,1,0:T(8,128)S(1)}, u32[]{:S(2)}, u32[]{:S(2)}) collective-permute-start(f32[1,64,256]{2,1,0:T(8,128)S(1)} %settle.1.refs_1_), channel_id=1, source_target_pairs={{0,1},{1,0},{2,3},{3,2},{4,5},{5,4},{6,7},{7,6},{8,9},{9,8},{10,11... | collective-permute-start | bytes 196616 | tf_op jit(solution)/shard_map/ppermute | solution.py:493
  15.4 3.5 %collective-permute-done.3 = f32[4,64,256]{2,1,0:T(8,128)S(1)} collective-permute-done((f32[4,64,256]{2,1,0:T(8,128)S(1)}, f32[4,64,256]{2,1,0:T(8,128)S(1)}, u32[]{:S(2)}, u32[]{:S(2)}) %collective-permute-start.3) | collective-permute-done | bytes 262176 | tf_op jit(solution)/shard_map/ppermute | solution.py:493
  19.0 0.9 %collective-permute-start.7 = (f32[4,64,256]{2,1,0:T(8,128)S(1)}, f32[4,64,256]{2,1,0:T(8,128)S(1)}, u32[]{:S(2)}, u32[]{:S(2)}) collective-permute-start(f32[4,64,256]{2,1,0:T(8,128)S(1)} %add.24.refs_7_), channel_id=1, source_target_pairs={{0,2},{2,0},{1,3},{3,1},{4,6},{6,4},{5,7},{7,5},{8,10},{10,8},{9,1... | collective-permute-start | bytes 786440 | tf_op jit(solution)/shard_map/ppermute | solution.py:496
  19.9 0.0 collective-permute-done.2.refs_2_
  19.9 0.0 copy-done.3
  19.9 0.0 copy-done.6
  20.0 1.8 %query_ready.1 = (f32[1,64,1024]{2,1,0:T(8,128)S(1)}, f32[1,64,1024]{2,1,0:T(8,128)S(1)}) custom-call(s32[1]{0:T(128)} %bitcast.1.refs_0_, f32[1,64,256]{2,1,0:T(8,128)S(1)} %settle.1.refs_1_, f32[1,64,256]{2,1,0:T(8,128)S(1)} %collective-permute-done.2.refs_2_, f32[1,256]{1,0:T(1,128)S(1)} %get-tuple-element.12.refs_2_.refs_3_, ...), custom_call_target="tpu_custom_call" | custom-call | flops 110000000 | tf_op jit(solution)/shard_map/query_ready/pallas_call | solution.py:31
  21.8 1.5 %collective-permute-start.8 = (f32[1,64,1024]{2,1,0:T(8,128)S(1)}, f32[1,64,1024]{2,1,0:T(8,128)S(1)}, u32[]{:S(2)}, u32[]{:S(2)}) collective-permute-start(f32[1,64,1024]{2,1,0:T(8,128)S(1)} %get-tuple-element.16.refs_2_), channel_id=1, source_target_pairs={{0,8},{8,0},{4,12},{12,4},{1,9},{9,1},{5,13},{13,5},{2,10},{10,2},... | collective-permute-start | bytes 786440 | tf_op jit(solution)/shard_map/ppermute | solution.py:496
  23.3 0.1 pad_add_fusion.refs_0_
  23.4 0.5 %collective-permute-start.6 = (f32[1,64,1024]{2,1,0:T(8,128)S(1)}, f32[1,64,1024]{2,1,0:T(8,128)S(1)}, u32[]{:S(2)}, u32[]{:S(2)}) collective-permute-start(f32[1,64,1024]{2,1,0:T(8,128)S(1)} %get-tuple-element.15.refs_1_), channel_id=1, source_target_pairs={{0,8},{8,0},{4,12},{12,4},{1,9},{9,1},{5,13},{13,5},{2,10},{10,2},... | collective-permute-start | bytes 786440 | tf_op jit(solution)/shard_map/ppermute | solution.py:496
  23.9 0.0 collective-permute-start.4
  23.9 0.5 %collective-permute-start.5 = (f32[1,64,1024]{2,1,0:T(8,128)S(1)}, f32[1,64,1024]{2,1,0:T(8,128)S(1)}, u32[]{:S(2)}, u32[]{:S(2)}) collective-permute-start(f32[1,64,1024]{2,1,0:T(8,128)S(1)} %get-tuple-element.16.refs_2_), channel_id=1, source_target_pairs={{0,4},{4,0},{8,12},{12,8},{1,5},{5,1},{9,13},{13,9},{2,6},{6,2},{1... | collective-permute-start | bytes 786440 | tf_op jit(solution)/shard_map/ppermute | solution.py:493
  24.4 0.0 copy-done.7
  24.4 1.3 %token_scale.1.refs_1_.refs_10_.refs_3_ = f32[4,256]{1,0:T(4,128)S(1)} custom-call(s32[4,256]{1,0:T(4,128)S(1)} %copy-done.7, f32[1002,128]{1,0:T(8,128)S(1)} %bitcast.5, f32[1,64,1024]{2,1,0:T(8,128)S(1)} %get-tuple-element.16.refs_2_), custom_call_target="tpu_custom_call" | custom-call | flops 110000000 | tf_op jit(solution)/shard_map/token_scale/pallas_call | solution.py:31
  25.7 3.5 %staged.1 = (bf16[2,4,256,2048]{3,2,1,0:T(8,128)(2,1)S(1)}, f32[8,128]{1,0:T(8,128)S(1)}) custom-call(bf16[2,4,256,2048]{3,2,1,0:T(8,128)(2,1)} %refs_0_.3, f32[4,256]{1,0:T(4,128)S(1)} %token_scale.1.refs_1_.refs_10_.refs_3_), custom_call_target="tpu_custom_call" | custom-call | flops 110000000 | tf_op jit(solution)/shard_map/staged/pallas_call | solution.py:31
  29.2 2.6 %collective-permute-done.7.refs_0_ = f32[4,64,256]{2,1,0:T(8,128)S(1)} collective-permute-done((f32[4,64,256]{2,1,0:T(8,128)S(1)}, f32[4,64,256]{2,1,0:T(8,128)S(1)}, u32[]{:S(2)}, u32[]{:S(2)}) %collective-permute-start.7) | collective-permute-done | bytes 262176 | tf_op jit(solution)/shard_map/ppermute | solution.py:496
  31.8 0.1 collective-permute-start.11
  31.9 0.0 collective-permute-done.8.refs_0_
  31.9 0.1 collective-permute-start.10
  32.0 1.3 %in_side_of_layer.2.refs_9_.refs_3_ = bf16[4,256,1024]{2,1,0:T(8,128)(2,1)S(1)} custom-call(s32[1]{0:T(128)S(6)} %sub.3.refs_0_, bf16[2,4,256,2048]{3,2,1,0:T(8,128)(2,1)S(1)} %get-tuple-element.18.refs_1_, bf16[2,16,64,128]{3,2,1,0:T(8,128)(2,1)S(1)} %copy-done.4, f32[4,64,256]{2,1,0:T(8,128)S(1)} %add.25.refs_1_.refs_3_.refs_9_), custom_call_target="tpu_custom_call" | custom-call | flops 2750000128 | tf_op jit(solution)/shard_map/in_side_of_layer/pallas_call | solution.py:31
  33.3 0.7 %collective-permute-done.6.refs_0_ = f32[1,64,1024]{2,1,0:T(8,128)S(1)} collective-permute-done((f32[1,64,1024]{2,1,0:T(8,128)S(1)}, f32[1,64,1024]{2,1,0:T(8,128)S(1)}, u32[]{:S(2)}, u32[]{:S(2)}) %collective-permute-start.6) | collective-permute-done | bytes 262176 | tf_op jit(solution)/shard_map/ppermute | solution.py:496
  34.0 0.0 collective-permute-start.9
  34.0 1.3 %in_side_of_layer.3.refs_11_ = bf16[4,256,1024]{2,1,0:T(8,128)(2,1)S(1)} custom-call(s32[1]{0:T(128)} %bitcast.1.refs_0_, bf16[2,4,256,2048]{3,2,1,0:T(8,128)(2,1)S(1)} %get-tuple-element.18.refs_1_, bf16[2,16,64,128]{3,2,1,0:T(8,128)(2,1)S(1)} %copy-done.4, bf16[4,256,1024]{2,1,0:T(8,128)(2,1)S(1)} %in_side_of_layer.2.refs_9_.refs_3_), custom_call_target="tpu_custom_call" | custom-call | flops 6600000000 | tf_op jit(solution)/shard_map/in_side_of_layer/pallas_call | solution.py:31
  35.3 0.0 collective-permute-done.4.refs_3_
  35.3 0.0 collective-permute-done.5.refs_4_
  35.3 0.0 collective-permute-done.10.refs_8_
  35.3 0.2 collective-permute-done.9.refs_7_
  35.6 0.8 %query_levers.1.refs_1_ = f32[4,256,256]{2,1,0:T(8,128)S(1)} custom-call(s32[1]{0:T(128)S(6)} %sub.3.refs_0_, f32[1,64,1024]{2,1,0:T(8,128)S(1)} %get-tuple-element.15.refs_1_, f32[1,64,1024]{2,1,0:T(8,128)S(1)} %get-tuple-element.16.refs_2_, f32[1,64,1024]{2,1,0:T(8,128)S(1)} %collective-permute-done.4.refs_3_, ...), custom_call_target="tpu_custom_call" | custom-call | flops 1650000000 | tf_op jit(solution)/shard_map/query_levers/pallas_call | solution.py:31
  36.4 1.5 %score_terms.1.refs_4_ = f32[4,128]{1,0:T(4,128)S(1)} custom-call(s32[2]{0:T(128)S(1)} %pad_add_fusion.refs_0_, f32[1,64,1024]{2,1,0:T(8,128)S(1)} %get-tuple-element.15.refs_1_, f32[1,64,1024]{2,1,0:T(8,128)S(1)} %get-tuple-element.16.refs_2_, f32[1,64,1024]{2,1,0:T(8,128)S(1)} %collective-permute-done.4.refs_3_, ...), custom_call_target="tpu_custom_call" | custom-call | flops 1650000000 | tf_op jit(solution)/shard_map/score_terms/pallas_call | solution.py:31
  37.8 1.2 %collective-permute-done.11.refs_2_ = f32[4,64,256]{2,1,0:T(8,128)S(1)} collective-permute-done((f32[4,64,256]{2,1,0:T(8,128)S(1)}, f32[4,64,256]{2,1,0:T(8,128)S(1)}, u32[]{:S(2)}, u32[]{:S(2)}) %collective-permute-start.11) | collective-permute-done | bytes 262176 | tf_op jit(solution)/shard_map/ppermute | solution.py:493
  39.1 0.2 lever_scores.1
  39.3 0.9 %collective-permute-start.12 = (f32[4,128]{1,0:T(4,128)S(1)}, f32[4,128]{1,0:T(4,128)S(1)}, u32[]{:S(2)}, u32[]{:S(2)}) collective-permute-start(f32[4,128]{1,0:T(4,128)S(1)} %lever_scores.1), channel_id=1, source_target_pairs={{0,1},{1,2},{2,3},{3,0},{4,5},{5,6},{6,7},{7,4},{8,9},{9,10},{10,1... | collective-permute-start | bytes 6152 | tf_op jit(solution)/shard_map/ppermute | solution.py:539
  40.1 1.6 %collective-permute-start.13 = (f32[4,128]{1,0:T(4,128)S(1)}, f32[4,128]{1,0:T(4,128)S(1)}, u32[]{:S(2)}, u32[]{:S(2)}) collective-permute-start(f32[4,128]{1,0:T(4,128)S(1)} %lever_scores.1), channel_id=1, source_target_pairs={{0,2},{1,3},{2,0},{3,1},{4,6},{5,7},{6,4},{7,5},{8,10},{9,11},{10,... | collective-permute-start | bytes 6152 | tf_op jit(solution)/shard_map/ppermute | solution.py:539
  41.8 1.4 %collective-permute-start.14 = (f32[4,128]{1,0:T(4,128)S(1)}, f32[4,128]{1,0:T(4,128)S(1)}, u32[]{:S(2)}, u32[]{:S(2)}) collective-permute-start(f32[4,128]{1,0:T(4,128)S(1)} %lever_scores.1), channel_id=1, source_target_pairs={{0,3},{1,0},{2,1},{3,2},{4,7},{5,4},{6,5},{7,6},{8,11},{9,8},{10,9... | collective-permute-start | bytes 6152 | tf_op jit(solution)/shard_map/ppermute | solution.py:539
  43.1 1.6 %collective-permute-done.12 = f32[4,128]{1,0:T(4,128)S(1)} collective-permute-done((f32[4,128]{1,0:T(4,128)S(1)}, f32[4,128]{1,0:T(4,128)S(1)}, u32[]{:S(2)}, u32[]{:S(2)}) %collective-permute-start.12) | collective-permute-done | bytes 2080 | tf_op jit(solution)/shard_map/ppermute | solution.py:539
  44.7 0.0 collective-permute-done.13
  44.7 0.7 %collective-permute-done.14 = f32[4,128]{1,0:T(4,128)S(1)} collective-permute-done((f32[4,128]{1,0:T(4,128)S(1)}, f32[4,128]{1,0:T(4,128)S(1)}, u32[]{:S(2)}, u32[]{:S(2)}) %collective-permute-start.14) | collective-permute-done | bytes 2080 | tf_op jit(solution)/shard_map/ppermute | solution.py:539
  45.4 0.6 %add_add_fusion = f32[4,128]{1,0:T(4,128)} fusion(f32[4,128]{1,0:T(4,128)S(1)} %collective-permute-done.14, f32[4,128]{1,0:T(4,128)S(1)} %collective-permute-done.13, f32[4,128]{1,0:T(4,128)S(1)} %lever_scores.1, f32[4,128]{1,0:T(4,128)S(1)} %collective-permute-done.12), kind=kLoop, calls=%fused_computation | loop fusion | flops 1536 | bytes 10240 | tf_op jit(solution)/shard_map/add | solution.py:539
  (8 shorter events, 0.1 us)
Async XLA Ops:
  0.0 5.1 %copy-start = (bf16[2,4,256,2048]{3,2,1,0:T(8,128)(2,1)S(1)}, bf16[2,4,256,2048]{3,2,1,0:T(8,128)(2,1)}, u32[]{:S(2)}) copy-start(bf16[2,4,256,2048]{3,2,1,0:T(8,128)(2,1)} %refs_5_.2) | copy-start | bytes 25165828
  0.0 5.1 %copy-start.1 = (bf16[2,64,2048]{2,1,0:T(8,128)(2,1)S(1)}, bf16[2,64,2048]{2,1,0:T(8,128)(2,1)}, u32[]{:S(2)}) copy-start(bf16[2,64,2048]{2,1,0:T(8,128)(2,1)} %refs_6_.2) | copy-start | bytes 1572868
  2.0 4.4 %copy-start.2 = (bf16[2,1,256,2048]{3,2,1,0:T(8,128)(2,1)S(1)}, bf16[2,1,256,2048]{3,2,1,0:T(8,128)(2,1)}, u32[]{:S(2)}) copy-start(bf16[2,1,256,2048]{3,2,1,0:T(8,128)(2,1)} %refs_1_.6) | copy-start | bytes 6291460
  2.0 5.3 %collective-permute-start = (f32[1,64,256]{2,1,0:T(8,128)S(1)}, f32[1,64,256]{2,1,0:T(8,128)S(1)}, u32[]{:S(2)}, u32[]{:S(2)}) collective-permute-start(f32[1,64,256]{2,1,0:T(8,128)S(1)} %first_partial.1.refs_3_), channel_id=1, source_target_pairs={{0,1},{1,0},{2,3},{3,2},{4,5},{5,4},{6,7},{7,6},{8,9},{9,8},{10,11... | collective-permute-start | bytes 196616 | tf_op jit(solution)/shard_map/ppermute | solution.py:493
  6.4 5.6 %copy-start.4 = (bf16[2,16,64,128]{3,2,1,0:T(8,128)(2,1)S(1)}, bf16[2,16,64,128]{3,2,1,0:T(8,128)(2,1)}, u32[]{:S(2)}) copy-start(bf16[2,16,64,128]{3,2,1,0:T(8,128)(2,1)} %refs_2_.11) | copy-start | bytes 1572868
  6.4 5.6 %copy-start.5 = (f32[128256]{0:T(1024)S(1)}, f32[128256]{0:T(1024)}, u32[]{:S(2)}) copy-start(f32[128256]{0:T(1024)} %param.17) | copy-start | bytes 1539076
  6.4 5.6 %copy-start.8 = (bf16[2,1,256,2048]{3,2,1,0:T(8,128)(2,1)S(1)}, bf16[2,1,256,2048]{3,2,1,0:T(8,128)(2,1)}, u32[]{:S(2)}) copy-start(bf16[2,1,256,2048]{3,2,1,0:T(8,128)(2,1)} %refs_2_.9) | copy-start | bytes 6291460
  6.4 5.6 %copy-start.9 = (s32[1,256]{1,0:T(1,128)S(1)}, s32[1,256]{1,0:T(1,128)}, u32[]{:S(2)}) copy-start(s32[1,256]{1,0:T(1,128)} %refs_1_.7) | copy-start | bytes 3076
  7.3 6.8 %collective-permute-start.1 = (f32[1,64,256]{2,1,0:T(8,128)S(1)}, f32[1,64,256]{2,1,0:T(8,128)S(1)}, u32[]{:S(2)}, u32[]{:S(2)}) collective-permute-start(f32[1,64,256]{2,1,0:T(8,128)S(1)} %add.23.refs_7_.refs_0_.refs_1_), channel_id=1, source_target_pairs={{0,2},{2,0},{1,3},{3,1},{4,6},{6,4},{5,7},{7,5},{8,10},{10,8},{9,1... | collective-permute-start | bytes 196616 | tf_op jit(solution)/shard_map/ppermute | solution.py:496
  10.4 8.5 %collective-permute-start.3 = (f32[4,64,256]{2,1,0:T(8,128)S(1)}, f32[4,64,256]{2,1,0:T(8,128)S(1)}, u32[]{:S(2)}, u32[]{:S(2)}) collective-permute-start(f32[4,64,256]{2,1,0:T(8,128)S(1)} %hold.4), channel_id=1, source_target_pairs={{0,1},{1,0},{2,3},{3,2},{4,5},{5,4},{6,7},{7,6},{8,9},{9,8},{10,11... | collective-permute-start | bytes 786440 | tf_op jit(solution)/shard_map/ppermute | solution.py:493
  12.0 7.9 %copy-start.3 = (f32[2,16,64,64]{3,2,1,0:T(8,128)S(1)}, f32[2,16,64,64]{3,2,1,0:T(8,128)}, u32[]{:S(2)}) copy-start(f32[2,16,64,64]{3,2,1,0:T(8,128)} %refs_6_.3) | copy-start | bytes 1572868
  12.0 7.9 %copy-start.6 = (f32[2,64,64]{2,1,0:T(8,128)S(1)}, f32[2,64,64]{2,1,0:T(8,128)}, u32[]{:S(2)}) copy-start(f32[2,64,64]{2,1,0:T(8,128)} %refs_5_.3) | copy-start | bytes 98308
  14.1 10.3 %copy-start.7 = (s32[4,256]{1,0:T(4,128)S(1)}, s32[4,256]{1,0:T(4,128)}, u32[]{:S(2)}) copy-start(s32[4,256]{1,0:T(4,128)} %refs_0_.2) | copy-start | bytes 12292
  14.2 5.8 %collective-permute-start.2 = (f32[1,64,256]{2,1,0:T(8,128)S(1)}, f32[1,64,256]{2,1,0:T(8,128)S(1)}, u32[]{:S(2)}, u32[]{:S(2)}) collective-permute-start(f32[1,64,256]{2,1,0:T(8,128)S(1)} %settle.1.refs_1_), channel_id=1, source_target_pairs={{0,1},{1,0},{2,3},{3,2},{4,5},{5,4},{6,7},{7,6},{8,9},{9,8},{10,11... | collective-permute-start | bytes 196616 | tf_op jit(solution)/shard_map/ppermute | solution.py:493
  19.0 12.8 %collective-permute-start.7 = (f32[4,64,256]{2,1,0:T(8,128)S(1)}, f32[4,64,256]{2,1,0:T(8,128)S(1)}, u32[]{:S(2)}, u32[]{:S(2)}) collective-permute-start(f32[4,64,256]{2,1,0:T(8,128)S(1)} %add.24.refs_7_), channel_id=1, source_target_pairs={{0,2},{2,0},{1,3},{3,1},{4,6},{6,4},{5,7},{7,5},{8,10},{10,8},{9,1... | collective-permute-start | bytes 786440 | tf_op jit(solution)/shard_map/ppermute | solution.py:496
  21.8 10.2 %collective-permute-start.8 = (f32[1,64,1024]{2,1,0:T(8,128)S(1)}, f32[1,64,1024]{2,1,0:T(8,128)S(1)}, u32[]{:S(2)}, u32[]{:S(2)}) collective-permute-start(f32[1,64,1024]{2,1,0:T(8,128)S(1)} %get-tuple-element.16.refs_2_), channel_id=1, source_target_pairs={{0,8},{8,0},{4,12},{12,4},{1,9},{9,1},{5,13},{13,5},{2,10},{10,2},... | collective-permute-start | bytes 786440 | tf_op jit(solution)/shard_map/ppermute | solution.py:496
  23.4 10.7 %collective-permute-start.6 = (f32[1,64,1024]{2,1,0:T(8,128)S(1)}, f32[1,64,1024]{2,1,0:T(8,128)S(1)}, u32[]{:S(2)}, u32[]{:S(2)}) collective-permute-start(f32[1,64,1024]{2,1,0:T(8,128)S(1)} %get-tuple-element.15.refs_1_), channel_id=1, source_target_pairs={{0,8},{8,0},{4,12},{12,4},{1,9},{9,1},{5,13},{13,5},{2,10},{10,2},... | collective-permute-start | bytes 786440 | tf_op jit(solution)/shard_map/ppermute | solution.py:496
  23.9 11.4 %collective-permute-start.4 = (f32[1,64,1024]{2,1,0:T(8,128)S(1)}, f32[1,64,1024]{2,1,0:T(8,128)S(1)}, u32[]{:S(2)}, u32[]{:S(2)}) collective-permute-start(f32[1,64,1024]{2,1,0:T(8,128)S(1)} %get-tuple-element.15.refs_1_), channel_id=1, source_target_pairs={{0,4},{4,0},{8,12},{12,8},{1,5},{5,1},{9,13},{13,9},{2,6},{6,2},{1... | collective-permute-start | bytes 786440 | tf_op jit(solution)/shard_map/ppermute | solution.py:493
  23.9 11.4 %collective-permute-start.5 = (f32[1,64,1024]{2,1,0:T(8,128)S(1)}, f32[1,64,1024]{2,1,0:T(8,128)S(1)}, u32[]{:S(2)}, u32[]{:S(2)}) collective-permute-start(f32[1,64,1024]{2,1,0:T(8,128)S(1)} %get-tuple-element.16.refs_2_), channel_id=1, source_target_pairs={{0,4},{4,0},{8,12},{12,8},{1,5},{5,1},{9,13},{13,9},{2,6},{6,2},{1... | collective-permute-start | bytes 786440 | tf_op jit(solution)/shard_map/ppermute | solution.py:493
  31.8 7.2 %collective-permute-start.11 = (f32[4,64,256]{2,1,0:T(8,128)S(1)}, f32[4,64,256]{2,1,0:T(8,128)S(1)}, u32[]{:S(2)}, u32[]{:S(2)}) collective-permute-start(f32[4,64,256]{2,1,0:T(8,128)S(1)} %add.25.refs_1_.refs_3_.refs_9_), channel_id=1, source_target_pairs={{0,1},{1,0},{2,3},{3,2},{4,5},{5,4},{6,7},{7,6},{8,9},{9,8},{10,11... | collective-permute-start | bytes 786440 | tf_op jit(solution)/shard_map/ppermute | solution.py:493
  31.9 3.4 %collective-permute-start.10 = (f32[1,64,1024]{2,1,0:T(8,128)S(1)}, f32[1,64,1024]{2,1,0:T(8,128)S(1)}, u32[]{:S(2)}, u32[]{:S(2)}) collective-permute-start(f32[1,64,1024]{2,1,0:T(8,128)S(1)} %hold.7.refs_6_), channel_id=1, source_target_pairs={{0,4},{4,0},{8,12},{12,8},{1,5},{5,1},{9,13},{13,9},{2,6},{6,2},{1... | collective-permute-start | bytes 786440 | tf_op jit(solution)/shard_map/ppermute | solution.py:493
  34.0 1.5 %collective-permute-start.9 = (f32[1,64,1024]{2,1,0:T(8,128)S(1)}, f32[1,64,1024]{2,1,0:T(8,128)S(1)}, u32[]{:S(2)}, u32[]{:S(2)}) collective-permute-start(f32[1,64,1024]{2,1,0:T(8,128)S(1)} %hold.6.refs_5_), channel_id=1, source_target_pairs={{0,4},{4,0},{8,12},{12,8},{1,5},{5,1},{9,13},{13,9},{2,6},{6,2},{1... | collective-permute-start | bytes 786440 | tf_op jit(solution)/shard_map/ppermute | solution.py:493
  39.3 5.4 %collective-permute-start.12 = (f32[4,128]{1,0:T(4,128)S(1)}, f32[4,128]{1,0:T(4,128)S(1)}, u32[]{:S(2)}, u32[]{:S(2)}) collective-permute-start(f32[4,128]{1,0:T(4,128)S(1)} %lever_scores.1), channel_id=1, source_target_pairs={{0,1},{1,2},{2,3},{3,0},{4,5},{5,6},{6,7},{7,4},{8,9},{9,10},{10,1... | collective-permute-start | bytes 6152 | tf_op jit(solution)/shard_map/ppermute | solution.py:539
  40.1 4.6 %collective-permute-start.13 = (f32[4,128]{1,0:T(4,128)S(1)}, f32[4,128]{1,0:T(4,128)S(1)}, u32[]{:S(2)}, u32[]{:S(2)}) collective-permute-start(f32[4,128]{1,0:T(4,128)S(1)} %lever_scores.1), channel_id=1, source_target_pairs={{0,2},{1,3},{2,0},{3,1},{4,6},{5,7},{6,4},{7,5},{8,10},{9,11},{10,... | collective-permute-start | bytes 6152 | tf_op jit(solution)/shard_map/ppermute | solution.py:539
  41.8 3.6 %collective-permute-start.14 = (f32[4,128]{1,0:T(4,128)S(1)}, f32[4,128]{1,0:T(4,128)S(1)}, u32[]{:S(2)}, u32[]{:S(2)}) collective-permute-start(f32[4,128]{1,0:T(4,128)S(1)} %lever_scores.1), channel_id=1, source_target_pairs={{0,3},{1,0},{2,1},{3,2},{4,7},{5,4},{6,5},{7,6},{8,11},{9,8},{10,9... | collective-permute-start | bytes 6152 | tf_op jit(solution)/shard_map/ppermute | solution.py:539

commit v6 on v5

--- a/solution.py
+++ b/solution.py
@@ -531,7 +531,10 @@
             across,
             [near(one, "dp") for one in across],
         ]
-        terms = score_terms(mine, flip, norm, every, owns, train_scale, in_own)
+        terms = lever_scores(
+            flip, norm, query_levers(mine, every, in_own), owns[0], train_scale,
+            jnp.zeros((n_dp, 128), F32),
+        )
         levers = query_levers(other, every, in_other)
         terms = lever_scores(flip, norm, levers, others[0], train_scale, terms)
         total = terms

time: 46.1 us -> 46 us (level)
  Pallas kernels: 17.4 us -> 16.9 us
  waiting for transfers between devices: 11 us -> 11.5 us
    pallas_call x13 -> x14, Pallas kernels: 17.4 us -> 16.9 us  [call(): pl.pallas_call(body, out_shape=out_shape, grid_spec=pltpu.PrefetchScalarG...]
    ppermute x8, waiting for transfers between devices: 5.42 us -> 5.89 us  [near(): return lax.ppermute(array, axis, NEAR)]
  transfers between devices with their start and end apart: 15 -> 15, of which waited for: 8 -> 8; matrix products, arithmetic and copies ran while one was open for 0% -> 0% of each run, Pallas kernels for 33% -> 32%
where the time goes in v6:
time: 46 us; the launch traced here: 45.9 us
  Pallas kernels  16.9 us (37%)
  starting transfers between devices  16.5 us (36%)
  waiting for transfers between devices  11.5 us (25%)
  other arithmetic  0.66 us (1%)
    pallas_call x14, Pallas kernels, call(): pl.pallas_call(body, out_shape=out_shape, grid_spec=pltpu.PrefetchScalarG...  16.9 us
    ppermute x8, starting transfers between devices, near(): return lax.ppermute(array, axis, NEAR)  6.56 us
    ppermute x4, starting transfers between devices, far(): return lax.ppermute(array, axis, FAR)  6.1 us
    ppermute x8, waiting for transfers between devices, near(): return lax.ppermute(array, axis, NEAR)  5.89 us
    ppermute x3, starting transfers between devices, local(): lax.ppermute(terms, 'head', [(idx, (idx + shift) % 4) for idx in range(4)])  3.87 us
    ppermute x4, waiting for transfers between devices, far(): return lax.ppermute(array, axis, FAR)  3.46 us
    ppermute x3, waiting for transfers between devices, local(): lax.ppermute(terms, 'head', [(idx, (idx + shift) % 4) for idx in range(4)])  2.18 us
  transfers between devices with their start and end apart: 15, of which 8 were waited for; matrix products, arithmetic and copies ran while one was open for 0% of the time, Pallas kernels for 32%

profile of v6, /device:TPU:0, one launch (start us, length us, event | category | flops | bytes accessed | tf_op | source)
XLA Modules:
  0.0 45.9 jit_solution(15477382348097755985)
XLA Ops:
  0.0 0.0 copy-start
  0.0 0.0 copy-start.1
  0.0 1.9 %first_partial.1.refs_3_ = f32[1,64,256]{2,1,0:T(8,128)S(1)} custom-call(s32[1]{0:T(128)S(6)} %sub.3.refs_0_, bf16[2,1,256,2048]{3,2,1,0:T(8,128)(2,1)} %refs_1_.6, bf16[2,64,2048]{2,1,0:T(8,128)(2,1)} %refs_6_.2), custom_call_target="tpu_custom_call" | custom-call | flops 8800000000 | tf_op jit(solution)/shard_map/first_partial/pallas_call | solution.py:31
  2.0 0.0 copy-start.2
  2.0 3.1 %collective-permute-start = (f32[1,64,256]{2,1,0:T(8,128)S(1)}, f32[1,64,256]{2,1,0:T(8,128)S(1)}, u32[]{:S(2)}, u32[]{:S(2)}) collective-permute-start(f32[1,64,256]{2,1,0:T(8,128)S(1)} %first_partial.1.refs_3_), channel_id=1, source_target_pairs={{0,1},{1,0},{2,3},{3,2},{4,5},{5,4},{6,7},{7,6},{8,9},{9,8},{10,11... | collective-permute-start | bytes 196616 | tf_op jit(solution)/shard_map/ppermute | solution.py:493
  5.1 0.0 copy-done
  5.1 0.0 copy-done.1
  5.1 1.3 %sides_partial.2.refs_3_.refs_0_ = f32[4,64,256]{2,1,0:T(8,128)S(1)} custom-call(s32[1]{0:T(128)S(6)} %sub.3.refs_0_, bf16[2,4,256,2048]{3,2,1,0:T(8,128)(2,1)S(1)} %copy-done, bf16[2,64,2048]{2,1,0:T(8,128)(2,1)S(1)} %copy-done.1, f32[1,64,256]{2,1,0:T(8,128)S(1)} %first_partial.1.refs_3_), custom_call_target="tpu_custom_call" | custom-call | flops 2200000000 | tf_op jit(solution)/shard_map/sides_partial/pallas_call | solution.py:31
  6.4 0.0 copy-done.2
  6.4 0.0 copy-start.4
  6.4 0.0 copy-start.5
  6.4 0.0 copy-start.8
  6.4 0.0 copy-start.9
  6.4 0.5 %sides_partial.3 = f32[1,64,256]{2,1,0:T(8,128)S(1)} custom-call(s32[1]{0:T(128)} %bitcast.1.refs_0_, bf16[2,1,256,2048]{3,2,1,0:T(8,128)(2,1)S(1)} %copy-done.2, bf16[2,64,2048]{2,1,0:T(8,128)(2,1)S(1)} %copy-done.1, f32[4,64,256]{2,1,0:T(8,128)S(1)} %sides_partial.2.refs_3_.refs_0_), custom_call_target="tpu_custom_call" | custom-call | flops 550000000 | tf_op jit(solution)/shard_map/sides_partial/pallas_call | solution.py:31
  6.9 0.4 collective-permute-done
  7.3 3.1 %collective-permute-start.1 = (f32[1,64,256]{2,1,0:T(8,128)S(1)}, f32[1,64,256]{2,1,0:T(8,128)S(1)}, u32[]{:S(2)}, u32[]{:S(2)}) collective-permute-start(f32[1,64,256]{2,1,0:T(8,128)S(1)} %add.23.refs_7_.refs_0_.refs_1_), channel_id=1, source_target_pairs={{0,2},{2,0},{1,3},{3,1},{4,6},{6,4},{5,7},{7,5},{8,10},{10,8},{9,1... | collective-permute-start | bytes 196616 | tf_op jit(solution)/shard_map/ppermute | solution.py:496
  10.4 1.6 %collective-permute-start.3 = (f32[4,64,256]{2,1,0:T(8,128)S(1)}, f32[4,64,256]{2,1,0:T(8,128)S(1)}, u32[]{:S(2)}, u32[]{:S(2)}) collective-permute-start(f32[4,64,256]{2,1,0:T(8,128)S(1)} %hold.4), channel_id=1, source_target_pairs={{0,1},{1,0},{2,3},{3,2},{4,5},{5,4},{6,7},{7,6},{8,9},{9,8},{10,11... | collective-permute-start | bytes 786440 | tf_op jit(solution)/shard_map/ppermute | solution.py:493
  12.0 0.0 copy-done.4
  12.0 0.0 copy-done.5
  12.0 0.0 copy-done.8
  12.0 0.0 copy-done.9
  12.0 0.0 copy-start.3
  12.0 0.0 copy-start.6
  12.0 2.1 %query_in_and_side.1 = (bf16[2,1,256,1024]{3,2,1,0:T(8,128)(2,1)S(1)}, f32[1,256]{1,0:T(1,128)S(1)}, f32[4,64,256]{2,1,0:T(8,128)S(1)}) custom-call(s32[1]{0:T(128)} %bitcast.1.refs_0_, s32[1,256]{1,0:T(1,128)S(1)} %copy-done.9, bf16[2,1,256,2048]{3,2,1,0:T(8,128)(2,1)S(1)} %copy-done.8, bf16[2,16,64,128]{3,2,1,0:T(8,128)(2,1)S(1)} %copy-done.4, ...), custom_call_target="tpu_custom_call" | custom-call | flops 3300000000 | tf_op jit(solution)/shard_map/query_in_and_side/pallas_call | solution.py:31
  14.1 0.0 copy-start.7
  14.2 0.0 collective-permute-done.1.refs_1_
  14.2 1.2 %collective-permute-start.2 = (f32[1,64,256]{2,1,0:T(8,128)S(1)}, f32[1,64,256]{2,1,0:T(8,128)S(1)}, u32[]{:S(2)}, u32[]{:S(2)}) collective-permute-start(f32[1,64,256]{2,1,0:T(8,128)S(1)} %settle.1.refs_1_), channel_id=1, source_target_pairs={{0,1},{1,0},{2,3},{3,2},{4,5},{5,4},{6,7},{7,6},{8,9},{9,8},{10,11... | collective-permute-start | bytes 196616 | tf_op jit(solution)/shard_map/ppermute | solution.py:493
  15.4 3.5 %collective-permute-done.3 = f32[4,64,256]{2,1,0:T(8,128)S(1)} collective-permute-done((f32[4,64,256]{2,1,0:T(8,128)S(1)}, f32[4,64,256]{2,1,0:T(8,128)S(1)}, u32[]{:S(2)}, u32[]{:S(2)}) %collective-permute-start.3) | collective-permute-done | bytes 262176 | tf_op jit(solution)/shard_map/ppermute | solution.py:493
  19.0 0.9 %collective-permute-start.7 = (f32[4,64,256]{2,1,0:T(8,128)S(1)}, f32[4,64,256]{2,1,0:T(8,128)S(1)}, u32[]{:S(2)}, u32[]{:S(2)}) collective-permute-start(f32[4,64,256]{2,1,0:T(8,128)S(1)} %add.24.refs_7_), channel_id=1, source_target_pairs={{0,2},{2,0},{1,3},{3,1},{4,6},{6,4},{5,7},{7,5},{8,10},{10,8},{9,1... | collective-permute-start | bytes 786440 | tf_op jit(solution)/shard_map/ppermute | solution.py:496
  19.9 0.0 collective-permute-done.2.refs_2_
  19.9 0.0 copy-done.3
  19.9 0.0 copy-done.6
  20.0 1.8 %query_ready.1 = (f32[1,64,1024]{2,1,0:T(8,128)S(1)}, f32[1,64,1024]{2,1,0:T(8,128)S(1)}) custom-call(s32[1]{0:T(128)} %bitcast.1.refs_0_, f32[1,64,256]{2,1,0:T(8,128)S(1)} %settle.1.refs_1_, f32[1,64,256]{2,1,0:T(8,128)S(1)} %collective-permute-done.2.refs_2_, f32[1,256]{1,0:T(1,128)S(1)} %get-tuple-element.12.refs_2_.refs_3_, ...), custom_call_target="tpu_custom_call" | custom-call | flops 110000000 | tf_op jit(solution)/shard_map/query_ready/pallas_call | solution.py:31
  21.8 1.5 %collective-permute-start.8 = (f32[1,64,1024]{2,1,0:T(8,128)S(1)}, f32[1,64,1024]{2,1,0:T(8,128)S(1)}, u32[]{:S(2)}, u32[]{:S(2)}) collective-permute-start(f32[1,64,1024]{2,1,0:T(8,128)S(1)} %get-tuple-element.16.refs_2_), channel_id=1, source_target_pairs={{0,8},{8,0},{4,12},{12,4},{1,9},{9,1},{5,13},{13,5},{2,10},{10,2},... | collective-permute-start | bytes 786440 | tf_op jit(solution)/shard_map/ppermute | solution.py:496
  23.3 0.5 %collective-permute-start.6 = (f32[1,64,1024]{2,1,0:T(8,128)S(1)}, f32[1,64,1024]{2,1,0:T(8,128)S(1)}, u32[]{:S(2)}, u32[]{:S(2)}) collective-permute-start(f32[1,64,1024]{2,1,0:T(8,128)S(1)} %get-tuple-element.15.refs_1_), channel_id=1, source_target_pairs={{0,8},{8,0},{4,12},{12,4},{1,9},{9,1},{5,13},{13,5},{2,10},{10,2},... | collective-permute-start | bytes 786440 | tf_op jit(solution)/shard_map/ppermute | solution.py:496
  23.8 0.0 collective-permute-start.4
  23.8 0.5 %collective-permute-start.5 = (f32[1,64,1024]{2,1,0:T(8,128)S(1)}, f32[1,64,1024]{2,1,0:T(8,128)S(1)}, u32[]{:S(2)}, u32[]{:S(2)}) collective-permute-start(f32[1,64,1024]{2,1,0:T(8,128)S(1)} %get-tuple-element.16.refs_2_), channel_id=1, source_target_pairs={{0,4},{4,0},{8,12},{12,8},{1,5},{5,1},{9,13},{13,9},{2,6},{6,2},{1... | collective-permute-start | bytes 786440 | tf_op jit(solution)/shard_map/ppermute | solution.py:493
  24.3 0.0 copy-done.7
  24.3 1.3 %token_scale.1.refs_1_.refs_3_ = f32[4,256]{1,0:T(4,128)S(1)} custom-call(s32[4,256]{1,0:T(4,128)S(1)} %copy-done.7, f32[1002,128]{1,0:T(8,128)S(1)} %bitcast.5, f32[1,64,1024]{2,1,0:T(8,128)S(1)} %get-tuple-element.16.refs_2_), custom_call_target="tpu_custom_call" | custom-call | flops 110000000 | tf_op jit(solution)/shard_map/token_scale/pallas_call | solution.py:31
  25.6 3.5 %staged.1 = (bf16[2,4,256,2048]{3,2,1,0:T(8,128)(2,1)S(1)}, f32[8,128]{1,0:T(8,128)S(1)}) custom-call(bf16[2,4,256,2048]{3,2,1,0:T(8,128)(2,1)} %refs_0_.3, f32[4,256]{1,0:T(4,128)S(1)} %token_scale.1.refs_1_.refs_3_), custom_call_target="tpu_custom_call" | custom-call | flops 110000000 | tf_op jit(solution)/shard_map/staged/pallas_call | solution.py:31
  29.1 2.7 %collective-permute-done.7.refs_0_ = f32[4,64,256]{2,1,0:T(8,128)S(1)} collective-permute-done((f32[4,64,256]{2,1,0:T(8,128)S(1)}, f32[4,64,256]{2,1,0:T(8,128)S(1)}, u32[]{:S(2)}, u32[]{:S(2)}) %collective-permute-start.7) | collective-permute-done | bytes 262176 | tf_op jit(solution)/shard_map/ppermute | solution.py:496
  31.8 0.1 collective-permute-start.11
  31.9 0.0 collective-permute-done.8.refs_0_
  31.9 0.1 collective-permute-start.10
  32.0 1.3 %in_side_of_layer.2.refs_9_.refs_3_ = bf16[4,256,1024]{2,1,0:T(8,128)(2,1)S(1)} custom-call(s32[1]{0:T(128)S(6)} %sub.3.refs_0_, bf16[2,4,256,2048]{3,2,1,0:T(8,128)(2,1)S(1)} %get-tuple-element.18.refs_1_, bf16[2,16,64,128]{3,2,1,0:T(8,128)(2,1)S(1)} %copy-done.4, f32[4,64,256]{2,1,0:T(8,128)S(1)} %add.25.refs_1_.refs_3_.refs_2_), custom_call_target="tpu_custom_call" | custom-call | flops 2750000128 | tf_op jit(solution)/shard_map/in_side_of_layer/pallas_call | solution.py:31
  33.3 0.7 %collective-permute-done.6.refs_0_ = f32[1,64,1024]{2,1,0:T(8,128)S(1)} collective-permute-done((f32[1,64,1024]{2,1,0:T(8,128)S(1)}, f32[1,64,1024]{2,1,0:T(8,128)S(1)}, u32[]{:S(2)}, u32[]{:S(2)}) %collective-permute-start.6) | collective-permute-done | bytes 262176 | tf_op jit(solution)/shard_map/ppermute | solution.py:496
  34.0 0.0 collective-permute-start.9
  34.0 1.3 %in_side_of_layer.3.refs_9_ = bf16[4,256,1024]{2,1,0:T(8,128)(2,1)S(1)} custom-call(s32[1]{0:T(128)} %bitcast.1.refs_0_, bf16[2,4,256,2048]{3,2,1,0:T(8,128)(2,1)S(1)} %get-tuple-element.18.refs_1_, bf16[2,16,64,128]{3,2,1,0:T(8,128)(2,1)S(1)} %copy-done.4, bf16[4,256,1024]{2,1,0:T(8,128)(2,1)S(1)} %in_side_of_layer.2.refs_9_.refs_3_), custom_call_target="tpu_custom_call" | custom-call | flops 6600000000 | tf_op jit(solution)/shard_map/in_side_of_layer/pallas_call | solution.py:31
  35.3 0.0 collective-permute-done.4.refs_3_
  35.3 0.0 collective-permute-done.5.refs_4_
  35.3 0.0 collective-permute-done.10.refs_8_
  35.3 0.2 collective-permute-done.9.refs_7_
  35.6 0.8 %query_levers.3.refs_1_ = f32[4,256,256]{2,1,0:T(8,128)S(1)} custom-call(s32[1]{0:T(128)} %bitcast.1.refs_0_, f32[1,64,1024]{2,1,0:T(8,128)S(1)} %get-tuple-element.15.refs_1_, f32[1,64,1024]{2,1,0:T(8,128)S(1)} %get-tuple-element.16.refs_2_, f32[1,64,1024]{2,1,0:T(8,128)S(1)} %collective-permute-done.4.refs_3_, ...), custom_call_target="tpu_custom_call" | custom-call | flops 1650000000 | tf_op jit(solution)/shard_map/query_levers/pallas_call | solution.py:31
  36.4 0.2 lever_scores.2.refs_4_
  36.6 0.8 %query_levers.2.refs_1_ = f32[4,256,256]{2,1,0:T(8,128)S(1)} custom-call(s32[1]{0:T(128)S(6)} %sub.3.refs_0_, f32[1,64,1024]{2,1,0:T(8,128)S(1)} %get-tuple-element.15.refs_1_, f32[1,64,1024]{2,1,0:T(8,128)S(1)} %get-tuple-element.16.refs_2_, f32[1,64,1024]{2,1,0:T(8,128)S(1)} %collective-permute-done.4.refs_3_, ...), custom_call_target="tpu_custom_call" | custom-call | flops 1650000000 | tf_op jit(solution)/shard_map/query_levers/pallas_call | solution.py:31
  37.4 1.7 %collective-permute-done.11.refs_2_ = f32[4,64,256]{2,1,0:T(8,128)S(1)} collective-permute-done((f32[4,64,256]{2,1,0:T(8,128)S(1)}, f32[4,64,256]{2,1,0:T(8,128)S(1)}, u32[]{:S(2)}, u32[]{:S(2)}) %collective-permute-start.11) | collective-permute-done | bytes 262176 | tf_op jit(solution)/shard_map/ppermute | solution.py:493
  39.1 0.2 lever_scores.3
  39.3 0.8 %collective-permute-start.12 = (f32[4,128]{1,0:T(4,128)S(1)}, f32[4,128]{1,0:T(4,128)S(1)}, u32[]{:S(2)}, u32[]{:S(2)}) collective-permute-start(f32[4,128]{1,0:T(4,128)S(1)} %lever_scores.3), channel_id=1, source_target_pairs={{0,1},{1,2},{2,3},{3,0},{4,5},{5,6},{6,7},{7,4},{8,9},{9,10},{10,1... | collective-permute-start | bytes 6152 | tf_op jit(solution)/shard_map/ppermute | solution.py:542
  40.0 1.7 %collective-permute-start.13 = (f32[4,128]{1,0:T(4,128)S(1)}, f32[4,128]{1,0:T(4,128)S(1)}, u32[]{:S(2)}, u32[]{:S(2)}) collective-permute-start(f32[4,128]{1,0:T(4,128)S(1)} %lever_scores.3), channel_id=1, source_target_pairs={{0,2},{1,3},{2,0},{3,1},{4,6},{5,7},{6,4},{7,5},{8,10},{9,11},{10,... | collective-permute-start | bytes 6152 | tf_op jit(solution)/shard_map/ppermute | solution.py:542
  41.7 1.4 %collective-permute-start.14 = (f32[4,128]{1,0:T(4,128)S(1)}, f32[4,128]{1,0:T(4,128)S(1)}, u32[]{:S(2)}, u32[]{:S(2)}) collective-permute-start(f32[4,128]{1,0:T(4,128)S(1)} %lever_scores.3), channel_id=1, source_target_pairs={{0,3},{1,0},{2,1},{3,2},{4,7},{5,4},{6,5},{7,6},{8,11},{9,8},{10,9... | collective-permute-start | bytes 6152 | tf_op jit(solution)/shard_map/ppermute | solution.py:542
  43.1 1.6 %collective-permute-done.12 = f32[4,128]{1,0:T(4,128)S(1)} collective-permute-done((f32[4,128]{1,0:T(4,128)S(1)}, f32[4,128]{1,0:T(4,128)S(1)}, u32[]{:S(2)}, u32[]{:S(2)}) %collective-permute-start.12) | collective-permute-done | bytes 2080 | tf_op jit(solution)/shard_map/ppermute | solution.py:542
  44.7 0.0 collective-permute-done.13
  44.7 0.6 %collective-permute-done.14 = f32[4,128]{1,0:T(4,128)S(1)} collective-permute-done((f32[4,128]{1,0:T(4,128)S(1)}, f32[4,128]{1,0:T(4,128)S(1)}, u32[]{:S(2)}, u32[]{:S(2)}) %collective-permute-start.14) | collective-permute-done | bytes 2080 | tf_op jit(solution)/shard_map/ppermute | solution.py:542
  45.3 0.6 %add_add_fusion = f32[4,128]{1,0:T(4,128)} fusion(f32[4,128]{1,0:T(4,128)S(1)} %collective-permute-done.14, f32[4,128]{1,0:T(4,128)S(1)} %collective-permute-done.13, f32[4,128]{1,0:T(4,128)S(1)} %lever_scores.3, f32[4,128]{1,0:T(4,128)S(1)} %collective-permute-done.12), kind=kLoop, calls=%fused_computation | loop fusion | flops 1536 | bytes 10240 | tf_op jit(solution)/shard_map/add | solution.py:542
  (9 shorter events, 0.1 us)
Async XLA Ops:
  0.0 5.1 %copy-start = (bf16[2,4,256,2048]{3,2,1,0:T(8,128)(2,1)S(1)}, bf16[2,4,256,2048]{3,2,1,0:T(8,128)(2,1)}, u32[]{:S(2)}) copy-start(bf16[2,4,256,2048]{3,2,1,0:T(8,128)(2,1)} %refs_5_.2) | copy-start | bytes 25165828
  0.0 5.1 %copy-start.1 = (bf16[2,64,2048]{2,1,0:T(8,128)(2,1)S(1)}, bf16[2,64,2048]{2,1,0:T(8,128)(2,1)}, u32[]{:S(2)}) copy-start(bf16[2,64,2048]{2,1,0:T(8,128)(2,1)} %refs_6_.2) | copy-start | bytes 1572868
  2.0 4.4 %copy-start.2 = (bf16[2,1,256,2048]{3,2,1,0:T(8,128)(2,1)S(1)}, bf16[2,1,256,2048]{3,2,1,0:T(8,128)(2,1)}, u32[]{:S(2)}) copy-start(bf16[2,1,256,2048]{3,2,1,0:T(8,128)(2,1)} %refs_1_.6) | copy-start | bytes 6291460
  2.0 5.3 %collective-permute-start = (f32[1,64,256]{2,1,0:T(8,128)S(1)}, f32[1,64,256]{2,1,0:T(8,128)S(1)}, u32[]{:S(2)}, u32[]{:S(2)}) collective-permute-start(f32[1,64,256]{2,1,0:T(8,128)S(1)} %first_partial.1.refs_3_), channel_id=1, source_target_pairs={{0,1},{1,0},{2,3},{3,2},{4,5},{5,4},{6,7},{7,6},{8,9},{9,8},{10,11... | collective-permute-start | bytes 196616 | tf_op jit(solution)/shard_map/ppermute | solution.py:493
  6.4 5.6 %copy-start.4 = (bf16[2,16,64,128]{3,2,1,0:T(8,128)(2,1)S(1)}, bf16[2,16,64,128]{3,2,1,0:T(8,128)(2,1)}, u32[]{:S(2)}) copy-start(bf16[2,16,64,128]{3,2,1,0:T(8,128)(2,1)} %refs_2_.11) | copy-start | bytes 1572868
  6.4 5.6 %copy-start.5 = (f32[128256]{0:T(1024)S(1)}, f32[128256]{0:T(1024)}, u32[]{:S(2)}) copy-start(f32[128256]{0:T(1024)} %param.17) | copy-start | bytes 1539076
  6.4 5.6 %copy-start.8 = (bf16[2,1,256,2048]{3,2,1,0:T(8,128)(2,1)S(1)}, bf16[2,1,256,2048]{3,2,1,0:T(8,128)(2,1)}, u32[]{:S(2)}) copy-start(bf16[2,1,256,2048]{3,2,1,0:T(8,128)(2,1)} %refs_2_.9) | copy-start | bytes 6291460
  6.4 5.6 %copy-start.9 = (s32[1,256]{1,0:T(1,128)S(1)}, s32[1,256]{1,0:T(1,128)}, u32[]{:S(2)}) copy-start(s32[1,256]{1,0:T(1,128)} %refs_1_.7) | copy-start | bytes 3076
  7.3 6.8 %collective-permute-start.1 = (f32[1,64,256]{2,1,0:T(8,128)S(1)}, f32[1,64,256]{2,1,0:T(8,128)S(1)}, u32[]{:S(2)}, u32[]{:S(2)}) collective-permute-start(f32[1,64,256]{2,1,0:T(8,128)S(1)} %add.23.refs_7_.refs_0_.refs_1_), channel_id=1, source_target_pairs={{0,2},{2,0},{1,3},{3,1},{4,6},{6,4},{5,7},{7,5},{8,10},{10,8},{9,1... | collective-permute-start | bytes 196616 | tf_op jit(solution)/shard_map/ppermute | solution.py:496
  10.4 8.5 %collective-permute-start.3 = (f32[4,64,256]{2,1,0:T(8,128)S(1)}, f32[4,64,256]{2,1,0:T(8,128)S(1)}, u32[]{:S(2)}, u32[]{:S(2)}) collective-permute-start(f32[4,64,256]{2,1,0:T(8,128)S(1)} %hold.4), channel_id=1, source_target_pairs={{0,1},{1,0},{2,3},{3,2},{4,5},{5,4},{6,7},{7,6},{8,9},{9,8},{10,11... | collective-permute-start | bytes 786440 | tf_op jit(solution)/shard_map/ppermute | solution.py:493
  12.0 7.9 %copy-start.3 = (f32[2,16,64,64]{3,2,1,0:T(8,128)S(1)}, f32[2,16,64,64]{3,2,1,0:T(8,128)}, u32[]{:S(2)}) copy-start(f32[2,16,64,64]{3,2,1,0:T(8,128)} %refs_6_.3) | copy-start | bytes 1572868
  12.0 7.9 %copy-start.6 = (f32[2,64,64]{2,1,0:T(8,128)S(1)}, f32[2,64,64]{2,1,0:T(8,128)}, u32[]{:S(2)}) copy-start(f32[2,64,64]{2,1,0:T(8,128)} %refs_5_.3) | copy-start | bytes 98308
  14.1 10.2 %copy-start.7 = (s32[4,256]{1,0:T(4,128)S(1)}, s32[4,256]{1,0:T(4,128)}, u32[]{:S(2)}) copy-start(s32[4,256]{1,0:T(4,128)} %refs_0_.2) | copy-start | bytes 12292
  14.2 5.8 %collective-permute-start.2 = (f32[1,64,256]{2,1,0:T(8,128)S(1)}, f32[1,64,256]{2,1,0:T(8,128)S(1)}, u32[]{:S(2)}, u32[]{:S(2)}) collective-permute-start(f32[1,64,256]{2,1,0:T(8,128)S(1)} %settle.1.refs_1_), channel_id=1, source_target_pairs={{0,1},{1,0},{2,3},{3,2},{4,5},{5,4},{6,7},{7,6},{8,9},{9,8},{10,11... | collective-permute-start | bytes 196616 | tf_op jit(solution)/shard_map/ppermute | solution.py:493
  19.0 12.8 %collective-permute-start.7 = (f32[4,64,256]{2,1,0:T(8,128)S(1)}, f32[4,64,256]{2,1,0:T(8,128)S(1)}, u32[]{:S(2)}, u32[]{:S(2)}) collective-permute-start(f32[4,64,256]{2,1,0:T(8,128)S(1)} %add.24.refs_7_), channel_id=1, source_target_pairs={{0,2},{2,0},{1,3},{3,1},{4,6},{6,4},{5,7},{7,5},{8,10},{10,8},{9,1... | collective-permute-start | bytes 786440 | tf_op jit(solution)/shard_map/ppermute | solution.py:496
  21.8 10.2 %collective-permute-start.8 = (f32[1,64,1024]{2,1,0:T(8,128)S(1)}, f32[1,64,1024]{2,1,0:T(8,128)S(1)}, u32[]{:S(2)}, u32[]{:S(2)}) collective-permute-start(f32[1,64,1024]{2,1,0:T(8,128)S(1)} %get-tuple-element.16.refs_2_), channel_id=1, source_target_pairs={{0,8},{8,0},{4,12},{12,4},{1,9},{9,1},{5,13},{13,5},{2,10},{10,2},... | collective-permute-start | bytes 786440 | tf_op jit(solution)/shard_map/ppermute | solution.py:496
  23.3 10.8 %collective-permute-start.6 = (f32[1,64,1024]{2,1,0:T(8,128)S(1)}, f32[1,64,1024]{2,1,0:T(8,128)S(1)}, u32[]{:S(2)}, u32[]{:S(2)}) collective-permute-start(f32[1,64,1024]{2,1,0:T(8,128)S(1)} %get-tuple-element.15.refs_1_), channel_id=1, source_target_pairs={{0,8},{8,0},{4,12},{12,4},{1,9},{9,1},{5,13},{13,5},{2,10},{10,2},... | collective-permute-start | bytes 786440 | tf_op jit(solution)/shard_map/ppermute | solution.py:496
  23.8 11.5 %collective-permute-start.4 = (f32[1,64,1024]{2,1,0:T(8,128)S(1)}, f32[1,64,1024]{2,1,0:T(8,128)S(1)}, u32[]{:S(2)}, u32[]{:S(2)}) collective-permute-start(f32[1,64,1024]{2,1,0:T(8,128)S(1)} %get-tuple-element.15.refs_1_), channel_id=1, source_target_pairs={{0,4},{4,0},{8,12},{12,8},{1,5},{5,1},{9,13},{13,9},{2,6},{6,2},{1... | collective-permute-start | bytes 786440 | tf_op jit(solution)/shard_map/ppermute | solution.py:493
  23.8 11.5 %collective-permute-start.5 = (f32[1,64,1024]{2,1,0:T(8,128)S(1)}, f32[1,64,1024]{2,1,0:T(8,128)S(1)}, u32[]{:S(2)}, u32[]{:S(2)}) collective-permute-start(f32[1,64,1024]{2,1,0:T(8,128)S(1)} %get-tuple-element.16.refs_2_), channel_id=1, source_target_pairs={{0,4},{4,0},{8,12},{12,8},{1,5},{5,1},{9,13},{13,9},{2,6},{6,2},{1... | collective-permute-start | bytes 786440 | tf_op jit(solution)/shard_map/ppermute | solution.py:493
  31.8 7.2 %collective-permute-start.11 = (f32[4,64,256]{2,1,0:T(8,128)S(1)}, f32[4,64,256]{2,1,0:T(8,128)S(1)}, u32[]{:S(2)}, u32[]{:S(2)}) collective-permute-start(f32[4,64,256]{2,1,0:T(8,128)S(1)} %add.25.refs_1_.refs_3_.refs_2_), channel_id=1, source_target_pairs={{0,1},{1,0},{2,3},{3,2},{4,5},{5,4},{6,7},{7,6},{8,9},{9,8},{10,11... | collective-permute-start | bytes 786440 | tf_op jit(solution)/shard_map/ppermute | solution.py:493
  31.9 3.4 %collective-permute-start.10 = (f32[1,64,1024]{2,1,0:T(8,128)S(1)}, f32[1,64,1024]{2,1,0:T(8,128)S(1)}, u32[]{:S(2)}, u32[]{:S(2)}) collective-permute-start(f32[1,64,1024]{2,1,0:T(8,128)S(1)} %hold.7.refs_6_), channel_id=1, source_target_pairs={{0,4},{4,0},{8,12},{12,8},{1,5},{5,1},{9,13},{13,9},{2,6},{6,2},{1... | collective-permute-start | bytes 786440 | tf_op jit(solution)/shard_map/ppermute | solution.py:493
  34.0 1.5 %collective-permute-start.9 = (f32[1,64,1024]{2,1,0:T(8,128)S(1)}, f32[1,64,1024]{2,1,0:T(8,128)S(1)}, u32[]{:S(2)}, u32[]{:S(2)}) collective-permute-start(f32[1,64,1024]{2,1,0:T(8,128)S(1)} %hold.6.refs_5_), channel_id=1, source_target_pairs={{0,4},{4,0},{8,12},{12,8},{1,5},{5,1},{9,13},{13,9},{2,6},{6,2},{1... | collective-permute-start | bytes 786440 | tf_op jit(solution)/shard_map/ppermute | solution.py:493
  39.3 5.4 %collective-permute-start.12 = (f32[4,128]{1,0:T(4,128)S(1)}, f32[4,128]{1,0:T(4,128)S(1)}, u32[]{:S(2)}, u32[]{:S(2)}) collective-permute-start(f32[4,128]{1,0:T(4,128)S(1)} %lever_scores.3), channel_id=1, source_target_pairs={{0,1},{1,2},{2,3},{3,0},{4,5},{5,6},{6,7},{7,4},{8,9},{9,10},{10,1... | collective-permute-start | bytes 6152 | tf_op jit(solution)/shard_map/ppermute | solution.py:542
  40.0 4.6 %collective-permute-start.13 = (f32[4,128]{1,0:T(4,128)S(1)}, f32[4,128]{1,0:T(4,128)S(1)}, u32[]{:S(2)}, u32[]{:S(2)}) collective-permute-start(f32[4,128]{1,0:T(4,128)S(1)} %lever_scores.3), channel_id=1, source_target_pairs={{0,2},{1,3},{2,0},{3,1},{4,6},{5,7},{6,4},{7,5},{8,10},{9,11},{10,... | collective-permute-start | bytes 6152 | tf_op jit(solution)/shard_map/ppermute | solution.py:542
  41.7 3.6 %collective-permute-start.14 = (f32[4,128]{1,0:T(4,128)S(1)}, f32[4,128]{1,0:T(4,128)S(1)}, u32[]{:S(2)}, u32[]{:S(2)}) collective-permute-start(f32[4,128]{1,0:T(4,128)S(1)} %lever_scores.3), channel_id=1, source_target_pairs={{0,3},{1,0},{2,1},{3,2},{4,7},{5,4},{6,5},{7,6},{8,11},{9,8},{10,9... | collective-permute-start | bytes 6152 | tf_op jit(solution)/shard_map/ppermute | solution.py:542
